TPU v7x, 512 devices: a whole 4x8x8 slice. The times are simulated.
512 devices in a mesh: ad: 64 (over x, y, core), tp: 8 (over z).
Axes of the slice: x: 4, y: 8, z: 8, core: 2. Of those that a mesh axis runs over, the one named last changes fastest.
Arguments:
- inputs: bfloat16 [512, 8192], P('ad', 'tp'), may hold values from -6 to 6
- w_gate: bfloat16 [28672, 8192], P('ad', 'tp'), may hold values from -0.0625 to 0.0625
- w_up: bfloat16 [28672, 8192], P('ad', 'tp'), may hold values from -0.0625 to 0.0625
- w_down: bfloat16 [28672, 8192], P('ad', 'tp'), may hold values from -0.03125 to 0.03125
- a_gate: bfloat16 [64, 8192, 64], P('ad', 'tp'), may hold values from -0.0625 to 0.0625
- a_up: bfloat16 [64, 8192, 64], P('ad', 'tp'), may hold values from -0.0625 to 0.0625
- b_gate: bfloat16 [64, 64, 28672], P(None, 'tp', 'ad'), may hold values from -0.75 to 0.75
- b_up: bfloat16 [64, 64, 28672], P(None, 'tp', 'ad'), may hold values from -0.75 to 0.75
- a_down: bfloat16 [28672, 64, 64], P('ad', None, 'tp'), may hold values from -0.03125 to 0.03125
- b_down: bfloat16 [64, 64, 8192], P('ad', None, 'tp'), may hold values from -0.75 to 0.75
- adapter_ids: int32 [512, 1], replicated, may hold values from 0 to 63; in each aligned block of 512 rows (0 to 511, 512 to 1023, ...) at most 24 rows name the same one
- owner_map: int32 [64], replicated, may hold values from 0 to 63, each once
Outputs:
- mixed: bfloat16 [512, 8192], P('ad', 'tp')
Inputs may be any that keep to these rules, and one draw needn't show every extreme that they name: `adapter_ids`: each row names one adapter; no adapter is named by more than 24 of the 512 rows, a bound that some block reaches. `owner_map`: each slot number appears once; slot k is held by index k of ad.
All inputs are finite; a program needn't handle non-finite values.
Results may differ from a plain program's by a relative error of at most 0.007.
Values may be sent and summed in bfloat16 or wider, within the bound.
No kernel may reach another device: no remote copies, remote signals or barrier semaphores. Data moves between devices by JAX's collectives and lax.ppermute only.
A program may use at most 64 MiB of HBM per device.

v0:
```python
import jax
import jax.numpy as jnp
from jax import lax
from jax.sharding import PartitionSpec as P

OCAP = 24


def per_device(
    inputs, w_gate, w_up, w_down, a_gate, a_up, b_gate, b_up, a_down, b_down, adapter_ids, owner_map
):
    here_owner = lax.axis_index("ad")
    total_rows = adapter_ids.shape[0]
    slot_count = owner_map.shape[0]
    unit_cols = w_gate.shape[0]
    rank_part = b_gate.shape[1]
    adapter = adapter_ids[:, 0]
    table = jnp.arange(slot_count, dtype=jnp.int32)
    row_slot = jnp.sum(jnp.where(adapter[:, None] == table[None, :], owner_map[None, :], 0), axis=1)
    onehot = (row_slot[:, None] == table[None, :]).astype(jnp.int32)
    position = jnp.sum((jnp.cumsum(onehot, axis=0) - onehot) * onehot, axis=1)
    places = jnp.arange(OCAP, dtype=jnp.int32)
    chosen = (row_slot == here_owner)[:, None] & (position[:, None] == places[None, :])
    picker = chosen.astype(jnp.bfloat16)
    row_index = jnp.arange(total_rows, dtype=jnp.int32)
    filled = jnp.sum(chosen.astype(jnp.int32), axis=0)
    target = jnp.sum(jnp.where(chosen, row_index[:, None], 0), axis=0) + (1 - filled) * total_rows
    contract_cols = (((1,), (1,)), ((), ()))
    contract_rows = (((0,), (0,)), ((), ()))
    piece = lax.all_gather(inputs, "ad", axis=0, tiled=True)
    gate_piece = lax.dot_general(piece, w_gate, contract_cols, preferred_element_type=jnp.float32)
    up_piece = lax.dot_general(piece, w_up, contract_cols, preferred_element_type=jnp.float32)
    gate_base = gate_piece
    up_base = up_piece
    picked = lax.dot_general(picker, piece, contract_rows, preferred_element_type=jnp.float32)
    gate_base, up_base, picked = (gate_base, up_base, picked)
    selected = picked.astype(jnp.bfloat16)
    shrink_gate = jnp.dot(selected, a_gate[0], preferred_element_type=jnp.float32)
    shrink_up = jnp.dot(selected, a_up[0], preferred_element_type=jnp.float32)
    part_gate, part_up = (
        lax.psum_scatter(shrink_gate, "tp", scatter_dimension=1, tiled=True),
        lax.psum_scatter(shrink_up, "tp", scatter_dimension=1, tiled=True),
    )
    low_gate = part_gate.astype(jnp.bfloat16)
    low_up = part_up.astype(jnp.bfloat16)
    placed_gate = jnp.dot(picker, low_gate, preferred_element_type=jnp.float32)
    placed_up = jnp.dot(picker, low_up, preferred_element_type=jnp.float32)
    total_gate, total_up = lax.psum((placed_gate, placed_up), "ad")
    row_gate = total_gate.astype(jnp.bfloat16)
    row_up = total_up.astype(jnp.bfloat16)
    onehot_low = onehot.astype(jnp.bfloat16)

    def expand(rows_low, weights):
        spread_rows = (onehot_low[:, :, None] * rows_low[:, None, :]).reshape(
            total_rows, slot_count * rank_part
        )
        return jnp.dot(
            spread_rows,
            weights.reshape(slot_count * rank_part, unit_cols),
            preferred_element_type=jnp.float32,
        )

    gate_part = gate_base + expand(row_gate, b_gate)
    up_part = up_base + expand(row_up, b_up)
    gate_rows, up_rows = (
        lax.psum_scatter(gate_part, "tp", scatter_dimension=0, tiled=True),
        lax.psum_scatter(up_part, "tp", scatter_dimension=0, tiled=True),
    )
    hidden_rows = (jax.nn.silu(gate_rows) * up_rows).astype(jnp.bfloat16)
    hidden_all = lax.all_gather(hidden_rows, "tp", axis=0, tiled=True)
    rank_full = jnp.dot(
        hidden_all,
        a_down.reshape(unit_cols, slot_count * rank_part),
        preferred_element_type=jnp.float32,
    )
    rank_full = rank_full.reshape(total_rows, slot_count, rank_part)
    rank_local = jnp.sum(rank_full * onehot.astype(jnp.float32)[:, :, None], axis=1)
    rank_total = lax.psum(rank_local, "ad")
    rank_all = lax.all_gather(rank_total.astype(jnp.bfloat16), "tp", axis=1, tiled=True)
    rank_pick = lax.dot_general(
        picker, rank_all, contract_rows, preferred_element_type=jnp.float32
    ).astype(jnp.bfloat16)
    delta = jnp.dot(rank_pick, b_down[0], preferred_element_type=jnp.float32)
    delta_rows = (
        jnp.zeros((total_rows, delta.shape[1]), jnp.float32).at[target].add(delta, mode="drop")
    )
    base_rows = jnp.dot(hidden_all, w_down, preferred_element_type=jnp.float32)
    mixed = lax.psum_scatter(base_rows + delta_rows, "ad", scatter_dimension=0, tiled=True)
    return mixed.astype(jnp.bfloat16)


def solution(mesh):
    placed = (
        P("ad", "tp"),
        P("ad", "tp"),
        P("ad", "tp"),
        P("ad", "tp"),
        P("ad", "tp", None),
        P("ad", "tp", None),
        P(None, "tp", "ad"),
        P(None, "tp", "ad"),
        P("ad", None, "tp"),
        P("ad", None, "tp"),
        P(),
        P(),
    )
    return jax.shard_map(
        per_device, mesh=mesh, in_specs=placed, out_specs=P("ad", "tp"), check_vma=False
    )
```

profile of v0, /device:TPU:16, one launch (start us, length us, event | category | flops | bytes accessed | tf_op | source)
XLA Modules:
  0.0 909.7 jit_solution(6058494948619989770)
XLA Ops:
  6.5 0.0 copy-start
  6.5 0.0 all-gather.2.cloned.1.call-start
  6.5 0.7 all-gather.2.cloned.1.call-update
  7.3 0.0 reduce-scatter.8.cloned.1.call-start
  7.3 0.8 select_reduce_fusion
  8.1 1.2 reduce-window.6
  9.3 0.2 slice_reduce_fusion
  9.6 1.3 dynamic-slice
  11.5 0.1 fusion.13
  11.7 0.7 convert_convert_fusion
  12.3 84.3 %all-gather.2.cloned.1.call-done = bf16[512,1024]{1,0:T(8,128)(2,1)} async-done(((bf16[8,1024]{1,0:T(8,128)(2,1)}), bf16[512,1024]{1,0:T(8,128)(2,1)}) %all-gather.2.cloned.1.call-update) | async-done | bytes 1048592 | tf_op jit(solution)/shard_map/all_gather | solution.py:30
  96.7 1.5 convolution_convert_fusion
  98.1 0.0 copy-start.2
  98.2 0.0 copy-start.3
  98.2 1.2 fusion.15
  99.4 0.0 copy-done.5
  99.4 0.2 fusion.17
  99.5 30.9 %all-reduce.3 = (bf16[24,64]{1,0:T(8,128)(2,1)S(1)}, bf16[24,64]{1,0:T(8,128)(2,1)S(1)}) all-reduce(f32[24,64]{1,0:T(8,128)S(1)} %fusion.15, f32[24,64]{1,0:T(8,128)S(1)} %fusion.17), channel_id=4, replica_groups=mesh['ad'=64,'tp'=8] {'tp'}, use_global_device_ids=true, to_apply=%region_7.8.clone | all-reduce | flops 3072 | bytes 18432
  130.4 0.2 fusion.23
  130.6 0.2 fusion.25
  130.9 236.2 %all-reduce.2 = (bf16[512,8]{0,1:T(8,128)(2,1)S(1)}, bf16[512,8]{0,1:T(8,128)(2,1)S(1)}) all-reduce(f32[512,8]{0,1:T(8,128)S(1)} %fusion.23, f32[512,8]{0,1:T(8,128)S(1)} %fusion.25), channel_id=1, replica_groups=mesh['ad'=64,'tp'=8] {'ad'}, use_global_device_ids=true, to_apply=%region_8.9 | all-reduce | flops 8192 | bytes 49152 | tf_op jit(solution)/shard_map/psum | solution.py:48
  367.1 1.5 convolution_bitcast_fusion
  368.7 1.7 convolution_add_fusion
  370.4 0.0 reduce-scatter.8.cloned.1.call-update
  370.4 0.0 reduce-scatter.6.cloned.1.call-start
  370.5 1.6 convolution_bitcast_fusion.1
  372.1 0.0 copy-done.4
  372.1 0.0 copy-start.6
  372.1 1.8 convolution_add_fusion.1
  373.9 0.0 reduce-scatter.6.cloned.1.call-update
  373.9 0.0 reduce-scatter.10.cloned.1.call-start
  373.9 0.1 convert_reduce_fusion
  374.1 39.4 %reduce-scatter.8.cloned.1.call-done = f32[64,448]{1,0:T(8,128)} async-done(((f32[512,448]{1,0:T(8,128)}), f32[64,448]{1,0:T(8,128)}) %reduce-scatter.8.cloned.1.call-update) | async-done | bytes 114704 | tf_op jit(solution)/shard_map/reduce_scatter | solution.py:67
  413.5 43.2 %reduce-scatter.6.cloned.1.call-done = f32[64,448]{1,0:T(8,128)} async-done(((f32[512,448]{1,0:T(8,128)}), f32[64,448]{1,0:T(8,128)}) %reduce-scatter.6.cloned.1.call-update) | async-done | bytes 114704 | tf_op jit(solution)/shard_map/reduce_scatter | solution.py:66
  456.7 1.0 multiply_convert_fusion
  457.7 25.3 %all_gather.10 = bf16[512,448]{1,0:T(8,128)(2,1)S(1)} all-gather(bf16[64,448]{1,0:T(8,128)(2,1)S(1)} %multiply_convert_fusion), channel_id=1, replica_groups=mesh['ad'=64,'tp'=8] {'tp'}, dimensions={0}, use_global_device_ids=true | all-gather | bytes 516096 | tf_op jit(solution)/shard_map/all_gather | solution.py:70
  483.0 0.0 copy-done.6
  483.0 1.5 fusion
  484.6 236.1 %psum.23 = bf16[512,8]{0,1:T(8,128)(2,1)S(1)} all-reduce(f32[512,8]{0,1:T(8,128)S(1)} %fusion), channel_id=1, replica_groups=mesh['ad'=64,'tp'=8] {'ad'}, use_global_device_ids=true, to_apply=%region_13.14 | all-reduce | flops 4096 | bytes 24576 | tf_op jit(solution)/shard_map/psum | solution.py:78
  720.7 26.5 %all_gather.11 = bf16[512,64]{0,1:T(8,128)(2,1)} all-gather(bf16[512,8]{0,1:T(8,128)(2,1)S(1)} %psum.23), channel_id=1, replica_groups=mesh['ad'=64,'tp'=8] {'tp'}, dimensions={1}, use_global_device_ids=true | all-gather | bytes 73728 | tf_op jit(solution)/shard_map/all_gather | solution.py:79
  747.2 0.0 copy-done
  747.2 0.7 fusion.41
  747.9 1.2 fusion.1
  749.2 1.6 scatter_fusion
  750.8 1.3 copy-done.1
  752.1 0.0 reduce-scatter.10.cloned.1.call-update
  752.1 149.7 %reduce-scatter.10.cloned.1.call-done = f32[8,1024]{1,0:T(8,128)} async-done(((f32[512,1024]{1,0:T(8,128)}), f32[8,1024]{1,0:T(8,128)}) %reduce-scatter.10.cloned.1.call-update) | async-done | bytes 32784 | tf_op jit(solution)/shard_map/reduce_scatter | solution.py:88
  901.8 1.4 convert_element_type.72
  (10 shorter events, 0.1 us)
Async XLA Ops:
  6.5 740.7 %copy-start = (bf16[448,1024]{1,0:T(8,128)(2,1)S(1)}, bf16[448,1024]{1,0:T(8,128)(2,1)}, u32[]{:S(2)}) copy-start(bf16[448,1024]{1,0:T(8,128)(2,1)} %param.15) | copy-start | bytes 2752516
  6.5 92.8 %copy-start.5 = (bf16[1,1024,64]{1,2,0:T(8,128)(2,1)S(1)}, bf16[1,1024,64]{1,2,0:T(8,128)(2,1)}, u32[]{:S(2)}) copy-start(bf16[1,1024,64]{1,2,0:T(8,128)(2,1)} %param.16) | copy-start | bytes 393220
  6.5 90.1 %all-gather.2.cloned.1.call-start = ((), (), s32[]{:S(2)}) async-start(), calls=%async_computation.3 | async-start | bytes 1064960 | tf_op jit(solution)/shard_map/all_gather | solution.py:30
  7.3 406.3 %reduce-scatter.8.cloned.1.call-start = ((), (), s32[]{:S(2)}) async-start(), calls=%async_computation.5 | async-start | bytes 1179648 | tf_op jit(solution)/shard_map/reduce_scatter | solution.py:67
  98.1 270.5 %copy-start.2 = (bf16[512,1024]{1,0:T(8,128)(2,1)S(1)}, bf16[512,1024]{1,0:T(8,128)(2,1)}, u32[]{:S(2)}) copy-start(bf16[512,1024]{1,0:T(8,128)(2,1)} %all-gather.2.cloned.1.call-done) | copy-start | bytes 3145732
  98.2 270.5 %copy-start.3 = (bf16[448,1024]{1,0:T(8,128)(2,1)S(1)}, bf16[448,1024]{1,0:T(8,128)(2,1)}, u32[]{:S(2)}) copy-start(bf16[448,1024]{1,0:T(8,128)(2,1)} %param.14) | copy-start | bytes 2752516
  370.4 1.7 copy-start.4
  370.4 86.3 %reduce-scatter.6.cloned.1.call-start = ((), (), s32[]{:S(2)}) async-start(), calls=%async_computation.4 | async-start | bytes 1179648 | tf_op jit(solution)/shard_map/reduce_scatter | solution.py:66
  372.1 111.0 %copy-start.6 = (f32[512,64]{0,1:T(8,128)S(1)}, f32[512,64]{0,1:T(8,128)}, u32[]{:S(2)}) copy-start(f32[512,64]{0,1:T(8,128)} %get-tuple-element.11) | copy-start | bytes 393220
  373.9 527.9 %reduce-scatter.10.cloned.1.call-start = ((), (), s32[]{:S(2)}) async-start(), calls=%async_computation.6 | async-start | bytes 2129920 | tf_op jit(solution)/shard_map/reduce_scatter | solution.py:88
  750.8 1.4 copy-start.1
Sparse Core Ops, SparseCore 0:
  10.7 85.9 all-gather.1
  370.5 42.9 reduce-scatter.7
  416.3 40.3 reduce-scatter.5
  752.2 149.5 reduce-scatter.9
where the time goes:
time: 910 us
  blocking collectives  555 us (61%)
  waiting for transfers between devices  317 us (35%)
  between operations  13.9 us (2%)
  matrix products  13.4 us (1%)
    psum x1, blocking collectives, per_device(): total_gate, total_up = lax.psum((placed_gate, placed_up), 'ad')  236 us
    psum x1, blocking collectives, per_device(): rank_total = lax.psum(rank_local, 'ad')  236 us
    reduce_scatter x1, waiting for transfers between devices, per_device(): lax.psum_scatter(base_rows + delta_rows, 'ad', scatter_dimension=0, tiled...  150 us
    all_gather x1, waiting for transfers between devices, per_device(): piece = lax.all_gather(inputs, 'ad', axis=0, tiled=True)  84.3 us
    reduce_scatter x1, waiting for transfers between devices, per_device(): lax.psum_scatter(gate_part, 'tp', scatter_dimension=0, tiled=True)  43.2 us
    reduce_scatter x1, waiting for transfers between devices, per_device(): lax.psum_scatter(up_part, 'tp', scatter_dimension=0, tiled=True)  39.4 us
    unnamed x1, blocking collectives  30.9 us
    all_gather x1, blocking collectives, per_device(): lax.all_gather(rank_total.astype(jnp.bfloat16), 'tp', axis=1, tiled=True)  26.5 us
  transfers between devices with their start and end apart: 4, of which 4 were waited for; matrix products, arithmetic and copies ran while one was open for 1% of the time, Pallas kernels for 0%

commit v1 on v0

v1 whole, which is shorter than its diff:
```python
import jax
import jax.numpy as jnp
from jax import lax
from jax.sharding import Mesh, PartitionSpec as P

OCAP = 24
F32 = jnp.float32
BF16 = jnp.bfloat16
NT = (((1,), (1,)), ((), ()))
TN = (((0,), (0,)), ((), ()))
OWN = ("x", "y", "c")
CHIPS = ("x", "y")


def spread(block, axes, count):
    copies = jnp.broadcast_to(block[None], (count,) + block.shape)
    return lax.all_to_all(copies, axes, 0, 0, tiled=True)


def per_device(
    inputs, w_gate, w_up, w_down, a_gate, a_up, b_gate, b_up, a_down, b_down, adapter_ids, owner_map
):
    chips = lax.axis_size("x") * lax.axis_size("y")
    cores = lax.axis_size("c")
    parts = lax.axis_size("z")
    owners = chips * cores
    here_owner = lax.axis_index(OWN)
    own_rows, width = inputs.shape
    rows = adapter_ids.shape[0]
    units = w_gate.shape[0]
    rank = a_gate.shape[2]
    rank_part = b_gate.shape[1]
    slots = owner_map.shape[0]

    half = spread(inputs, CHIPS, chips).reshape(chips * own_rows, width)
    piece = lax.all_gather(half, "c", axis=0, tiled=True)

    adapter = adapter_ids[:, 0].reshape(chips, cores, own_rows).transpose(1, 0, 2).reshape(rows)
    table = jnp.arange(slots, dtype=jnp.int32)
    row_slot = jnp.sum(jnp.where(adapter[:, None] == table[None, :], owner_map[None, :], 0), axis=1)
    onehot = (row_slot[:, None] == table[None, :]).astype(jnp.int32)
    position = jnp.sum((jnp.cumsum(onehot, axis=0) - onehot) * onehot, axis=1)
    place = row_slot * OCAP + position
    places = (place[:, None] == jnp.arange(slots * OCAP, dtype=jnp.int32)[None, :]).astype(BF16)
    mine = (
        place[:, None] == here_owner * OCAP + jnp.arange(OCAP, dtype=jnp.int32)[None, :]
    ).astype(BF16)
    slot_rows = (table[:, None] == row_slot[None, :]).astype(BF16)

    selected = lax.dot_general(mine, piece, TN, preferred_element_type=F32).astype(BF16)
    shrunk = jnp.stack(
        [
            jnp.dot(selected, a_gate[0], preferred_element_type=F32).reshape(OCAP, parts, rank_part),
            jnp.dot(selected, a_up[0], preferred_element_type=F32).reshape(OCAP, parts, rank_part),
        ],
        axis=2,
    )
    shrunk = shrunk.transpose(1, 0, 2, 3).reshape(parts, OCAP, 2 * rank_part).astype(BF16)
    shrunk = lax.all_to_all(shrunk, "z", 0, 0, tiled=True)
    shrunk = jnp.sum(shrunk.astype(F32), axis=0).astype(BF16)
    low_all = spread(shrunk, OWN, owners).reshape(owners * OCAP, 2 * rank_part)
    low_rows = lax.dot_general(
        low_all, places, (((0,), (1,)), ((), ())), preferred_element_type=F32
    ).astype(BF16)

    def expand(low, weights):
        wide = (slot_rows[:, None, :] * low[None, :, :]).reshape(slots * rank_part, rows)
        return lax.dot_general(
            weights.reshape(slots * rank_part, units), wide, TN, preferred_element_type=F32
        )

    gate_part = lax.dot_general(w_gate, piece, NT, preferred_element_type=F32) + expand(
        low_rows[:rank_part], b_gate
    )
    up_part = lax.dot_general(w_up, piece, NT, preferred_element_type=F32) + expand(
        low_rows[rank_part:], b_up
    )
    both = jnp.stack(
        [
            gate_part.astype(BF16).reshape(parts, units // parts, rows),
            up_part.astype(BF16).reshape(parts, units // parts, rows),
        ],
        axis=1,
    )
    both = lax.all_to_all(both, "z", 0, 0, tiled=True)
    both = jnp.sum(both.astype(F32), axis=0)
    hidden = (jax.nn.silu(both[0]) * both[1]).astype(BF16)
    hidden_all = spread(hidden, "z", parts).reshape(units, rows)

    rank_full = lax.dot_general(
        a_down.reshape(units, slots * rank_part), hidden_all, TN, preferred_element_type=F32
    )
    rank_rows = jnp.sum(
        rank_full.reshape(slots, rank_part, rows) * slot_rows.astype(F32)[:, None, :], axis=0
    ).astype(BF16)
    rank_sent = lax.dot_general(
        places, rank_rows, (((0,), (1,)), ((), ())), preferred_element_type=F32
    ).astype(BF16)
    rank_sum = lax.all_to_all(
        rank_sent.reshape(owners, OCAP, rank_part), OWN, 0, 0, tiled=True
    )
    rank_sum = jnp.sum(rank_sum.astype(F32), axis=0).astype(BF16)
    rank_all = spread(rank_sum, "z", parts).transpose(1, 0, 2).reshape(OCAP, rank)
    rank_mine = jnp.dot(mine, rank_all, preferred_element_type=F32).astype(BF16)
    out = lax.dot_general(hidden_all, w_down, TN, preferred_element_type=F32) + jnp.dot(
        rank_mine, b_down[0], preferred_element_type=F32
    )
    out = out.astype(BF16).reshape(cores, chips, own_rows, width)
    out = lax.all_to_all(out, "c", 0, 0, tiled=True)
    out = jnp.sum(out.astype(F32), axis=0).astype(BF16)
    out = lax.all_to_all(out, CHIPS, 0, 0, tiled=True)
    return jnp.sum(out.astype(F32), axis=0).astype(BF16)


def solution(mesh):
    side = (4, 8, 2, 8)
    fine = Mesh(mesh.devices.reshape(side), ("x", "y", "c", "z"))
    ad, tp = ("x", "y", "c"), "z"
    placed = (
        P(ad, tp),
        P(ad, tp),
        P(ad, tp),
        P(ad, tp),
        P(ad, tp, None),
        P(ad, tp, None),
        P(None, tp, ad),
        P(None, tp, ad),
        P(ad, None, tp),
        P(ad, None, tp),
        P(),
        P(),
    )
    return jax.shard_map(
        per_device, mesh=fine, in_specs=placed, out_specs=P(ad, tp), check_vma=False
    )
```

time: 910 us -> 207 us (0.23)
  the two profiles are of different devices: /device:TPU:16 before, /device:TPU:8 now
where the time goes in v1:
time: 207 us; the launch traced here: 206 us
  blocking collectives  142 us (69%)
  waiting for transfers between devices  22.4 us (11%)
  between operations  13.7 us (7%)
  starting transfers between devices  10.3 us (5%)
  matrix products  9.41 us (5%)
  local copies, waits for them, and re-layouts  4.38 us (2%)
  other arithmetic  3.45 us (2%)
    all_to_all x3, blocking collectives, spread(): return lax.all_to_all(copies, axes, 0, 0, tiled=True)  56.8 us
    all_to_all x1, blocking collectives, per_device(): both = lax.all_to_all(both, 'z', 0, 0, tiled=True)  29 us
    all_to_all x1, blocking collectives, per_device(): out = lax.all_to_all(out, CHIPS, 0, 0, tiled=True)  22.5 us
    all_to_all x1, blocking collectives, per_device(): shrunk = lax.all_to_all(shrunk, 'z', 0, 0, tiled=True)  14.9 us
    all_to_all x1, blocking collectives, per_device(): lax.all_to_all(rank_sent.reshape(owners, OCAP, rank_part), OWN, 0, 0, til...  14.7 us
    all_gather x1, waiting for transfers between devices, per_device(): piece = lax.all_gather(half, 'c', axis=0, tiled=True)  13.4 us
    all_to_all x1, starting transfers between devices, spread(): return lax.all_to_all(copies, axes, 0, 0, tiled=True)  10.2 us
    all_to_all x1, waiting for transfers between devices, spread(): return lax.all_to_all(copies, axes, 0, 0, tiled=True)  8.92 us
  transfers between devices with their start and end apart: 2, of which 2 were waited for; matrix products, arithmetic and copies ran while one was open for 2% of the time, Pallas kernels for 0%

profile of v1, /device:TPU:8, one launch (start us, length us, event | category | flops | bytes accessed | tf_op | source)
XLA Modules:
  0.0 206.0 jit_solution(2855906881145549815)
XLA Ops:
  6.5 0.0 all-gather.2.cloned.1.call-start
  6.6 0.9 broadcast_in_dim.22
  7.5 27.7 %all_to_all.45 = bf16[32,8,1024]{2,1,0:T(8,128)(2,1)} all-to-all(bf16[32,8,1024]{2,1,0:T(8,128)(2,1)S(1)} %broadcast_in_dim.22), channel_id=1, replica_groups=mesh['x'=4,'y'=8,'c'=2,'z'=8] {'x','y'}, dimensions={0} | all-to-all | bytes 1048576 | tf_op jit(solution)/shard_map/all_to_all | solution.py:17
  35.1 0.0 all-gather.2.cloned.1.call-update
  35.2 0.5 broadcast.55
  35.7 0.7 reduce.9
  36.4 0.1 reshape_squeeze.3
  36.5 0.1 eq.85
  36.6 0.1 select_reduce_fusion
  36.7 1.2 reduce-window.6
  37.9 0.2 slice_reduce_fusion
  38.2 0.1 fusion.28
  38.3 13.4 %all-gather.2.cloned.1.call-done = bf16[512,1024]{1,0:T(8,128)(2,1)} async-done(((bf16[256,1024]{1,0:T(8,128)(2,1)}), bf16[512,1024]{1,0:T(8,128)(2,1)}) %all-gather.2.cloned.1.call-update) | async-done | bytes 1048592 | tf_op jit(solution)/shard_map/all_gather | solution.py:36
  51.7 1.6 fusion.10
  53.4 0.2 fusion.13
  53.6 0.2 fusion.12
  53.8 0.1 reshape.134
  53.9 14.9 %all_to_all.46 = bf16[8,2,192]{2,1,0:T(2,128)(2,1)S(1)} all-to-all(bf16[8,2,192]{2,1,0:T(2,128)(2,1)S(1)} %reshape.134), channel_id=1, replica_groups=mesh['x'=4,'y'=8,'c'=2,'z'=8] {'z'}, dimensions={0} | all-to-all | bytes 12288 | tf_op jit(solution)/shard_map/all_to_all | solution.py:59
  68.8 0.1 reshape.135
  68.9 0.9 reshape.136
  69.8 10.2 %all-to-all-start.2 = ((bf16[64,2,192]{2,1,0:T(2,128)(2,1)}), bf16[64,2,192]{2,1,0:T(2,128)(2,1)S(1)}, u32[]{:S(2)}, u32[]{:S(2)}) async-start(bf16[64,2,192]{2,1,0:T(2,128)(2,1)} %reshape.136), calls=%async_computation.2 | async-start | bytes 131072 | tf_op jit(solution)/shard_map/all_to_all | solution.py:17
  80.1 8.9 %all-to-all-done.2 = bf16[64,2,192]{2,1,0:T(2,128)(2,1)S(1)} async-done(((bf16[64,2,192]{2,1,0:T(2,128)(2,1)}), bf16[64,2,192]{2,1,0:T(2,128)(2,1)S(1)}, u32[]{:S(2)}, u32[]{:S(2)}) %all-to-all-start.2) | async-done | bytes 49184 | tf_op jit(solution)/shard_map/all_to_all | solution.py:17
  89.0 0.2 reshape.137
  89.2 0.1 copy.40
  89.3 0.3 reshape.114
  89.7 0.7 fusion.11
  90.4 0.5 convolution_bitcast_fusion.2
  90.9 1.5 convolution_bitcast_fusion.1
  92.4 0.7 fusion.6
  93.1 0.4 copy-done.7
  93.6 0.7 fusion.7
  94.2 0.1 pad_maximum_fusion
  94.3 29.0 %all_to_all.47 = bf16[8,2,56,512]{3,2,1,0:T(8,128)(2,1)S(1)} all-to-all(bf16[8,2,56,512]{3,2,1,0:T(8,128)(2,1)S(1)} %pad_maximum_fusion), channel_id=1, replica_groups=mesh['x'=4,'y'=8,'c'=2,'z'=8] {'z'}, dimensions={0} | all-to-all | bytes 1835008 | tf_op jit(solution)/shard_map/all_to_all | solution.py:85
  123.4 0.1 convert_reduce_fusion
  123.6 19.0 %all_to_all.48 = bf16[8,56,512]{2,1,0:T(8,128)(2,1)S(1)} all-to-all(bf16[8,56,512]{2,1,0:T(8,128)(2,1)S(1)} %broadcast_in_dim.27), channel_id=1, replica_groups=mesh['x'=4,'y'=8,'c'=2,'z'=8] {'z'}, dimensions={0} | all-to-all | bytes 917504 | tf_op jit(solution)/shard_map/all_to_all | solution.py:17
  142.5 0.4 fusion.8
  143.0 0.6 fusion.2
  143.6 0.2 reshape.118
  143.8 0.1 copy.45
  143.9 14.7 %all_to_all.49 = bf16[64,24,8]{1,2,0:T(8,128)(2,1)S(1)} all-to-all(bf16[64,24,8]{1,2,0:T(8,128)(2,1)S(1)} %copy.45), channel_id=1, replica_groups=mesh['x'=4,'y'=8,'c'=2,'z'=8] {'x','y','c'}, dimensions={0} | all-to-all | bytes 49152 | tf_op jit(solution)/shard_map/all_to_all | solution.py:99
  158.6 0.1 reduce_sum.89
  158.7 10.1 %all_to_all.50 = bf16[8,24,8]{1,2,0:T(8,128)(2,1)S(1)} all-to-all(bf16[8,24,8]{1,2,0:T(8,128)(2,1)S(1)} %broadcast_in_dim.28), channel_id=1, replica_groups=mesh['x'=4,'y'=8,'c'=2,'z'=8] {'z'}, dimensions={0} | all-to-all | bytes 6144 | tf_op jit(solution)/shard_map/all_to_all | solution.py:17
  168.8 1.6 fusion.9
  170.4 0.7 add_convert_fusion
  171.1 4.6 %all_to_all.51 = bf16[2,32,8,1024]{3,2,1,0:T(8,128)(2,1)S(1)} all-to-all(bf16[2,32,8,1024]{3,2,1,0:T(8,128)(2,1)S(1)} %bitcast.111), channel_id=1, replica_groups=mesh['x'=4,'y'=8,'c'=2,'z'=8] {'c'}, dimensions={0} | all-to-all | bytes 2097152 | tf_op jit(solution)/shard_map/all_to_all | solution.py:109
  175.7 0.2 reduce_sum.90
  176.0 22.5 %all_to_all.52 = bf16[32,8,1024]{2,1,0:T(8,128)(2,1)S(1)} all-to-all(bf16[32,8,1024]{2,1,0:T(8,128)(2,1)S(1)} %reduce_sum.90), channel_id=1, replica_groups=mesh['x'=4,'y'=8,'c'=2,'z'=8] {'x','y'}, dimensions={0} | all-to-all | bytes 1048576 | tf_op jit(solution)/shard_map/all_to_all | solution.py:111
  198.5 0.7 reduce_sum.91
  (33 shorter events, 0.3 us)
Async XLA Ops:
  6.5 163.9 %copy-start = (bf16[448,1024]{1,0:T(8,128)(2,1)S(1)}, bf16[448,1024]{1,0:T(8,128)(2,1)}, u32[]{:S(2)}) copy-start(bf16[448,1024]{1,0:T(8,128)(2,1)} %param.15) | copy-start | bytes 2752516
  6.5 29.2 %copy-start.4 = (s32[512,1]{0,1:T(1,128)S(1)}, s32[512,1]{0,1:T(1,128)}, u32[]{:S(2)}) copy-start(s32[512,1]{0,1:T(1,128)} %param.22) | copy-start | bytes 6148
  6.5 30.0 %copy-start.5 = (s32[64]{0:T(128)S(1)}, s32[64]{0:T(128)}, u32[]{:S(2)}) copy-start(s32[64]{0:T(128)} %param.23) | copy-start | bytes 772
  6.5 46.8 %copy-start.2 = (bf16[1,1024,64]{1,2,0:T(8,128)(2,1)S(1)}, bf16[1,1024,64]{1,2,0:T(8,128)(2,1)}, u32[]{:S(2)}) copy-start(bf16[1,1024,64]{1,2,0:T(8,128)(2,1)} %param.17) | copy-start | bytes 393220
  6.5 47.0 %copy-start.3 = (bf16[1,1024,64]{1,2,0:T(8,128)(2,1)S(1)}, bf16[1,1024,64]{1,2,0:T(8,128)(2,1)}, u32[]{:S(2)}) copy-start(bf16[1,1024,64]{1,2,0:T(8,128)(2,1)} %param.16) | copy-start | bytes 393220
  6.5 45.2 %all-gather.2.cloned.1.call-start = ((), (), s32[]{:S(2)}) async-start(), calls=%async_computation.9 | async-start | bytes 1572864 | tf_op jit(solution)/shard_map/all_gather | solution.py:36
  38.3 52.1 %copy-start.8 = (bf16[64,8,448]{2,1,0:T(8,128)(2,1)S(1)}, bf16[64,8,448]{2,1,0:T(8,128)(2,1)}, u32[]{:S(2)}) copy-start(bf16[64,8,448]{2,1,0:T(8,128)(2,1)} %param.18) | copy-start | bytes 1376260
  69.8 19.2 %all-to-all-start.2 = ((bf16[64,2,192]{2,1,0:T(2,128)(2,1)}), bf16[64,2,192]{2,1,0:T(2,128)(2,1)S(1)}, u32[]{:S(2)}, u32[]{:S(2)}) async-start(bf16[64,2,192]{2,1,0:T(2,128)(2,1)} %reshape.136), calls=%async_computation.2 | async-start | bytes 131072 | tf_op jit(solution)/shard_map/all_to_all | solution.py:17
  89.7 2.7 %copy-start.1 = (bf16[512,1024]{1,0:T(8,128)(2,1)S(1)}, bf16[512,1024]{1,0:T(8,128)(2,1)}, u32[]{:S(2)}) copy-start(bf16[512,1024]{1,0:T(8,128)(2,1)} %all-gather.2.cloned.1.call-done) | copy-start | bytes 3145732
  89.7 2.7 %copy-start.6 = (bf16[448,1024]{1,0:T(8,128)(2,1)S(1)}, bf16[448,1024]{1,0:T(8,128)(2,1)}, u32[]{:S(2)}) copy-start(bf16[448,1024]{1,0:T(8,128)(2,1)} %param.13) | copy-start | bytes 2752516
  92.4 1.2 copy-start.7
  94.3 48.2 %copy-start.9 = (bf16[448,64,8]{0,2,1:T(8,128)(2,1)S(1)}, bf16[448,64,8]{0,2,1:T(8,128)(2,1)}, u32[]{:S(2)}) copy-start(bf16[448,64,8]{0,2,1:T(8,128)(2,1)} %param.20) | copy-start | bytes 1376260
Sparse Core Ops, SparseCore 0:
  35.3 16.4 all-gather.1

commit v2 on v1

--- a/solution.py
+++ b/solution.py
@@ -32,15 +32,23 @@
     rank_part = b_gate.shape[1]
     slots = owner_map.shape[0]
 
+    swap = [(0, 1), (1, 0)]
     half = spread(inputs, CHIPS, chips).reshape(chips * own_rows, width)
-    piece = lax.all_gather(half, "c", axis=0, tiled=True)
+    piece = jnp.concatenate([half, lax.ppermute(half, "c", swap)], axis=0)
 
-    adapter = adapter_ids[:, 0].reshape(chips, cores, own_rows).transpose(1, 0, 2).reshape(rows)
+    adapter = adapter_ids[:, 0]
     table = jnp.arange(slots, dtype=jnp.int32)
     row_slot = jnp.sum(jnp.where(adapter[:, None] == table[None, :], owner_map[None, :], 0), axis=1)
     onehot = (row_slot[:, None] == table[None, :]).astype(jnp.int32)
     position = jnp.sum((jnp.cumsum(onehot, axis=0) - onehot) * onehot, axis=1)
     place = row_slot * OCAP + position
+
+    def ordered(values):
+        by_core = values.reshape(chips, cores, own_rows).transpose(1, 0, 2)
+        by_core = by_core.reshape(cores, chips * own_rows)
+        return jnp.where(lax.axis_index("c") == 0, by_core, by_core[::-1]).reshape(rows)
+
+    row_slot, place = ordered(row_slot), ordered(place)
     places = (place[:, None] == jnp.arange(slots * OCAP, dtype=jnp.int32)[None, :]).astype(BF16)
     mine = (
         place[:, None] == here_owner * OCAP + jnp.arange(OCAP, dtype=jnp.int32)[None, :]
@@ -105,10 +113,9 @@
     out = lax.dot_general(hidden_all, w_down, TN, preferred_element_type=F32) + jnp.dot(
         rank_mine, b_down[0], preferred_element_type=F32
     )
-    out = out.astype(BF16).reshape(cores, chips, own_rows, width)
-    out = lax.all_to_all(out, "c", 0, 0, tiled=True)
-    out = jnp.sum(out.astype(F32), axis=0).astype(BF16)
-    out = lax.all_to_all(out, CHIPS, 0, 0, tiled=True)
+    kept, given = out[: rows // cores], out[rows // cores :].astype(BF16)
+    out = (kept + lax.ppermute(given, "c", swap).astype(F32)).astype(BF16)
+    out = lax.all_to_all(out.reshape(chips, own_rows, width), CHIPS, 0, 0, tiled=True)
     return jnp.sum(out.astype(F32), axis=0).astype(BF16)
 
 

time: 207 us -> 179 us (0.86)
  blocking collectives: 142 us -> 95.3 us
  starting transfers between devices: 10.3 us -> 29.6 us
  between operations: 13.7 us -> 0.4 us
  waiting for transfers between devices: 22.4 us -> 34.9 us
    all_to_all x3 -> x2, blocking collectives: 56.8 us -> 29.1 us  [spread(): return lax.all_to_all(copies, axes, 0, 0, tiled=True)]
    all_to_all x3 -> x1, blocking collectives: 42 us -> 22.5 us  [per_device(): lax.all_to_all(out.reshape(chips, own_rows, width), CHIPS, 0, 0, tiled=True)]
    all_to_all x1 -> x2, waiting for transfers between devices: 8.92 us -> 23.7 us  [spread(): return lax.all_to_all(copies, axes, 0, 0, tiled=True)]
    all_gather x1 -> x0, waiting for transfers between devices: 13.4 us -> none  [per_device(): piece = lax.all_gather(half, 'c', axis=0, tiled=True)]
    all_to_all x0 -> x1, starting transfers between devices: none -> 10.3 us  [per_device(): shrunk = lax.all_to_all(shrunk, 'z', 0, 0, tiled=True)]
    all_to_all x0 -> x1, waiting for transfers between devices: none -> 7.72 us  [per_device(): shrunk = lax.all_to_all(shrunk, 'z', 0, 0, tiled=True)]
    all_to_all x1 -> x2, starting transfers between devices: 10.2 us -> 15.4 us  [spread(): return lax.all_to_all(copies, axes, 0, 0, tiled=True)]
    ppermute x0 -> x2, starting transfers between devices: none -> 3.83 us  [the longest x1 1.92 us: per_device(): out = (kept + lax.ppermute(given, 'c', swap).astype(F32)).astype(BF16)]
  transfers between devices with their start and end apart: 2 -> 5, of which waited for: 2 -> 5; matrix products, arithmetic and copies ran while one was open for 2% -> 2% of each run, Pallas kernels for 0% -> 0%
where the time goes in v2:
time: 179 us; the launch traced here: 178 us
  blocking collectives  95.3 us (53%)
  waiting for transfers between devices  34.9 us (19%)
  starting transfers between devices  29.6 us (17%)
  matrix products  9.18 us (5%)
  local copies, waits for them, and re-layouts  5.75 us (3%)
  other arithmetic  3.42 us (2%)
    all_to_all x2, blocking collectives, spread(): return lax.all_to_all(copies, axes, 0, 0, tiled=True)  29.1 us
    all_to_all x1, blocking collectives, per_device(): both = lax.all_to_all(both, 'z', 0, 0, tiled=True)  29 us
    all_to_all x2, waiting for transfers between devices, spread(): return lax.all_to_all(copies, axes, 0, 0, tiled=True)  23.7 us
    all_to_all x1, blocking collectives, per_device(): lax.all_to_all(out.reshape(chips, own_rows, width), CHIPS, 0, 0, tiled=True)  22.5 us
    all_to_all x2, starting transfers between devices, spread(): return lax.all_to_all(copies, axes, 0, 0, tiled=True)  15.4 us
    all_to_all x1, blocking collectives, per_device(): lax.all_to_all(rank_sent.reshape(owners, OCAP, rank_part), OWN, 0, 0, til...  14.7 us
    all_to_all x1, starting transfers between devices, per_device(): shrunk = lax.all_to_all(shrunk, 'z', 0, 0, tiled=True)  10.3 us
    all_to_all x1, waiting for transfers between devices, per_device(): shrunk = lax.all_to_all(shrunk, 'z', 0, 0, tiled=True)  7.72 us
  transfers between devices with their start and end apart: 5, of which 5 were waited for; matrix products, arithmetic and copies ran while one was open for 2% of the time, Pallas kernels for 0%

profile of v2, /device:TPU:8, one launch (start us, length us, event | category | flops | bytes accessed | tf_op | source)
XLA Modules:
  0.0 178.5 jit_solution(10843472041966286839)
XLA Ops:
  0.0 1.7 broadcast_in_dim.22
  1.7 10.2 %all-to-all-start = ((bf16[32,8,1024]{2,1,0:T(8,128)(2,1)}), bf16[32,8,1024]{2,1,0:T(8,128)(2,1)S(1)}, u32[]{:S(2)}, u32[]{:S(2)}) async-start(bf16[32,8,1024]{2,1,0:T(8,128)(2,1)} %broadcast_in_dim.22), calls=%async_computation | async-start | bytes 1048576 | tf_op jit(solution)/shard_map/all_to_all | solution.py:17
  11.9 0.8 select_reduce_fusion
  12.6 0.1 reshape.124
  12.8 0.1 reshape.125
  13.0 1.2 reduce-window.6
  14.2 0.2 slice_reduce_fusion
  14.5 0.1 fusion.30
  14.6 0.1 reduce_sum.76
  14.7 14.8 %all-to-all-done = bf16[32,8,1024]{2,1,0:T(8,128)(2,1)S(1)} async-done(((bf16[32,8,1024]{2,1,0:T(8,128)(2,1)}), bf16[32,8,1024]{2,1,0:T(8,128)(2,1)S(1)}, u32[]{:S(2)}, u32[]{:S(2)}) %all-to-all-start) | async-done | bytes 524320 | tf_op jit(solution)/shard_map/all_to_all | solution.py:17
  29.5 1.9 %collective-permute-start = (bf16[256,1024]{1,0:T(8,128)(2,1)S(1)}, bf16[256,1024]{1,0:T(8,128)(2,1)S(1)}, u32[]{:S(2)}, u32[]{:S(2)}) collective-permute-start(bf16[256,1024]{1,0:T(8,128)(2,1)S(1)} %bitcast.120), channel_id=1, source_target_pairs={{0,8},{8,0},{1,9},{9,1},{2,10},{10,2},{3,11},{11,3},{4,12},{12,4},... | collective-permute-start | bytes 1572872 | tf_op jit(solution)/shard_map/ppermute | solution.py:37
  31.4 0.1 reshape.127
  31.6 1.6 collective-permute-done
  33.3 0.4 fusion.10
  33.7 0.2 fusion.13
  33.9 0.2 fusion.12
  34.0 0.7 reshape.141
  34.8 10.3 %all-to-all-start.1 = ((bf16[8,2,192]{2,1,0:T(2,128)(2,1)}), bf16[8,2,192]{2,1,0:T(2,128)(2,1)S(1)}, u32[]{:S(2)}, u32[]{:S(2)}) async-start(bf16[8,2,192]{2,1,0:T(2,128)(2,1)} %reshape.141), calls=%async_computation.1 | async-start | bytes 16384 | tf_op jit(solution)/shard_map/all_to_all | solution.py:67
  45.1 7.7 %all-to-all-done.1 = bf16[8,2,192]{2,1,0:T(2,128)(2,1)S(1)} async-done(((bf16[8,2,192]{2,1,0:T(2,128)(2,1)}), bf16[8,2,192]{2,1,0:T(2,128)(2,1)S(1)}, u32[]{:S(2)}, u32[]{:S(2)}) %all-to-all-start.1) | async-done | bytes 6176 | tf_op jit(solution)/shard_map/all_to_all | solution.py:67
  52.8 0.1 reshape.142
  53.0 0.9 reshape.143
  53.8 5.3 %all-to-all-start.2 = ((bf16[64,2,192]{2,1,0:T(2,128)(2,1)}), bf16[64,2,192]{2,1,0:T(2,128)(2,1)S(1)}, u32[]{:S(2)}, u32[]{:S(2)}) async-start(bf16[64,2,192]{2,1,0:T(2,128)(2,1)} %reshape.143), calls=%async_computation.2 | async-start | bytes 131072 | tf_op jit(solution)/shard_map/all_to_all | solution.py:17
  59.2 8.9 %all-to-all-done.2 = bf16[64,2,192]{2,1,0:T(2,128)(2,1)S(1)} async-done(((bf16[64,2,192]{2,1,0:T(2,128)(2,1)}), bf16[64,2,192]{2,1,0:T(2,128)(2,1)S(1)}, u32[]{:S(2)}, u32[]{:S(2)}) %all-to-all-start.2) | async-done | bytes 49184 | tf_op jit(solution)/shard_map/all_to_all | solution.py:17
  68.0 0.2 reshape.144
  68.4 0.3 reshape.130
  68.7 0.7 fusion.11
  69.4 1.5 convolution_bitcast_fusion.2
  70.9 1.5 convolution_bitcast_fusion.1
  72.5 0.7 fusion.6
  73.1 0.5 copy-done.4
  73.6 0.7 fusion.7
  74.3 0.1 pad_maximum_fusion.1
  74.4 29.0 %all_to_all.40 = bf16[8,2,56,512]{3,2,1,0:T(8,128)(2,1)S(1)} all-to-all(bf16[8,2,56,512]{3,2,1,0:T(8,128)(2,1)S(1)} %pad_maximum_fusion.1), channel_id=1, replica_groups=mesh['x'=4,'y'=8,'c'=2,'z'=8] {'z'}, dimensions={0} | all-to-all | bytes 1835008 | tf_op jit(solution)/shard_map/all_to_all | solution.py:93
  103.4 0.1 convert_reduce_fusion
  103.6 18.9 %all_to_all.41 = bf16[8,56,512]{2,1,0:T(8,128)(2,1)S(1)} all-to-all(bf16[8,56,512]{2,1,0:T(8,128)(2,1)S(1)} %broadcast_in_dim.27), channel_id=1, replica_groups=mesh['x'=4,'y'=8,'c'=2,'z'=8] {'z'}, dimensions={0} | all-to-all | bytes 917504 | tf_op jit(solution)/shard_map/all_to_all | solution.py:17
  122.6 0.4 fusion.8
  123.0 0.6 fusion.2
  123.7 0.2 reshape.134
  123.9 0.1 copy.39
  124.0 14.7 %all_to_all.42 = bf16[64,24,8]{1,2,0:T(8,128)(2,1)S(1)} all-to-all(bf16[64,24,8]{1,2,0:T(8,128)(2,1)S(1)} %copy.39), channel_id=1, replica_groups=mesh['x'=4,'y'=8,'c'=2,'z'=8] {'x','y','c'}, dimensions={0} | all-to-all | bytes 49152 | tf_op jit(solution)/shard_map/all_to_all | solution.py:107
  138.7 10.1 %all_to_all.43 = bf16[8,24,8]{1,2,0:T(8,128)(2,1)S(1)} all-to-all(bf16[8,24,8]{1,2,0:T(8,128)(2,1)S(1)} %broadcast_in_dim.28), channel_id=1, replica_groups=mesh['x'=4,'y'=8,'c'=2,'z'=8] {'z'}, dimensions={0} | all-to-all | bytes 6144 | tf_op jit(solution)/shard_map/all_to_all | solution.py:17
  148.9 1.6 fusion.9
  150.5 0.7 convolution_add_fusion
  151.3 1.9 %collective-permute-start.1 = (bf16[256,1024]{1,0:T(8,128)(2,1)S(1)}, bf16[256,1024]{1,0:T(8,128)(2,1)S(1)}, u32[]{:S(2)}, u32[]{:S(2)}) collective-permute-start(bf16[256,1024]{1,0:T(8,128)(2,1)S(1)} %slice.55), channel_id=1, source_target_pairs={{0,8},{8,0},{1,9},{9,1},{2,10},{10,2},{3,11},{11,3},{4,12},{12,4},... | collective-permute-start | bytes 1572872 | tf_op jit(solution)/shard_map/ppermute | solution.py:117
  153.2 1.9 %collective-permute-done.1 = bf16[256,1024]{1,0:T(8,128)(2,1)S(1)} collective-permute-done((bf16[256,1024]{1,0:T(8,128)(2,1)S(1)}, bf16[256,1024]{1,0:T(8,128)(2,1)S(1)}, u32[]{:S(2)}, u32[]{:S(2)}) %collective-permute-start.1) | collective-permute-done | bytes 524320 | tf_op jit(solution)/shard_map/ppermute | solution.py:117
  155.1 0.1 fusion.15
  155.2 22.5 %all_to_all.44 = bf16[32,8,1024]{2,1,0:T(8,128)(2,1)S(1)} all-to-all(bf16[32,8,1024]{2,1,0:T(8,128)(2,1)S(1)} %fusion.15), channel_id=1, replica_groups=mesh['x'=4,'y'=8,'c'=2,'z'=8] {'x','y'}, dimensions={0} | all-to-all | bytes 1048576 | tf_op jit(solution)/shard_map/all_to_all | solution.py:118
  177.8 0.7 reduce_sum.81
  (38 shorter events, 0.7 us)
Async XLA Ops:
  0.0 150.5 %copy-start = (bf16[448,1024]{1,0:T(8,128)(2,1)S(1)}, bf16[448,1024]{1,0:T(8,128)(2,1)}, u32[]{:S(2)}) copy-start(bf16[448,1024]{1,0:T(8,128)(2,1)} %param.15) | copy-start | bytes 2752516
  0.0 33.6 %copy-start.1 = (bf16[1,1024,64]{1,2,0:T(8,128)(2,1)S(1)}, bf16[1,1024,64]{1,2,0:T(8,128)(2,1)}, u32[]{:S(2)}) copy-start(bf16[1,1024,64]{1,2,0:T(8,128)(2,1)} %param.17) | copy-start | bytes 393220
  0.0 33.8 %copy-start.2 = (bf16[1,1024,64]{1,2,0:T(8,128)(2,1)S(1)}, bf16[1,1024,64]{1,2,0:T(8,128)(2,1)}, u32[]{:S(2)}) copy-start(bf16[1,1024,64]{1,2,0:T(8,128)(2,1)} %param.16) | copy-start | bytes 393220
  1.7 27.8 %all-to-all-start = ((bf16[32,8,1024]{2,1,0:T(8,128)(2,1)}), bf16[32,8,1024]{2,1,0:T(8,128)(2,1)S(1)}, u32[]{:S(2)}, u32[]{:S(2)}) async-start(bf16[32,8,1024]{2,1,0:T(8,128)(2,1)} %broadcast_in_dim.22), calls=%async_computation | async-start | bytes 1048576 | tf_op jit(solution)/shard_map/all_to_all | solution.py:17
  29.5 3.8 %collective-permute-start = (bf16[256,1024]{1,0:T(8,128)(2,1)S(1)}, bf16[256,1024]{1,0:T(8,128)(2,1)S(1)}, u32[]{:S(2)}, u32[]{:S(2)}) collective-permute-start(bf16[256,1024]{1,0:T(8,128)(2,1)S(1)} %bitcast.120), channel_id=1, source_target_pairs={{0,8},{8,0},{1,9},{9,1},{2,10},{10,2},{3,11},{11,3},{4,12},{12,4},... | collective-permute-start | bytes 1572872 | tf_op jit(solution)/shard_map/ppermute | solution.py:37
  33.3 25.9 %copy-start.6 = (bf16[256,1024]{1,0:T(8,128)(2,1)}, bf16[256,1024]{1,0:T(8,128)(2,1)S(1)}, u32[]{:S(2)}) copy-start(bf16[256,1024]{1,0:T(8,128)(2,1)S(1)} %collective-permute-done) | copy-start | bytes 1572868
  34.8 18.0 %all-to-all-start.1 = ((bf16[8,2,192]{2,1,0:T(2,128)(2,1)}), bf16[8,2,192]{2,1,0:T(2,128)(2,1)S(1)}, u32[]{:S(2)}, u32[]{:S(2)}) async-start(bf16[8,2,192]{2,1,0:T(2,128)(2,1)} %reshape.141), calls=%async_computation.1 | async-start | bytes 16384 | tf_op jit(solution)/shard_map/all_to_all | solution.py:67
  53.8 14.2 %all-to-all-start.2 = ((bf16[64,2,192]{2,1,0:T(2,128)(2,1)}), bf16[64,2,192]{2,1,0:T(2,128)(2,1)S(1)}, u32[]{:S(2)}, u32[]{:S(2)}) async-start(bf16[64,2,192]{2,1,0:T(2,128)(2,1)} %reshape.143), calls=%async_computation.2 | async-start | bytes 131072 | tf_op jit(solution)/shard_map/all_to_all | solution.py:17
  68.7 3.8 %copy-start.3 = (bf16[448,1024]{1,0:T(8,128)(2,1)S(1)}, bf16[448,1024]{1,0:T(8,128)(2,1)}, u32[]{:S(2)}) copy-start(bf16[448,1024]{1,0:T(8,128)(2,1)} %param.13) | copy-start | bytes 2752516
  68.7 3.8 %copy-start.7 = (bf16[256,1024]{1,0:T(8,128)(2,1)S(1)}, bf16[256,1024]{1,0:T(8,128)(2,1)}, u32[]{:S(2)}) copy-start(bf16[256,1024]{1,0:T(8,128)(2,1)} %copy-done.6) | copy-start | bytes 1572868
  72.5 1.2 copy-start.4
  74.4 48.2 %copy-start.5 = (bf16[448,64,8]{0,2,1:T(8,128)(2,1)S(1)}, bf16[448,64,8]{0,2,1:T(8,128)(2,1)}, u32[]{:S(2)}) copy-start(bf16[448,64,8]{0,2,1:T(8,128)(2,1)} %param.20) | copy-start | bytes 1376260
  151.3 3.8 %collective-permute-start.1 = (bf16[256,1024]{1,0:T(8,128)(2,1)S(1)}, bf16[256,1024]{1,0:T(8,128)(2,1)S(1)}, u32[]{:S(2)}, u32[]{:S(2)}) collective-permute-start(bf16[256,1024]{1,0:T(8,128)(2,1)S(1)} %slice.55), channel_id=1, source_target_pairs={{0,8},{8,0},{1,9},{9,1},{2,10},{10,2},{3,11},{11,3},{4,12},{12,4},... | collective-permute-start | bytes 1572872 | tf_op jit(solution)/shard_map/ppermute | solution.py:117

commit v3 on v2

--- a/solution.py
+++ b/solution.py
@@ -4,6 +4,7 @@
 from jax.sharding import Mesh, PartitionSpec as P
 
 OCAP = 24
+LANES = 128
 F32 = jnp.float32
 BF16 = jnp.bfloat16
 NT = (((1,), (1,)), ((), ()))
@@ -32,6 +33,9 @@
     rank_part = b_gate.shape[1]
     slots = owner_map.shape[0]
 
+    down_shrink = lax.all_gather(a_down.reshape(units, slots * rank_part), "z", axis=0)
+    down_expand = lax.all_gather(b_down[0], OWN, axis=0)
+
     swap = [(0, 1), (1, 0)]
     half = spread(inputs, CHIPS, chips).reshape(chips * own_rows, width)
     piece = jnp.concatenate([half, lax.ppermute(half, "c", swap)], axis=0)
@@ -48,6 +52,7 @@
         by_core = by_core.reshape(cores, chips * own_rows)
         return jnp.where(lax.axis_index("c") == 0, by_core, by_core[::-1]).reshape(rows)
 
+    row_slot_all = row_slot
     row_slot, place = ordered(row_slot), ordered(place)
     places = (place[:, None] == jnp.arange(slots * OCAP, dtype=jnp.int32)[None, :]).astype(BF16)
     mine = (
@@ -66,7 +71,11 @@
     shrunk = shrunk.transpose(1, 0, 2, 3).reshape(parts, OCAP, 2 * rank_part).astype(BF16)
     shrunk = lax.all_to_all(shrunk, "z", 0, 0, tiled=True)
     shrunk = jnp.sum(shrunk.astype(F32), axis=0).astype(BF16)
-    low_all = spread(shrunk, OWN, owners).reshape(owners * OCAP, 2 * rank_part)
+    low_all = spread(shrunk, OWN, owners)
+    gate_base = lax.dot_general(w_gate, piece, NT, preferred_element_type=F32)
+    up_base = lax.dot_general(w_up, piece, NT, preferred_element_type=F32)
+    low_all, gate_base, up_base = lax.optimization_barrier((low_all, gate_base, up_base))
+    low_all = low_all.reshape(owners * OCAP, 2 * rank_part)
     low_rows = lax.dot_general(
         low_all, places, (((0,), (1,)), ((), ())), preferred_element_type=F32
     ).astype(BF16)
@@ -77,12 +86,8 @@
             weights.reshape(slots * rank_part, units), wide, TN, preferred_element_type=F32
         )
 
-    gate_part = lax.dot_general(w_gate, piece, NT, preferred_element_type=F32) + expand(
-        low_rows[:rank_part], b_gate
-    )
-    up_part = lax.dot_general(w_up, piece, NT, preferred_element_type=F32) + expand(
-        low_rows[rank_part:], b_up
-    )
+    gate_part = gate_base + expand(low_rows[:rank_part], b_gate)
+    up_part = up_base + expand(low_rows[rank_part:], b_up)
     both = jnp.stack(
         [
             gate_part.astype(BF16).reshape(parts, units // parts, rows),
@@ -95,28 +100,29 @@
     hidden = (jax.nn.silu(both[0]) * both[1]).astype(BF16)
     hidden_all = spread(hidden, "z", parts).reshape(units, rows)
 
-    rank_full = lax.dot_general(
-        a_down.reshape(units, slots * rank_part), hidden_all, TN, preferred_element_type=F32
-    )
-    rank_rows = jnp.sum(
-        rank_full.reshape(slots, rank_part, rows) * slot_rows.astype(F32)[:, None, :], axis=0
-    ).astype(BF16)
-    rank_sent = lax.dot_general(
-        places, rank_rows, (((0,), (1,)), ((), ())), preferred_element_type=F32
-    ).astype(BF16)
-    rank_sum = lax.all_to_all(
-        rank_sent.reshape(owners, OCAP, rank_part), OWN, 0, 0, tiled=True
-    )
-    rank_sum = jnp.sum(rank_sum.astype(F32), axis=0).astype(BF16)
-    rank_all = spread(rank_sum, "z", parts).transpose(1, 0, 2).reshape(OCAP, rank)
-    rank_mine = jnp.dot(mine, rank_all, preferred_element_type=F32).astype(BF16)
-    out = lax.dot_general(hidden_all, w_down, TN, preferred_element_type=F32) + jnp.dot(
-        rank_mine, b_down[0], preferred_element_type=F32
-    )
+    slot_mask = slot_rows.astype(F32)[:, None, :]
+
+    def shrink(block):
+        full = lax.dot_general(block, hidden_all, TN, preferred_element_type=F32)
+        return jnp.sum(full.reshape(slots, rank_part, rows) * slot_mask, axis=0)
+
+    low_width = -(-rank // LANES) * LANES
+    low = jnp.concatenate([shrink(down_shrink[k]) for k in range(parts)], axis=0).astype(BF16)
+    low = lax.dot_general(low, jnp.eye(rank, low_width, dtype=BF16), TN, preferred_element_type=F32)
+    out = lax.dot_general(hidden_all, w_down, TN, preferred_element_type=F32)
+    out = jnp.concatenate([out, low], axis=1)
     kept, given = out[: rows // cores], out[rows // cores :].astype(BF16)
     out = (kept + lax.ppermute(given, "c", swap).astype(F32)).astype(BF16)
-    out = lax.all_to_all(out.reshape(chips, own_rows, width), CHIPS, 0, 0, tiled=True)
-    return jnp.sum(out.astype(F32), axis=0).astype(BF16)
+    out = lax.all_to_all(out.reshape(chips, own_rows, width + low_width), CHIPS, 0, 0, tiled=True)
+    out = jnp.sum(out.astype(F32), axis=0)
+    low = out[:, width : width + rank].astype(BF16)
+    own_slot = lax.dynamic_slice(row_slot_all, (here_owner * own_rows,), (own_rows,))
+    own_hot = (own_slot[:, None] == table[None, :]).astype(BF16)
+    wide = (own_hot[:, :, None] * low[:, None, :]).reshape(own_rows, slots * rank)
+    delta = jnp.dot(
+        wide, down_expand.reshape(slots * rank, width), preferred_element_type=F32
+    )
+    return (out[:, :width] + delta).astype(BF16)
 
 
 def solution(mesh):

time: 179 us -> 181 us (1.011)
  the two profiles are of different devices: /device:TPU:8 before, /device:TPU:1 now
where the time goes in v3:
time: 181 us; the launch traced here: 180 us
  waiting for transfers between devices  47.6 us (26%)
  blocking collectives  47.5 us (26%)
  starting transfers between devices  39.9 us (22%)
  matrix products  20.7 us (11%)
  between operations  13.9 us (8%)
  local copies, waits for them, and re-layouts  7.13 us (4%)
  other arithmetic  3.64 us (2%)
    all_to_all x1, blocking collectives, per_device(): both = lax.all_to_all(both, 'z', 0, 0, tiled=True)  28.8 us
    all_to_all x2, waiting for transfers between devices, spread(): return lax.all_to_all(copies, axes, 0, 0, tiled=True)  19.7 us
    all_to_all x1, blocking collectives, spread(): return lax.all_to_all(copies, axes, 0, 0, tiled=True)  18.8 us
    all_to_all x1, waiting for transfers between devices, per_device(): lax.all_to_all(out.reshape(chips, own_rows, width + low_width), CHIPS, 0,...  18.4 us
    all_to_all x2, starting transfers between devices, spread(): return lax.all_to_all(copies, axes, 0, 0, tiled=True)  18.1 us
    all_to_all x1, starting transfers between devices, per_device(): shrunk = lax.all_to_all(shrunk, 'z', 0, 0, tiled=True)  10 us
    dot_general x8, matrix products, shrink(): full = lax.dot_general(block, hidden_all, TN, preferred_element_type=F32)  6.26 us
    ppermute x1, starting transfers between devices, per_device(): piece = jnp.concatenate([half, lax.ppermute(half, 'c', swap)], axis=0)  5.41 us
  transfers between devices with their start and end apart: 8, of which 7 were waited for; matrix products, arithmetic and copies ran while one was open for 13% of the time, Pallas kernels for 0%

profile of v3, /device:TPU:1, one launch (start us, length us, event | category | flops | bytes accessed | tf_op | source)
XLA Modules:
  0.0 180.5 jit_solution(3918206426492335529)
XLA Ops:
  6.5 2.1 %copy.42 = bf16[1,448,512]{2,1,0:T(8,128)(2,1)} copy(bf16[1,448,512]{1,2,0:T(8,128)(2,1)} %bitcast.222) | data formatting | bytes 917504 | tf_op jit(solution)/shard_map/all_gather;reshape | solution.py:36
  8.7 0.7 all-gather.5.cloned.1.call-update
  9.5 1.7 broadcast_in_dim.22
  11.1 10.5 %all-to-all-start = ((bf16[32,8,1024]{2,1,0:T(8,128)(2,1)}), bf16[32,8,1024]{2,1,0:T(8,128)(2,1)S(1)}, u32[]{:S(2)}, u32[]{:S(2)}) async-start(bf16[32,8,1024]{2,1,0:T(8,128)(2,1)} %broadcast_in_dim.22), calls=%async_computation | async-start | bytes 1048576 | tf_op jit(solution)/shard_map/all_to_all | solution.py:18
  21.9 1.2 reduce-window.6
  23.1 0.2 slice_reduce_fusion
  23.4 0.1 fusion.42
  23.5 0.1 reduce_sum.127
  24.1 11.9 %all-to-all-done = bf16[32,8,1024]{2,1,0:T(8,128)(2,1)S(1)} async-done(((bf16[32,8,1024]{2,1,0:T(8,128)(2,1)}), bf16[32,8,1024]{2,1,0:T(8,128)(2,1)S(1)}, u32[]{:S(2)}, u32[]{:S(2)}) %all-to-all-start) | async-done | bytes 524320 | tf_op jit(solution)/shard_map/all_to_all | solution.py:18
  36.0 5.4 %collective-permute-start = (bf16[256,1024]{1,0:T(8,128)(2,1)S(1)}, bf16[256,1024]{1,0:T(8,128)(2,1)}, u32[]{:S(2)}, u32[]{:S(2)}) collective-permute-start(bf16[256,1024]{1,0:T(8,128)(2,1)S(1)} %bitcast.218), channel_id=1, source_target_pairs={{0,8},{8,0},{1,9},{9,1},{2,10},{10,2},{3,11},{11,3},{4,12},{12,4},... | collective-permute-start | bytes 1572872 | tf_op jit(solution)/shard_map/ppermute | solution.py:41
  41.4 0.7 fusion.57
  42.1 0.9 collective-permute-done
  43.0 1.4 fusion.26
  44.5 0.2 fusion.28
  44.7 0.2 fusion.29
  44.9 0.7 reshape.179
  45.6 10.0 %all-to-all-start.1 = ((bf16[8,2,192]{2,1,0:T(2,128)(2,1)}), bf16[8,2,192]{2,1,0:T(2,128)(2,1)S(1)}, u32[]{:S(2)}, u32[]{:S(2)}) async-start(bf16[8,2,192]{2,1,0:T(2,128)(2,1)} %reshape.179), calls=%async_computation.1 | async-start | bytes 16384 | tf_op jit(solution)/shard_map/all_to_all | solution.py:72
  55.6 1.7 convolution_bitcast_fusion.10
  57.3 4.9 %all-to-all-done.1 = bf16[8,2,192]{2,1,0:T(2,128)(2,1)S(1)} async-done(((bf16[8,2,192]{2,1,0:T(2,128)(2,1)}), bf16[8,2,192]{2,1,0:T(2,128)(2,1)S(1)}, u32[]{:S(2)}, u32[]{:S(2)}) %all-to-all-start.1) | async-done | bytes 6176 | tf_op jit(solution)/shard_map/all_to_all | solution.py:72
  62.4 0.9 reshape.181
  63.3 7.6 %all-to-all-start.2 = ((bf16[64,2,192]{2,1,0:T(2,128)(2,1)}), bf16[64,2,192]{2,1,0:T(2,128)(2,1)S(1)}, u32[]{:S(2)}, u32[]{:S(2)}) async-start(bf16[64,2,192]{2,1,0:T(2,128)(2,1)} %reshape.181), calls=%async_computation.2 | async-start | bytes 131072 | tf_op jit(solution)/shard_map/all_to_all | solution.py:18
  70.9 2.0 %convolution_bitcast_fusion.11 = f32[448,512]{1,0:T(8,128)S(1)} fusion(bf16[448,1024]{1,0:T(8,128)(2,1)} %param.13, bf16[256,1024]{1,0:T(8,128)(2,1)} %collective-permute-done, bf16[256,1024]{1,0:T(8,128)(2,1)S(1)} %bitcast.221), kind=kOutput, calls=%fused_computation.25 | convolution fusion | flops 471859200 | bytes 2883584 | tf_op jit(solution)/shard_map/dot_general | solution.py:75
  72.9 7.8 %all-to-all-done.2 = bf16[64,2,192]{2,1,0:T(2,128)(2,1)S(1)} async-done(((bf16[64,2,192]{2,1,0:T(2,128)(2,1)}), bf16[64,2,192]{2,1,0:T(2,128)(2,1)S(1)}, u32[]{:S(2)}, u32[]{:S(2)}) %all-to-all-start.2) | async-done | bytes 49184 | tf_op jit(solution)/shard_map/all_to_all | solution.py:18
  80.7 0.2 reshape.182
  81.0 0.3 reshape.163
  81.3 0.7 fusion.27
  82.1 1.5 fusion.13
  83.6 0.5 fusion.12
  84.1 28.8 %all_to_all.30 = bf16[8,2,56,512]{3,2,1,0:T(8,128)(2,1)S(1)} all-to-all(bf16[8,2,56,512]{3,2,1,0:T(8,128)(2,1)S(1)} %pad_maximum_fusion.2), channel_id=1, replica_groups=mesh['x'=4,'y'=8,'c'=2,'z'=8] {'z'}, dimensions={0} | all-to-all | bytes 1835008 | tf_op jit(solution)/shard_map/all_to_all | solution.py:98
  112.9 0.1 convert_reduce_fusion
  113.1 18.8 %all_to_all.31 = bf16[8,56,512]{2,1,0:T(8,128)(2,1)S(1)} all-to-all(bf16[8,56,512]{2,1,0:T(8,128)(2,1)S(1)} %broadcast_in_dim.25), channel_id=1, replica_groups=mesh['x'=4,'y'=8,'c'=2,'z'=8] {'z'}, dimensions={0} | all-to-all | bytes 917504 | tf_op jit(solution)/shard_map/all_to_all | solution.py:18
  131.9 0.7 fusion.63
  132.7 1.7 fusion.14
  134.4 1.6 fusion.15
  136.1 0.5 fusion.16
  136.6 0.5 fusion.17
  137.1 0.5 fusion.18
  137.6 0.5 fusion.19
  138.1 0.5 fusion.20
  138.6 0.5 fusion.21
  139.1 0.2 fusion.55
  139.4 2.5 %collective-permute-start.1 = (bf16[256,1152]{1,0:T(8,128)(2,1)S(1)}, bf16[256,1152]{1,0:T(8,128)(2,1)S(1)}, u32[]{:S(2)}, u32[]{:S(2)}) collective-permute-start(bf16[256,1152]{1,0:T(8,128)(2,1)S(1)} %fusion.25), channel_id=1, source_target_pairs={{0,8},{8,0},{1,9},{9,1},{2,10},{10,2},{3,11},{11,3},{4,12},{12,4},... | collective-permute-start | bytes 1769480 | tf_op jit(solution)/shard_map/ppermute | solution.py:115
  141.9 1.6 collective-permute-done.1
  143.5 1.0 fusion.30
  144.5 3.9 %all-to-all-start.5 = ((bf16[32,8,1152]{2,1,0:T(8,128)(2,1)}), bf16[32,8,1152]{2,1,0:T(8,128)(2,1)S(1)}, u32[]{:S(2)}, u32[]{:S(2)}) async-start(bf16[32,8,1152]{2,1,0:T(8,128)(2,1)} %fusion.30), calls=%async_computation.5 | async-start | bytes 1179648 | tf_op jit(solution)/shard_map/all_to_all | solution.py:116
  148.5 18.4 %all-to-all-done.5 = bf16[32,8,1152]{2,1,0:T(8,128)(2,1)S(1)} async-done(((bf16[32,8,1152]{2,1,0:T(8,128)(2,1)}), bf16[32,8,1152]{2,1,0:T(8,128)(2,1)S(1)}, u32[]{:S(2)}, u32[]{:S(2)}) %all-to-all-start.5) | async-done | bytes 589856 | tf_op jit(solution)/shard_map/all_to_all | solution.py:116
  166.9 1.4 all-gather.5.cloned.1.call-done
  168.3 5.4 %fusion.54 = bf16[8,1024]{1,0:T(8,128)(2,1)} fusion(f32[8,1152]{1,0:T(8,128)S(1)} %convert_reduce_fusion.1, bf16[64,64,1024]{2,1,0:T(8,128)(2,1)} %all-gather.5.cloned.1.call-done, bf16[8,64]{1,0:T(8,128)(2,1)S(1)} %slice.134, bf16[8,64]{0,1:T(8,128)(2,1)S(1)} %fusion.56), kind=kOutput, calls=%fused_computation.96 | convolution fusion | flops 67158016 | bytes 8439808 | tf_op jit(solution)/shard_map/dot_general | solution.py:122
  (60 shorter events, 1.4 us)
Async XLA Ops:
  6.5 125.4 %copy-start = (bf16[448,1024]{1,0:T(8,128)(2,1)S(1)}, bf16[448,1024]{1,0:T(8,128)(2,1)}, u32[]{:S(2)}) copy-start(bf16[448,1024]{1,0:T(8,128)(2,1)} %param.15) | copy-start | bytes 2752516
  6.5 15.1 %copy-start.5 = (s32[512,1]{0,1:T(1,128)S(1)}, s32[512,1]{0,1:T(1,128)}, u32[]{:S(2)}) copy-start(s32[512,1]{0,1:T(1,128)} %param.22) | copy-start | bytes 6148
  6.5 15.1 %copy-start.6 = (s32[64]{0:T(128)S(1)}, s32[64]{0:T(128)}, u32[]{:S(2)}) copy-start(s32[64]{0:T(128)} %param.23) | copy-start | bytes 772
  6.5 126.1 %all-gather.3.cloned.1.call-start = ((), (), s32[]{:S(2)}) async-start(), calls=%async_computation.6 | async-start | bytes 4128768 | tf_op jit(solution)/shard_map/all_gather | solution.py:36
  8.7 35.8 %copy-start.2 = (bf16[1,1024,64]{1,2,0:T(8,128)(2,1)S(1)}, bf16[1,1024,64]{1,2,0:T(8,128)(2,1)}, u32[]{:S(2)}) copy-start(bf16[1,1024,64]{1,2,0:T(8,128)(2,1)} %param.16) | copy-start | bytes 393220
  8.7 159.6 %all-gather.5.cloned.1.call-start = ((), (), s32[]{:S(2)}) async-start(), calls=%async_computation.7 | async-start | bytes 8519680 | tf_op jit(solution)/shard_map/all_gather | solution.py:37
  9.4 35.2 %copy-start.3 = (bf16[1,1024,64]{1,2,0:T(8,128)(2,1)S(1)}, bf16[1,1024,64]{1,2,0:T(8,128)(2,1)}, u32[]{:S(2)}) copy-start(bf16[1,1024,64]{1,2,0:T(8,128)(2,1)} %param.17) | copy-start | bytes 393220
  9.5 46.1 %copy-start.8 = (bf16[448,1024]{1,0:T(8,128)(2,1)S(1)}, bf16[448,1024]{1,0:T(8,128)(2,1)}, u32[]{:S(2)}) copy-start(bf16[448,1024]{1,0:T(8,128)(2,1)} %param.14) | copy-start | bytes 2752516
  11.1 24.8 %all-to-all-start = ((bf16[32,8,1024]{2,1,0:T(8,128)(2,1)}), bf16[32,8,1024]{2,1,0:T(8,128)(2,1)S(1)}, u32[]{:S(2)}, u32[]{:S(2)}) async-start(bf16[32,8,1024]{2,1,0:T(8,128)(2,1)} %broadcast_in_dim.22), calls=%async_computation | async-start | bytes 1048576 | tf_op jit(solution)/shard_map/all_to_all | solution.py:18
  36.0 7.1 %collective-permute-start = (bf16[256,1024]{1,0:T(8,128)(2,1)S(1)}, bf16[256,1024]{1,0:T(8,128)(2,1)}, u32[]{:S(2)}, u32[]{:S(2)}) collective-permute-start(bf16[256,1024]{1,0:T(8,128)(2,1)S(1)} %bitcast.218), channel_id=1, source_target_pairs={{0,8},{8,0},{1,9},{9,1},{2,10},{10,2},{3,11},{11,3},{4,12},{12,4},... | collective-permute-start | bytes 1572872 | tf_op jit(solution)/shard_map/ppermute | solution.py:41
  45.6 16.7 %all-to-all-start.1 = ((bf16[8,2,192]{2,1,0:T(2,128)(2,1)}), bf16[8,2,192]{2,1,0:T(2,128)(2,1)S(1)}, u32[]{:S(2)}, u32[]{:S(2)}) async-start(bf16[8,2,192]{2,1,0:T(2,128)(2,1)} %reshape.179), calls=%async_computation.1 | async-start | bytes 16384 | tf_op jit(solution)/shard_map/all_to_all | solution.py:72
  63.3 17.4 %all-to-all-start.2 = ((bf16[64,2,192]{2,1,0:T(2,128)(2,1)}), bf16[64,2,192]{2,1,0:T(2,128)(2,1)S(1)}, u32[]{:S(2)}, u32[]{:S(2)}) async-start(bf16[64,2,192]{2,1,0:T(2,128)(2,1)} %reshape.181), calls=%async_computation.2 | async-start | bytes 131072 | tf_op jit(solution)/shard_map/all_to_all | solution.py:18
  81.3 2.2 %copy-start.1 = (bf16[64,8,448]{2,1,0:T(8,128)(2,1)S(1)}, bf16[64,8,448]{2,1,0:T(8,128)(2,1)}, u32[]{:S(2)}) copy-start(bf16[64,8,448]{2,1,0:T(8,128)(2,1)} %param.19) | copy-start | bytes 1376260
  132.7 3.4 %copy-start.4 = (f32[64,512]{1,0:T(8,128)S(1)}, f32[64,512]{1,0:T(8,128)}, u32[]{:S(2)}) copy-start(f32[64,512]{1,0:T(8,128)} %get-tuple-element.13) | copy-start | bytes 393220
  132.7 3.4 %copy-start.7 = (bf16[8,448,512]{2,1,0:T(8,128)(2,1)S(1)}, bf16[8,448,512]{2,1,0:T(8,128)(2,1)}, u32[]{:S(2)}) copy-start(bf16[8,448,512]{2,1,0:T(8,128)(2,1)} %all-gather.3.cloned.1.call-done) | copy-start | bytes 11010052
  139.4 4.1 %collective-permute-start.1 = (bf16[256,1152]{1,0:T(8,128)(2,1)S(1)}, bf16[256,1152]{1,0:T(8,128)(2,1)S(1)}, u32[]{:S(2)}, u32[]{:S(2)}) collective-permute-start(bf16[256,1152]{1,0:T(8,128)(2,1)S(1)} %fusion.25), channel_id=1, source_target_pairs={{0,8},{8,0},{1,9},{9,1},{2,10},{10,2},{3,11},{11,3},{4,12},{12,4},... | collective-permute-start | bytes 1769480 | tf_op jit(solution)/shard_map/ppermute | solution.py:115
  144.5 22.4 %all-to-all-start.5 = ((bf16[32,8,1152]{2,1,0:T(8,128)(2,1)}), bf16[32,8,1152]{2,1,0:T(8,128)(2,1)S(1)}, u32[]{:S(2)}, u32[]{:S(2)}) async-start(bf16[32,8,1152]{2,1,0:T(8,128)(2,1)} %fusion.30), calls=%async_computation.5 | async-start | bytes 1179648 | tf_op jit(solution)/shard_map/all_to_all | solution.py:116
Sparse Core Ops, SparseCore 0:
  9.4 59.1 all-gather.2
  72.0 96.2 all-gather.4

commit v4 on v2

v4 whole, which is shorter than its diff:
```python
import jax
import jax.numpy as jnp
from jax import lax
from jax.sharding import Mesh, PartitionSpec as P

OCAP = 24
LANES = 128
F32 = jnp.float32
BF16 = jnp.bfloat16
NT = (((1,), (1,)), ((), ()))
TN = (((0,), (0,)), ((), ()))
OWN = ("x", "y", "c")
CHIPS = ("x", "y")


def spread(block, axes, count):
    copies = jnp.broadcast_to(block[None], (count,) + block.shape)
    return lax.all_to_all(copies, axes, 0, 0, tiled=True)


def per_device(
    inputs, w_gate, w_up, w_down, a_gate, a_up, b_gate, b_up, a_down, b_down, adapter_ids, owner_map
):
    chips = lax.axis_size("x") * lax.axis_size("y")
    cores = lax.axis_size("c")
    parts = lax.axis_size("z")
    owners = chips * cores
    here_owner = lax.axis_index(OWN)
    own_rows, width = inputs.shape
    rows = adapter_ids.shape[0]
    units = w_gate.shape[0]
    rank = a_gate.shape[2]
    rank_part = b_gate.shape[1]
    slots = owner_map.shape[0]

    swap = [(0, 1), (1, 0)]
    half = spread(inputs, CHIPS, chips)
    down_other = lax.ppermute(b_down[0], "c", swap)
    half, down_other = lax.optimization_barrier((half, down_other))
    half = half.reshape(chips * own_rows, width)
    piece = jnp.concatenate([half, lax.ppermute(half, "c", swap)], axis=0)

    adapter = adapter_ids[:, 0]
    table = jnp.arange(slots, dtype=jnp.int32)
    row_slot = jnp.sum(jnp.where(adapter[:, None] == table[None, :], owner_map[None, :], 0), axis=1)
    onehot = (row_slot[:, None] == table[None, :]).astype(jnp.int32)
    position = jnp.sum((jnp.cumsum(onehot, axis=0) - onehot) * onehot, axis=1)

    def ordered(values):
        by_core = values.reshape(chips, cores, own_rows).transpose(1, 0, 2)
        by_core = by_core.reshape(cores, chips * own_rows)
        return jnp.where(lax.axis_index("c") == 0, by_core, by_core[::-1]).reshape(rows)

    row_slot, position = ordered(row_slot), ordered(position)
    up_per = LANES // (2 * rank_part)
    up_lines = OCAP // up_per
    place_of = jnp.arange(OCAP, dtype=jnp.int32)
    mine = ((row_slot == here_owner)[:, None] & (position[:, None] == place_of[None, :])).astype(BF16)
    up_line = row_slot * up_lines + position // up_per
    up_lines_all = jnp.arange(slots * up_lines, dtype=jnp.int32)
    up_pick = (up_line[:, None] == up_lines_all[None, :]).astype(BF16)
    lane = jnp.arange(LANES, dtype=jnp.int32)
    up_lane = lane[:, None] // (2 * rank_part) == (position % up_per)[None, :]
    half_rows = chips * own_rows
    here_core = lax.axis_index("c")
    row_core = jnp.where(jnp.arange(rows) < half_rows, here_core, 1 - here_core)
    apart = (row_slot % cores) ^ row_core
    down_per = LANES // rank_part
    down_lines = cores * OCAP // down_per
    seat = apart * OCAP + position
    down_line = (row_slot - row_slot % cores + row_core) * down_lines + seat // down_per
    down_lines_all = jnp.arange(owners * down_lines, dtype=jnp.int32)
    down_pick = (down_lines_all[:, None] == down_line[None, :]).astype(BF16)
    down_seat = jnp.arange(down_per, dtype=jnp.int32)[:, None] == (seat % down_per)[None, :]
    down_seat = down_seat.astype(BF16)[:, None, :]
    our_line = down_line[:half_rows, None] - here_owner * down_lines
    ours = (our_line == jnp.arange(down_lines, dtype=jnp.int32)[None, :]).astype(BF16)
    our_seat = (seat % down_per)[:half_rows, None] == (lane // rank_part)[None, :]
    our_slot = [(apart[:half_rows, None] == u).astype(BF16) for u in range(cores)]
    slot_rows = (table[:, None] == row_slot[None, :]).astype(BF16)

    selected = lax.dot_general(mine, piece, TN, preferred_element_type=F32).astype(BF16)
    shrunk = jnp.concatenate(
        [
            jnp.dot(selected, a_gate[0], preferred_element_type=F32),
            jnp.dot(selected, a_up[0], preferred_element_type=F32),
        ],
        axis=1,
    ).astype(BF16)
    column = jnp.arange(parts * LANES, dtype=jnp.int32)
    part, seat_up = column // LANES, column % LANES // (2 * rank_part)
    low = column % (2 * rank_part)
    source = part * rank_part + low % rank_part + low // rank_part * rank
    move = (jnp.arange(2 * rank, dtype=jnp.int32)[:, None] == source[None, :]).astype(BF16)
    shrunk = jnp.dot(shrunk, move, preferred_element_type=F32)
    shrunk = jnp.where(place_of[:, None] % up_per == seat_up[None, :], shrunk, 0).astype(BF16)
    line_of = jnp.arange(up_lines, dtype=jnp.int32)[:, None] == place_of[None, :] // up_per
    shrunk = jnp.dot(line_of.astype(BF16), shrunk, preferred_element_type=F32).astype(BF16)
    shrunk = shrunk.reshape(up_lines, parts, LANES).transpose(1, 0, 2)
    shrunk = lax.all_to_all(shrunk, "z", 0, 0, tiled=True)
    shrunk = jnp.sum(shrunk.astype(F32), axis=0).astype(BF16)
    low_all = spread(shrunk, OWN, owners)
    gate_base = lax.dot_general(w_gate, piece, NT, preferred_element_type=F32)
    up_base = lax.dot_general(w_up, piece, NT, preferred_element_type=F32)
    low_all, gate_base, up_base = lax.optimization_barrier((low_all, gate_base, up_base))
    low_rows = lax.dot_general(
        low_all.reshape(slots * up_lines, LANES),
        up_pick,
        (((0,), (1,)), ((), ())),
        preferred_element_type=F32,
    )
    low_rows = jnp.where(up_lane, low_rows, 0).reshape(up_per, 2 * rank_part, rows)
    low_rows = jnp.sum(low_rows, axis=0).astype(BF16)

    def expand(low, weights):
        wide = (slot_rows[:, None, :] * low[None, :, :]).reshape(slots * rank_part, rows)
        return lax.dot_general(
            weights.reshape(slots * rank_part, units), wide, TN, preferred_element_type=F32
        )

    gate_part = gate_base + expand(low_rows[:rank_part], b_gate)
    up_part = up_base + expand(low_rows[rank_part:], b_up)
    both = jnp.stack(
        [
            gate_part.astype(BF16).reshape(parts, units // parts, rows),
            up_part.astype(BF16).reshape(parts, units // parts, rows),
        ],
        axis=1,
    )
    both = lax.all_to_all(both, "z", 0, 0, tiled=True)
    both = jnp.sum(both.astype(F32), axis=0)
    hidden = (jax.nn.silu(both[0]) * both[1]).astype(BF16)
    hidden_all = spread(hidden, "z", parts).reshape(units, rows)

    rank_full = lax.dot_general(
        a_down.reshape(units, slots * rank_part), hidden_all, TN, preferred_element_type=F32
    )
    rank_rows = jnp.sum(
        rank_full.reshape(slots, rank_part, rows) * slot_rows.astype(F32)[:, None, :], axis=0
    ).astype(BF16)
    rank_wide = (down_seat * rank_rows[None, :, :]).reshape(LANES, rows)
    rank_sent = lax.dot_general(down_pick, rank_wide, NT, preferred_element_type=F32).astype(BF16)
    rank_sum = lax.all_to_all(
        rank_sent.reshape(owners, down_lines, LANES), OWN, 0, 0, tiled=True
    )
    out = lax.dot_general(hidden_all, w_down, TN, preferred_element_type=F32)
    rank_sum, out = lax.optimization_barrier((rank_sum, out))
    rank_sum = jnp.sum(rank_sum.astype(F32), axis=0).astype(BF16)
    rank_all = spread(rank_sum, "z", parts)
    kept, given = out[:half_rows], out[half_rows:].astype(BF16)
    out = kept + lax.ppermute(given, "c", swap).astype(F32)
    rank_all, out = lax.optimization_barrier((rank_all, out))
    rank_ours = lax.dot_general(
        ours, rank_all, (((1,), (1,)), ((), ())), preferred_element_type=F32
    )
    rank_ours = jnp.where(our_seat[:, None, :], rank_ours, 0).astype(BF16)
    gathered = column // LANES * rank_part + column % rank_part
    fold = (gathered[:, None] == jnp.arange(rank, dtype=jnp.int32)[None, :]).astype(BF16)
    rank_ours = jnp.dot(
        rank_ours.reshape(half_rows, parts * LANES), fold, preferred_element_type=F32
    ).astype(BF16)
    for in_slot, factor in zip(our_slot, (b_down[0], down_other)):
        out = out + jnp.dot(rank_ours * in_slot, factor, preferred_element_type=F32)
    out = out.astype(BF16)
    out = lax.all_to_all(out.reshape(chips, own_rows, width), CHIPS, 0, 0, tiled=True)
    return jnp.sum(out.astype(F32), axis=0).astype(BF16)


def solution(mesh):
    side = (4, 8, 2, 8)
    fine = Mesh(mesh.devices.reshape(side), ("x", "y", "c", "z"))
    ad, tp = ("x", "y", "c"), "z"
    placed = (
        P(ad, tp),
        P(ad, tp),
        P(ad, tp),
        P(ad, tp),
        P(ad, tp, None),
        P(ad, tp, None),
        P(None, tp, ad),
        P(None, tp, ad),
        P(ad, None, tp),
        P(ad, None, tp),
        P(),
        P(),
    )
    return jax.shard_map(
        per_device, mesh=fine, in_specs=placed, out_specs=P(ad, tp), check_vma=False
    )
```

time: 179 us -> 180 us (level)
  blocking collectives: 95.3 us -> 50.3 us
  waiting for transfers between devices: 34.9 us -> 57.6 us
  starting transfers between devices: 29.6 us -> 44.6 us
  other arithmetic: 3.42 us -> 9.03 us
  matrix products: 9.18 us -> 11.4 us
    all_to_all x3 -> x0, blocking collectives: 43.8 us -> none  [the longest x2 29.1 us: spread(): return lax.all_to_all(copies, axes, 0, 0, tiled=True)]
    all_to_all x2 -> x4, waiting for transfers between devices: 23.7 us -> 42.4 us  [spread(): return lax.all_to_all(copies, axes, 0, 0, tiled=True)]
    all_to_all x0 -> x1, waiting for transfers between devices: none -> 8.21 us  [per_device(): lax.all_to_all(rank_sent.reshape(owners, down_lines, LANES), OWN, 0, 0, t...]
    all_to_all x2 -> x4, starting transfers between devices: 15.4 us -> 22.4 us  [spread(): return lax.all_to_all(copies, axes, 0, 0, tiled=True)]
    all_to_all x0 -> x1, starting transfers between devices: none -> 6.03 us  [per_device(): lax.all_to_all(rank_sent.reshape(owners, down_lines, LANES), OWN, 0, 0, t...]
    dot_general x6 -> x9, matrix products: 5.02 us -> 7.88 us  [the longest x1 2.02 us: per_device(): up_base = lax.dot_general(w_up, piece, NT, preferred_element_type=F32)]
    unnamed x23 -> x28, local copies, waits for them, and re-layouts: 2.48 us -> 0.06 us
    ppermute x1 -> x2, starting transfers between devices: 1.92 us -> 3.93 us  [the longest x1 2.01 us: per_device(): out = kept + lax.ppermute(given, 'c', swap).astype(F32)]
  transfers between devices with their start and end apart: 5 -> 9, of which waited for: 5 -> 7; matrix products, arithmetic and copies ran while one was open for 2% -> 7% of each run, Pallas kernels for 0% -> 0%
where the time goes in v4:
time: 180 us
  waiting for transfers between devices  57.6 us (32%)
  blocking collectives  50.3 us (28%)
  starting transfers between devices  44.6 us (25%)
  matrix products  11.4 us (6%)
  other arithmetic  9.03 us (5%)
  local copies, waits for them, and re-layouts  6.14 us (3%)
    all_to_all x4, waiting for transfers between devices, spread(): return lax.all_to_all(copies, axes, 0, 0, tiled=True)  42.4 us
    all_to_all x1, blocking collectives, per_device(): both = lax.all_to_all(both, 'z', 0, 0, tiled=True)  29 us
    all_to_all x4, starting transfers between devices, spread(): return lax.all_to_all(copies, axes, 0, 0, tiled=True)  22.4 us
    all_to_all x1, blocking collectives, per_device(): lax.all_to_all(out.reshape(chips, own_rows, width), CHIPS, 0, 0, tiled=True)  21.3 us
    all_to_all x1, starting transfers between devices, per_device(): shrunk = lax.all_to_all(shrunk, 'z', 0, 0, tiled=True)  10.3 us
    all_to_all x1, waiting for transfers between devices, per_device(): lax.all_to_all(rank_sent.reshape(owners, down_lines, LANES), OWN, 0, 0, t...  8.21 us
    all_to_all x1, starting transfers between devices, per_device(): lax.all_to_all(rank_sent.reshape(owners, down_lines, LANES), OWN, 0, 0, t...  6.03 us
    all_to_all x1, waiting for transfers between devices, per_device(): shrunk = lax.all_to_all(shrunk, 'z', 0, 0, tiled=True)  5.85 us
  transfers between devices with their start and end apart: 9, of which 7 were waited for; matrix products, arithmetic and copies ran while one was open for 7% of the time, Pallas kernels for 0%

profile of v4, /device:TPU:8, one launch (start us, length us, event | category | flops | bytes accessed | tf_op | source)
XLA Modules:
  0.0 179.5 jit_solution(10328720210775468223)
XLA Ops:
  0.0 1.6 broadcast_in_dim.49
  1.7 10.3 %all-to-all-start = ((bf16[32,8,1024]{2,1,0:T(8,128)(2,1)}), bf16[32,8,1024]{2,1,0:T(8,128)(2,1)S(1)}, u32[]{:S(2)}, u32[]{:S(2)}) async-start(bf16[32,8,1024]{2,1,0:T(8,128)(2,1)} %broadcast_in_dim.49), calls=%async_computation | async-start | bytes 1048576 | tf_op jit(solution)/shard_map/all_to_all | solution.py:18
  12.0 1.9 %collective-permute-start = (bf16[64,1024]{1,0:T(8,128)(2,1)}, bf16[64,1024]{1,0:T(8,128)(2,1)S(1)}, u32[]{:S(2)}, u32[]{:S(2)}) collective-permute-start(bf16[64,1024]{1,0:T(8,128)(2,1)} %bitcast.117), channel_id=1, source_target_pairs={{0,8},{8,0},{1,9},{9,1},{2,10},{10,2},{3,11},{11,3},{4,12},{12,4},... | collective-permute-start | bytes 393224 | tf_op jit(solution)/shard_map/ppermute | solution.py:38
  13.9 0.8 select_reduce_fusion
  14.8 1.2 reduce-window.6
  16.0 0.2 slice_reduce_fusion
  17.0 12.5 %all-to-all-done = bf16[32,8,1024]{2,1,0:T(8,128)(2,1)S(1)} async-done(((bf16[32,8,1024]{2,1,0:T(8,128)(2,1)}), bf16[32,8,1024]{2,1,0:T(8,128)(2,1)S(1)}, u32[]{:S(2)}, u32[]{:S(2)}) %all-to-all-start) | async-done | bytes 524320 | tf_op jit(solution)/shard_map/all_to_all | solution.py:18
  29.6 1.9 %collective-permute-start.1 = (bf16[256,1024]{1,0:T(8,128)(2,1)S(1)}, bf16[256,1024]{1,0:T(8,128)(2,1)S(1)}, u32[]{:S(2)}, u32[]{:S(2)}) collective-permute-start(bf16[256,1024]{1,0:T(8,128)(2,1)S(1)} %bitcast.112), channel_id=1, source_target_pairs={{0,8},{8,0},{1,9},{9,1},{2,10},{10,2},{3,11},{11,3},{4,12},{12,4},... | collective-permute-start | bytes 1572872 | tf_op jit(solution)/shard_map/ppermute | solution.py:41
  31.5 0.7 fusion.53
  32.2 1.2 collective-permute-done.1
  33.4 0.5 convolution_convert_fusion.1
  34.2 1.0 fusion.11
  35.1 10.3 %all-to-all-start.1 = ((bf16[8,3,128]{2,1,0:T(4,128)(2,1)}), bf16[8,3,128]{2,1,0:T(4,128)(2,1)S(1)}, u32[]{:S(2)}, u32[]{:S(2)}) async-start(bf16[8,3,128]{2,1,0:T(4,128)(2,1)} %fusion.11), calls=%async_computation.1 | async-start | bytes 16384 | tf_op jit(solution)/shard_map/all_to_all | solution.py:100
  45.4 1.9 %convolution_bitcast_fusion.4 = f32[448,512]{1,0:T(8,128)S(1)} fusion(bf16[448,1024]{1,0:T(8,128)(2,1)} %param.13, bf16[256,1024]{1,0:T(8,128)(2,1)S(1)} %collective-permute-done.1, bf16[256,1024]{1,0:T(8,128)(2,1)S(1)} %bitcast.114), kind=kOutput, calls=%fused_computation.7 | convolution fusion | flops 471859200 | bytes 2883584 | tf_op jit(solution)/shard_map/dot_general | solution.py:103
  47.3 5.9 %all-to-all-done.1 = bf16[8,3,128]{2,1,0:T(4,128)(2,1)S(1)} async-done(((bf16[8,3,128]{2,1,0:T(4,128)(2,1)}), bf16[8,3,128]{2,1,0:T(4,128)(2,1)S(1)}, u32[]{:S(2)}, u32[]{:S(2)}) %all-to-all-start.1) | async-done | bytes 6176 | tf_op jit(solution)/shard_map/all_to_all | solution.py:100
  53.2 0.6 broadcast_in_dim.52
  53.8 5.3 %all-to-all-start.2 = ((bf16[64,3,128]{2,1,0:T(4,128)(2,1)}), bf16[64,3,128]{2,1,0:T(4,128)(2,1)S(1)}, u32[]{:S(2)}, u32[]{:S(2)}) async-start(bf16[64,3,128]{2,1,0:T(4,128)(2,1)} %broadcast_in_dim.52), calls=%async_computation.2 | async-start | bytes 131072 | tf_op jit(solution)/shard_map/all_to_all | solution.py:18
  59.1 2.0 %convolution_bitcast_fusion.3 = f32[448,512]{1,0:T(8,128)S(1)} fusion(bf16[448,1024]{1,0:T(8,128)(2,1)} %param.14, bf16[256,1024]{1,0:T(8,128)(2,1)} %copy-done.12, bf16[256,1024]{1,0:T(8,128)(2,1)S(1)} %bitcast.115), kind=kOutput, calls=%fused_computation.6 | convolution fusion | flops 471859200 | bytes 2883584 | tf_op jit(solution)/shard_map/dot_general | solution.py:104
  61.1 6.9 %all-to-all-done.2 = bf16[64,3,128]{2,1,0:T(4,128)(2,1)S(1)} async-done(((bf16[64,3,128]{2,1,0:T(4,128)(2,1)}), bf16[64,3,128]{2,1,0:T(4,128)(2,1)S(1)}, u32[]{:S(2)}, u32[]{:S(2)}) %all-to-all-start.2) | async-done | bytes 49184 | tf_op jit(solution)/shard_map/all_to_all | solution.py:18
  68.1 1.0 convolution_select_fusion
  69.1 1.0 reduce_sum.84
  70.1 1.5 fusion.4
  71.6 0.5 fusion.5
  72.2 29.0 %all_to_all.40 = bf16[8,2,56,512]{3,2,1,0:T(8,128)(2,1)S(1)} all-to-all(bf16[8,2,56,512]{3,2,1,0:T(8,128)(2,1)S(1)} %pad_maximum_fusion.1), channel_id=1, replica_groups=mesh['x'=4,'y'=8,'c'=2,'z'=8] {'z'}, dimensions={0} | all-to-all | bytes 1835008 | tf_op jit(solution)/shard_map/all_to_all | solution.py:130
  101.4 0.8 broadcast_in_dim.55
  102.2 3.5 %all-to-all-start.4 = ((bf16[8,56,512]{2,1,0:T(8,128)(2,1)}), bf16[8,56,512]{2,1,0:T(8,128)(2,1)S(1)}, u32[]{:S(2)}, u32[]{:S(2)}) async-start(bf16[8,56,512]{2,1,0:T(8,128)(2,1)} %broadcast_in_dim.55), calls=%async_computation.4 | async-start | bytes 917504 | tf_op jit(solution)/shard_map/all_to_all | solution.py:18
  105.7 16.4 %all-to-all-done.4 = bf16[8,56,512]{2,1,0:T(8,128)(2,1)S(1)} async-done(((bf16[8,56,512]{2,1,0:T(8,128)(2,1)}), bf16[8,56,512]{2,1,0:T(8,128)(2,1)S(1)}, u32[]{:S(2)}, u32[]{:S(2)}) %all-to-all-start.4) | async-done | bytes 458784 | tf_op jit(solution)/shard_map/all_to_all | solution.py:18
  122.1 0.4 fusion.6
  122.8 0.7 reshape.520
  123.4 6.0 %all-to-all-start.5 = ((bf16[64,3,128]{2,1,0:T(4,128)(2,1)}), bf16[64,3,128]{2,1,0:T(4,128)(2,1)}, u32[]{:S(2)}, u32[]{:S(2)}) async-start(bf16[64,3,128]{2,1,0:T(4,128)(2,1)} %reshape.520), calls=%async_computation.5 | async-start | bytes 131072 | tf_op jit(solution)/shard_map/all_to_all | solution.py:143
  129.5 0.7 fusion.106
  130.2 8.2 %all-to-all-done.5 = bf16[64,3,128]{2,1,0:T(4,128)(2,1)} async-done(((bf16[64,3,128]{2,1,0:T(4,128)(2,1)}), bf16[64,3,128]{2,1,0:T(4,128)(2,1)}, u32[]{:S(2)}, u32[]{:S(2)}) %all-to-all-start.5) | async-done | bytes 49184 | tf_op jit(solution)/shard_map/all_to_all | solution.py:143
  138.4 0.9 slice.66
  139.3 2.0 %collective-permute-start.2 = (bf16[256,1024]{1,0:T(8,128)(2,1)}, bf16[256,1024]{1,0:T(8,128)(2,1)S(1)}, u32[]{:S(2)}, u32[]{:S(2)}) collective-permute-start(bf16[256,1024]{1,0:T(8,128)(2,1)} %slice.66), channel_id=1, source_target_pairs={{0,8},{8,0},{1,9},{9,1},{2,10},{10,2},{3,11},{11,3},{4,12},{12,4},... | collective-permute-start | bytes 1572872 | tf_op jit(solution)/shard_map/ppermute | solution.py:151
  141.3 0.6 compare_convert_fusion
  141.9 0.7 broadcast_compare_fusion
  142.6 0.9 reduce_sum.87
  143.5 0.6 broadcast_in_dim.56
  144.1 3.3 %all-to-all-start.6 = ((bf16[8,3,128]{2,1,0:T(4,128)(2,1)}), bf16[8,3,128]{2,1,0:T(4,128)(2,1)S(1)}, u32[]{:S(2)}, u32[]{:S(2)}) async-start(bf16[8,3,128]{2,1,0:T(4,128)(2,1)} %broadcast_in_dim.56), calls=%async_computation.6 | async-start | bytes 16384 | tf_op jit(solution)/shard_map/all_to_all | solution.py:18
  147.5 1.1 convert_add_fusion
  148.6 6.6 %all-to-all-done.6 = bf16[8,3,128]{2,1,0:T(4,128)(2,1)S(1)} async-done(((bf16[8,3,128]{2,1,0:T(4,128)(2,1)}), bf16[8,3,128]{2,1,0:T(4,128)(2,1)S(1)}, u32[]{:S(2)}, u32[]{:S(2)}) %all-to-all-start.6) | async-done | bytes 6176 | tf_op jit(solution)/shard_map/all_to_all | solution.py:18
  155.2 0.3 fusion.54
  155.5 0.9 select_convert_fusion
  156.4 0.5 convolution_convert_fusion.2
  156.9 0.3 fusion.48
  157.2 0.3 fusion.7
  157.6 21.3 %all_to_all.41 = bf16[32,8,1024]{2,1,0:T(8,128)(2,1)S(1)} all-to-all(bf16[32,8,1024]{2,1,0:T(8,128)(2,1)S(1)} %fusion.7), channel_id=1, replica_groups=mesh['x'=4,'y'=8,'c'=2,'z'=8] {'x','y'}, dimensions={0} | all-to-all | bytes 1048576 | tf_op jit(solution)/shard_map/all_to_all | solution.py:165
  178.8 0.7 reduce_sum.88
  (62 shorter events, 1.8 us)
Async XLA Ops:
  0.0 129.5 %copy-start = (bf16[448,1024]{1,0:T(8,128)(2,1)S(1)}, bf16[448,1024]{1,0:T(8,128)(2,1)}, u32[]{:S(2)}) copy-start(bf16[448,1024]{1,0:T(8,128)(2,1)} %param.15) | copy-start | bytes 2752516
  1.7 32.2 %copy-start.7 = (bf16[1,1024,64]{1,2,0:T(8,128)(2,1)S(1)}, bf16[1,1024,64]{1,2,0:T(8,128)(2,1)}, u32[]{:S(2)}) copy-start(bf16[1,1024,64]{1,2,0:T(8,128)(2,1)} %param.17) | copy-start | bytes 393220
  1.7 32.3 %copy-start.8 = (bf16[1,1024,64]{1,2,0:T(8,128)(2,1)S(1)}, bf16[1,1024,64]{1,2,0:T(8,128)(2,1)}, u32[]{:S(2)}) copy-start(bf16[1,1024,64]{1,2,0:T(8,128)(2,1)} %param.16) | copy-start | bytes 393220
  1.7 27.9 %all-to-all-start = ((bf16[32,8,1024]{2,1,0:T(8,128)(2,1)}), bf16[32,8,1024]{2,1,0:T(8,128)(2,1)S(1)}, u32[]{:S(2)}, u32[]{:S(2)}) async-start(bf16[32,8,1024]{2,1,0:T(8,128)(2,1)} %broadcast_in_dim.49), calls=%async_computation | async-start | bytes 1048576 | tf_op jit(solution)/shard_map/all_to_all | solution.py:18
  12.0 5.1 %collective-permute-start = (bf16[64,1024]{1,0:T(8,128)(2,1)}, bf16[64,1024]{1,0:T(8,128)(2,1)S(1)}, u32[]{:S(2)}, u32[]{:S(2)}) collective-permute-start(bf16[64,1024]{1,0:T(8,128)(2,1)} %bitcast.117), channel_id=1, source_target_pairs={{0,8},{8,0},{1,9},{9,1},{2,10},{10,2},{3,11},{11,3},{4,12},{12,4},... | collective-permute-start | bytes 393224 | tf_op jit(solution)/shard_map/ppermute | solution.py:38
  17.0 18.1 %copy-start.4 = (bf16[64,1024]{1,0:T(8,128)(2,1)}, bf16[64,1024]{1,0:T(8,128)(2,1)S(1)}, u32[]{:S(2)}) copy-start(bf16[64,1024]{1,0:T(8,128)(2,1)S(1)} %collective-permute-done) | copy-start | bytes 393220
  29.6 3.8 %collective-permute-start.1 = (bf16[256,1024]{1,0:T(8,128)(2,1)S(1)}, bf16[256,1024]{1,0:T(8,128)(2,1)S(1)}, u32[]{:S(2)}, u32[]{:S(2)}) collective-permute-start(bf16[256,1024]{1,0:T(8,128)(2,1)S(1)} %bitcast.112), channel_id=1, source_target_pairs={{0,8},{8,0},{1,9},{9,1},{2,10},{10,2},{3,11},{11,3},{4,12},{12,4},... | collective-permute-start | bytes 1572872 | tf_op jit(solution)/shard_map/ppermute | solution.py:41
  33.4 13.9 %copy-start.12 = (bf16[256,1024]{1,0:T(8,128)(2,1)}, bf16[256,1024]{1,0:T(8,128)(2,1)S(1)}, u32[]{:S(2)}) copy-start(bf16[256,1024]{1,0:T(8,128)(2,1)S(1)} %collective-permute-done.1) | copy-start | bytes 1572868
  35.1 18.0 %all-to-all-start.1 = ((bf16[8,3,128]{2,1,0:T(4,128)(2,1)}), bf16[8,3,128]{2,1,0:T(4,128)(2,1)S(1)}, u32[]{:S(2)}, u32[]{:S(2)}) async-start(bf16[8,3,128]{2,1,0:T(4,128)(2,1)} %fusion.11), calls=%async_computation.1 | async-start | bytes 16384 | tf_op jit(solution)/shard_map/all_to_all | solution.py:100
  53.8 14.2 %all-to-all-start.2 = ((bf16[64,3,128]{2,1,0:T(4,128)(2,1)}), bf16[64,3,128]{2,1,0:T(4,128)(2,1)S(1)}, u32[]{:S(2)}, u32[]{:S(2)}) async-start(bf16[64,3,128]{2,1,0:T(4,128)(2,1)} %broadcast_in_dim.52), calls=%async_computation.2 | async-start | bytes 131072 | tf_op jit(solution)/shard_map/all_to_all | solution.py:18
  61.1 10.5 %copy-start.2 = (bf16[64,8,448]{2,1,0:T(8,128)(2,1)S(1)}, bf16[64,8,448]{2,1,0:T(8,128)(2,1)}, u32[]{:S(2)}) copy-start(bf16[64,8,448]{2,1,0:T(8,128)(2,1)} %param.18) | copy-start | bytes 1376260
  72.1 49.9 %copy-start.6 = (f32[64,512]{1,0:T(8,128)S(1)}, f32[64,512]{1,0:T(8,128)}, u32[]{:S(2)}) copy-start(f32[64,512]{1,0:T(8,128)} %get-tuple-element.32) | copy-start | bytes 393220
  72.2 49.9 %copy-start.11 = (bf16[448,64,8]{0,2,1:T(8,128)(2,1)S(1)}, bf16[448,64,8]{0,2,1:T(8,128)(2,1)}, u32[]{:S(2)}) copy-start(bf16[448,64,8]{0,2,1:T(8,128)(2,1)} %param.20) | copy-start | bytes 1376260
  102.2 19.9 %all-to-all-start.4 = ((bf16[8,56,512]{2,1,0:T(8,128)(2,1)}), bf16[8,56,512]{2,1,0:T(8,128)(2,1)S(1)}, u32[]{:S(2)}, u32[]{:S(2)}) async-start(bf16[8,56,512]{2,1,0:T(8,128)(2,1)} %broadcast_in_dim.55), calls=%async_computation.4 | async-start | bytes 917504 | tf_op jit(solution)/shard_map/all_to_all | solution.py:18
  123.4 15.0 %all-to-all-start.5 = ((bf16[64,3,128]{2,1,0:T(4,128)(2,1)}), bf16[64,3,128]{2,1,0:T(4,128)(2,1)}, u32[]{:S(2)}, u32[]{:S(2)}) async-start(bf16[64,3,128]{2,1,0:T(4,128)(2,1)} %reshape.520), calls=%async_computation.5 | async-start | bytes 131072 | tf_op jit(solution)/shard_map/all_to_all | solution.py:143
  139.3 8.2 %collective-permute-start.2 = (bf16[256,1024]{1,0:T(8,128)(2,1)}, bf16[256,1024]{1,0:T(8,128)(2,1)S(1)}, u32[]{:S(2)}, u32[]{:S(2)}) collective-permute-start(bf16[256,1024]{1,0:T(8,128)(2,1)} %slice.66), channel_id=1, source_target_pairs={{0,8},{8,0},{1,9},{9,1},{2,10},{10,2},{3,11},{11,3},{4,12},{12,4},... | collective-permute-start | bytes 1572872 | tf_op jit(solution)/shard_map/ppermute | solution.py:151
  144.1 11.0 %all-to-all-start.6 = ((bf16[8,3,128]{2,1,0:T(4,128)(2,1)}), bf16[8,3,128]{2,1,0:T(4,128)(2,1)S(1)}, u32[]{:S(2)}, u32[]{:S(2)}) async-start(bf16[8,3,128]{2,1,0:T(4,128)(2,1)} %broadcast_in_dim.56), calls=%async_computation.6 | async-start | bytes 16384 | tf_op jit(solution)/shard_map/all_to_all | solution.py:18
  148.6 8.3 %copy-start.3 = (bf16[1,64,1024]{2,1,0:T(8,128)(2,1)S(1)}, bf16[1,64,1024]{2,1,0:T(8,128)(2,1)}, u32[]{:S(2)}) copy-start(bf16[1,64,1024]{2,1,0:T(8,128)(2,1)} %param.21) | copy-start | bytes 393220
  148.6 8.3 %copy-start.10 = (bf16[256]{0:T(256)(128)(2,1)S(1)}, bf16[256]{0:T(256)(128)(2,1)}, u32[]{:S(2)}) copy-start(bf16[256]{0:T(256)(128)(2,1)} %get-tuple-element.29) | copy-start | bytes 1540
  148.6 8.6 %copy-start.1 = (f32[256,1024]{1,0:T(8,128)S(1)}, f32[256,1024]{1,0:T(8,128)}, u32[]{:S(2)}) copy-start(f32[256,1024]{1,0:T(8,128)} %convert_add_fusion) | copy-start | bytes 3145732
  148.6 8.6 %copy-start.5 = (bf16[64,1024]{1,0:T(8,128)(2,1)S(1)}, bf16[64,1024]{1,0:T(8,128)(2,1)}, u32[]{:S(2)}) copy-start(bf16[64,1024]{1,0:T(8,128)(2,1)} %copy-done.4) | copy-start | bytes 393220
  148.6 8.6 %copy-start.9 = (bf16[256]{0:T(256)(128)(2,1)S(1)}, bf16[256]{0:T(256)(128)(2,1)}, u32[]{:S(2)}) copy-start(bf16[256]{0:T(256)(128)(2,1)} %get-tuple-element.28) | copy-start | bytes 1540

commit v5 on v4

--- a/solution.py
+++ b/solution.py
@@ -102,15 +102,20 @@
     low_all = spread(shrunk, OWN, owners)
     gate_base = lax.dot_general(w_gate, piece, NT, preferred_element_type=F32)
     up_base = lax.dot_general(w_up, piece, NT, preferred_element_type=F32)
-    low_all, gate_base, up_base = lax.optimization_barrier((low_all, gate_base, up_base))
+    masks = (down_pick, down_seat, ours, our_seat, *our_slot)
+    low_all, gate_base, up_base, masks = lax.optimization_barrier(
+        (low_all, gate_base, up_base, masks)
+    )
+    down_pick, down_seat, ours, our_seat, *our_slot = masks
     low_rows = lax.dot_general(
         low_all.reshape(slots * up_lines, LANES),
         up_pick,
         (((0,), (1,)), ((), ())),
         preferred_element_type=F32,
     )
-    low_rows = jnp.where(up_lane, low_rows, 0).reshape(up_per, 2 * rank_part, rows)
-    low_rows = jnp.sum(low_rows, axis=0).astype(BF16)
+    low_rows = jnp.where(up_lane, low_rows, 0).astype(BF16)
+    gather_up = jnp.arange(2 * rank_part, dtype=jnp.int32)[:, None] == lane[None, :] % (2 * rank_part)
+    low_rows = jnp.dot(gather_up.astype(BF16), low_rows, preferred_element_type=F32).astype(BF16)
 
     def expand(low, weights):
         wide = (slot_rows[:, None, :] * low[None, :, :]).reshape(slots * rank_part, rows)
@@ -144,12 +149,11 @@
         rank_sent.reshape(owners, down_lines, LANES), OWN, 0, 0, tiled=True
     )
     out = lax.dot_general(hidden_all, w_down, TN, preferred_element_type=F32)
-    rank_sum, out = lax.optimization_barrier((rank_sum, out))
+    kept, given = out[:half_rows], out[half_rows:].astype(BF16)
+    rank_sum, kept, given = lax.optimization_barrier((rank_sum, kept, given))
     rank_sum = jnp.sum(rank_sum.astype(F32), axis=0).astype(BF16)
     rank_all = spread(rank_sum, "z", parts)
-    kept, given = out[:half_rows], out[half_rows:].astype(BF16)
     out = kept + lax.ppermute(given, "c", swap).astype(F32)
-    rank_all, out = lax.optimization_barrier((rank_all, out))
     rank_ours = lax.dot_general(
         ours, rank_all, (((1,), (1,)), ((), ())), preferred_element_type=F32
     )

time: 180 us -> 174 us (0.967)
  waiting for transfers between devices: 57.6 us -> 35.2 us
  blocking collectives: 50.3 us -> 69 us
  starting transfers between devices: 44.6 us -> 41.1 us
    all_to_all x4 -> x3, waiting for transfers between devices: 42.4 us -> 20.7 us  [spread(): return lax.all_to_all(copies, axes, 0, 0, tiled=True)]
    all_to_all x0 -> x1, blocking collectives: none -> 18.9 us  [spread(): return lax.all_to_all(copies, axes, 0, 0, tiled=True)]
    all_to_all x4 -> x3, starting transfers between devices: 22.4 us -> 18.9 us  [spread(): return lax.all_to_all(copies, axes, 0, 0, tiled=True)]
    optimization_barrier x0 -> x2, other arithmetic: none -> 2.41 us  [per_device(): lax.optimization_barrier((low_all, gate_base, up_base, masks))]
  transfers between devices with their start and end apart: 9 -> 8, of which waited for: 7 -> 6; matrix products, arithmetic and copies ran while one was open for 7% -> 9% of each run, Pallas kernels for 0% -> 0%
where the time goes in v5:
time: 174 us; the launch traced here: 173 us
  blocking collectives  69 us (40%)
  starting transfers between devices  41.1 us (24%)
  waiting for transfers between devices  35.2 us (20%)
  matrix products  11.9 us (7%)
  other arithmetic  9.56 us (5%)
  local copies, waits for them, and re-layouts  5.71 us (3%)
    all_to_all x1, blocking collectives, per_device(): both = lax.all_to_all(both, 'z', 0, 0, tiled=True)  29 us
    all_to_all x1, blocking collectives, per_device(): lax.all_to_all(out.reshape(chips, own_rows, width), CHIPS, 0, 0, tiled=True)  21 us
    all_to_all x3, waiting for transfers between devices, spread(): return lax.all_to_all(copies, axes, 0, 0, tiled=True)  20.7 us
    all_to_all x1, blocking collectives, spread(): return lax.all_to_all(copies, axes, 0, 0, tiled=True)  18.9 us
    all_to_all x3, starting transfers between devices, spread(): return lax.all_to_all(copies, axes, 0, 0, tiled=True)  18.9 us
    all_to_all x1, starting transfers between devices, per_device(): shrunk = lax.all_to_all(shrunk, 'z', 0, 0, tiled=True)  10.3 us
    all_to_all x1, waiting for transfers between devices, per_device(): lax.all_to_all(rank_sent.reshape(owners, down_lines, LANES), OWN, 0, 0, t...  8.13 us
    all_to_all x1, starting transfers between devices, per_device(): lax.all_to_all(rank_sent.reshape(owners, down_lines, LANES), OWN, 0, 0, t...  6.07 us
  transfers between devices with their start and end apart: 8, of which 6 were waited for; matrix products, arithmetic and copies ran while one was open for 9% of the time, Pallas kernels for 0%

profile of v5, /device:TPU:8, one launch (start us, length us, event | category | flops | bytes accessed | tf_op | source)
XLA Modules:
  0.0 172.9 jit_solution(6664809881458647288)
XLA Ops:
  0.0 1.6 broadcast_in_dim.47
  1.6 10.3 %all-to-all-start = ((bf16[32,8,1024]{2,1,0:T(8,128)(2,1)}), bf16[32,8,1024]{2,1,0:T(8,128)(2,1)S(1)}, u32[]{:S(2)}, u32[]{:S(2)}) async-start(bf16[32,8,1024]{2,1,0:T(8,128)(2,1)} %broadcast_in_dim.47), calls=%async_computation | async-start | bytes 1048576 | tf_op jit(solution)/shard_map/all_to_all | solution.py:18
  11.9 1.9 %collective-permute-start = (bf16[64,1024]{1,0:T(8,128)(2,1)}, bf16[64,1024]{1,0:T(8,128)(2,1)S(1)}, u32[]{:S(2)}, u32[]{:S(2)}) collective-permute-start(bf16[64,1024]{1,0:T(8,128)(2,1)} %bitcast.118), channel_id=1, source_target_pairs={{0,8},{8,0},{1,9},{9,1},{2,10},{10,2},{3,11},{11,3},{4,12},{12,4},... | collective-permute-start | bytes 393224 | tf_op jit(solution)/shard_map/ppermute | solution.py:38
  13.9 0.8 select_reduce_fusion
  14.8 1.2 reduce-window.6
  16.0 0.2 slice_reduce_fusion
  17.1 0.7 broadcast_compare_fusion
  17.8 0.6 reshape.522
  18.4 0.6 reshape.523
  19.0 10.6 %all-to-all-done = bf16[32,8,1024]{2,1,0:T(8,128)(2,1)S(1)} async-done(((bf16[32,8,1024]{2,1,0:T(8,128)(2,1)}), bf16[32,8,1024]{2,1,0:T(8,128)(2,1)S(1)}, u32[]{:S(2)}, u32[]{:S(2)}) %all-to-all-start) | async-done | bytes 524320 | tf_op jit(solution)/shard_map/all_to_all | solution.py:18
  29.6 1.9 %collective-permute-start.1 = (bf16[256,1024]{1,0:T(8,128)(2,1)S(1)}, bf16[256,1024]{1,0:T(8,128)(2,1)S(1)}, u32[]{:S(2)}, u32[]{:S(2)}) collective-permute-start(bf16[256,1024]{1,0:T(8,128)(2,1)S(1)} %bitcast.114), channel_id=1, source_target_pairs={{0,8},{8,0},{1,9},{9,1},{2,10},{10,2},{3,11},{11,3},{4,12},{12,4},... | collective-permute-start | bytes 1572872 | tf_op jit(solution)/shard_map/ppermute | solution.py:41
  31.5 0.7 fusion.19
  32.2 0.7 fusion.63
  32.9 0.5 collective-permute-done.1
  33.4 0.5 convolution_convert_fusion.1
  34.1 1.0 fusion.12
  35.1 10.3 %all-to-all-start.1 = ((bf16[8,3,128]{2,1,0:T(4,128)(2,1)}), bf16[8,3,128]{2,1,0:T(4,128)(2,1)S(1)}, u32[]{:S(2)}, u32[]{:S(2)}) async-start(bf16[8,3,128]{2,1,0:T(4,128)(2,1)} %fusion.12), calls=%async_computation.1 | async-start | bytes 16384 | tf_op jit(solution)/shard_map/all_to_all | solution.py:100
  45.4 1.9 %convolution_bitcast_fusion.4 = f32[448,512]{1,0:T(8,128)S(1)} fusion(bf16[448,1024]{1,0:T(8,128)(2,1)} %param.13, bf16[256,1024]{1,0:T(8,128)(2,1)S(1)} %collective-permute-done.1, bf16[256,1024]{1,0:T(8,128)(2,1)S(1)} %bitcast.116), kind=kOutput, calls=%fused_computation.6 | convolution fusion | flops 471859200 | bytes 2883584 | tf_op jit(solution)/shard_map/dot_general | solution.py:103
  47.3 5.9 %all-to-all-done.1 = bf16[8,3,128]{2,1,0:T(4,128)(2,1)S(1)} async-done(((bf16[8,3,128]{2,1,0:T(4,128)(2,1)}), bf16[8,3,128]{2,1,0:T(4,128)(2,1)S(1)}, u32[]{:S(2)}, u32[]{:S(2)}) %all-to-all-start.1) | async-done | bytes 6176 | tf_op jit(solution)/shard_map/all_to_all | solution.py:100
  53.2 0.6 broadcast_in_dim.49
  53.8 5.3 %all-to-all-start.2 = ((bf16[64,3,128]{2,1,0:T(4,128)(2,1)}), bf16[64,3,128]{2,1,0:T(4,128)(2,1)S(1)}, u32[]{:S(2)}, u32[]{:S(2)}) async-start(bf16[64,3,128]{2,1,0:T(4,128)(2,1)} %broadcast_in_dim.49), calls=%async_computation.2 | async-start | bytes 131072 | tf_op jit(solution)/shard_map/all_to_all | solution.py:18
  59.1 2.0 %convolution_bitcast_fusion.3 = f32[448,512]{1,0:T(8,128)S(1)} fusion(bf16[448,1024]{1,0:T(8,128)(2,1)} %param.14, bf16[256,1024]{1,0:T(8,128)(2,1)} %copy-done.13, bf16[256,1024]{1,0:T(8,128)(2,1)S(1)} %bitcast.117), kind=kOutput, calls=%fused_computation.5 | convolution fusion | flops 471859200 | bytes 2883584 | tf_op jit(solution)/shard_map/dot_general | solution.py:104
  61.1 6.9 %all-to-all-done.2 = bf16[64,3,128]{2,1,0:T(4,128)(2,1)S(1)} async-done(((bf16[64,3,128]{2,1,0:T(4,128)(2,1)}), bf16[64,3,128]{2,1,0:T(4,128)(2,1)S(1)}, u32[]{:S(2)}, u32[]{:S(2)}) %all-to-all-start.2) | async-done | bytes 49184 | tf_op jit(solution)/shard_map/all_to_all | solution.py:18
  68.1 0.4 fusion.10
  68.5 1.5 fusion.3
  70.0 0.5 fusion.4
  70.6 29.0 %all_to_all.40 = bf16[8,2,56,512]{3,2,1,0:T(8,128)(2,1)S(1)} all-to-all(bf16[8,2,56,512]{3,2,1,0:T(8,128)(2,1)S(1)} %pad_maximum_fusion.1), channel_id=1, replica_groups=mesh['x'=4,'y'=8,'c'=2,'z'=8] {'z'}, dimensions={0} | all-to-all | bytes 1835008 | tf_op jit(solution)/shard_map/all_to_all | solution.py:135
  99.8 18.9 %all_to_all.41 = bf16[8,56,512]{2,1,0:T(8,128)(2,1)S(1)} all-to-all(bf16[8,56,512]{2,1,0:T(8,128)(2,1)S(1)} %broadcast_in_dim.55), channel_id=1, replica_groups=mesh['x'=4,'y'=8,'c'=2,'z'=8] {'z'}, dimensions={0} | all-to-all | bytes 917504 | tf_op jit(solution)/shard_map/all_to_all | solution.py:18
  118.8 0.4 fusion.5
  119.2 0.2 convolution_convert_fusion
  119.4 0.7 reshape.519
  120.1 6.1 %all-to-all-start.5 = ((bf16[64,3,128]{2,1,0:T(4,128)(2,1)}), bf16[64,3,128]{2,1,0:T(4,128)(2,1)}, u32[]{:S(2)}, u32[]{:S(2)}) async-start(bf16[64,3,128]{2,1,0:T(4,128)(2,1)} %reshape.519), calls=%async_computation.5 | async-start | bytes 131072 | tf_op jit(solution)/shard_map/all_to_all | solution.py:148
  126.2 0.7 fusion.118
  127.0 8.1 %all-to-all-done.5 = bf16[64,3,128]{2,1,0:T(4,128)(2,1)} async-done(((bf16[64,3,128]{2,1,0:T(4,128)(2,1)}), bf16[64,3,128]{2,1,0:T(4,128)(2,1)}, u32[]{:S(2)}, u32[]{:S(2)}) %all-to-all-start.5) | async-done | bytes 49184 | tf_op jit(solution)/shard_map/all_to_all | solution.py:148
  135.1 0.9 reduce_sum.77
  136.1 0.6 broadcast_in_dim.57
  136.7 3.3 %all-to-all-start.6 = ((bf16[8,3,128]{2,1,0:T(4,128)(2,1)}), bf16[8,3,128]{2,1,0:T(4,128)(2,1)S(1)}, u32[]{:S(2)}, u32[]{:S(2)}) async-start(bf16[8,3,128]{2,1,0:T(4,128)(2,1)} %broadcast_in_dim.57), calls=%async_computation.6 | async-start | bytes 16384 | tf_op jit(solution)/shard_map/all_to_all | solution.py:18
  140.0 1.2 reduce.4
  141.2 1.2 reduce.5
  142.4 2.0 %collective-permute-start.2 = (bf16[256,1024]{1,0:T(8,128)(2,1)S(1)}, bf16[256,1024]{1,0:T(8,128)(2,1)}, u32[]{:S(2)}, u32[]{:S(2)}) collective-permute-start(bf16[256,1024]{1,0:T(8,128)(2,1)S(1)} %slice.66), channel_id=1, source_target_pairs={{0,8},{8,0},{1,9},{9,1},{2,10},{10,2},{3,11},{11,3},{4,12},{12,4},... | collective-permute-start | bytes 1572872 | tf_op jit(solution)/shard_map/ppermute | solution.py:156
  144.4 3.2 %all-to-all-done.6 = bf16[8,3,128]{2,1,0:T(4,128)(2,1)S(1)} async-done(((bf16[8,3,128]{2,1,0:T(4,128)(2,1)}), bf16[8,3,128]{2,1,0:T(4,128)(2,1)S(1)}, u32[]{:S(2)}, u32[]{:S(2)}) %all-to-all-start.6) | async-done | bytes 6176 | tf_op jit(solution)/shard_map/all_to_all | solution.py:18
  147.7 0.3 fusion.64
  148.1 0.9 select_convert_fusion
  149.0 0.5 convolution_convert_fusion.2
  149.5 0.3 fusion.58
  149.9 1.4 fusion.13
  151.2 21.0 %all_to_all.42 = bf16[32,8,1024]{2,1,0:T(8,128)(2,1)S(1)} all-to-all(bf16[32,8,1024]{2,1,0:T(8,128)(2,1)S(1)} %fusion.13), channel_id=1, replica_groups=mesh['x'=4,'y'=8,'c'=2,'z'=8] {'x','y'}, dimensions={0} | all-to-all | bytes 1048576 | tf_op jit(solution)/shard_map/all_to_all | solution.py:169
  172.2 0.7 reduce_sum.78
  (69 shorter events, 1.7 us)
Async XLA Ops:
  0.0 126.2 %copy-start = (bf16[448,1024]{1,0:T(8,128)(2,1)S(1)}, bf16[448,1024]{1,0:T(8,128)(2,1)}, u32[]{:S(2)}) copy-start(bf16[448,1024]{1,0:T(8,128)(2,1)} %param.15) | copy-start | bytes 2752516
  1.6 32.2 %copy-start.8 = (bf16[1,1024,64]{1,2,0:T(8,128)(2,1)S(1)}, bf16[1,1024,64]{1,2,0:T(8,128)(2,1)}, u32[]{:S(2)}) copy-start(bf16[1,1024,64]{1,2,0:T(8,128)(2,1)} %param.17) | copy-start | bytes 393220
  1.6 32.3 %copy-start.9 = (bf16[1,1024,64]{1,2,0:T(8,128)(2,1)S(1)}, bf16[1,1024,64]{1,2,0:T(8,128)(2,1)}, u32[]{:S(2)}) copy-start(bf16[1,1024,64]{1,2,0:T(8,128)(2,1)} %param.16) | copy-start | bytes 393220
  1.6 27.9 %all-to-all-start = ((bf16[32,8,1024]{2,1,0:T(8,128)(2,1)}), bf16[32,8,1024]{2,1,0:T(8,128)(2,1)S(1)}, u32[]{:S(2)}, u32[]{:S(2)}) async-start(bf16[32,8,1024]{2,1,0:T(8,128)(2,1)} %broadcast_in_dim.47), calls=%async_computation | async-start | bytes 1048576 | tf_op jit(solution)/shard_map/all_to_all | solution.py:18
  11.9 7.0 %collective-permute-start = (bf16[64,1024]{1,0:T(8,128)(2,1)}, bf16[64,1024]{1,0:T(8,128)(2,1)S(1)}, u32[]{:S(2)}, u32[]{:S(2)}) collective-permute-start(bf16[64,1024]{1,0:T(8,128)(2,1)} %bitcast.118), channel_id=1, source_target_pairs={{0,8},{8,0},{1,9},{9,1},{2,10},{10,2},{3,11},{11,3},{4,12},{12,4},... | collective-permute-start | bytes 393224 | tf_op jit(solution)/shard_map/ppermute | solution.py:38
  19.0 16.1 %copy-start.5 = (bf16[64,1024]{1,0:T(8,128)(2,1)}, bf16[64,1024]{1,0:T(8,128)(2,1)S(1)}, u32[]{:S(2)}) copy-start(bf16[64,1024]{1,0:T(8,128)(2,1)S(1)} %collective-permute-done) | copy-start | bytes 393220
  29.6 3.8 %collective-permute-start.1 = (bf16[256,1024]{1,0:T(8,128)(2,1)S(1)}, bf16[256,1024]{1,0:T(8,128)(2,1)S(1)}, u32[]{:S(2)}, u32[]{:S(2)}) collective-permute-start(bf16[256,1024]{1,0:T(8,128)(2,1)S(1)} %bitcast.114), channel_id=1, source_target_pairs={{0,8},{8,0},{1,9},{9,1},{2,10},{10,2},{3,11},{11,3},{4,12},{12,4},... | collective-permute-start | bytes 1572872 | tf_op jit(solution)/shard_map/ppermute | solution.py:41
  33.4 13.9 %copy-start.13 = (bf16[256,1024]{1,0:T(8,128)(2,1)}, bf16[256,1024]{1,0:T(8,128)(2,1)S(1)}, u32[]{:S(2)}) copy-start(bf16[256,1024]{1,0:T(8,128)(2,1)S(1)} %collective-permute-done.1) | copy-start | bytes 1572868
  35.1 18.0 %all-to-all-start.1 = ((bf16[8,3,128]{2,1,0:T(4,128)(2,1)}), bf16[8,3,128]{2,1,0:T(4,128)(2,1)S(1)}, u32[]{:S(2)}, u32[]{:S(2)}) async-start(bf16[8,3,128]{2,1,0:T(4,128)(2,1)} %fusion.12), calls=%async_computation.1 | async-start | bytes 16384 | tf_op jit(solution)/shard_map/all_to_all | solution.py:100
  53.8 14.2 %all-to-all-start.2 = ((bf16[64,3,128]{2,1,0:T(4,128)(2,1)}), bf16[64,3,128]{2,1,0:T(4,128)(2,1)S(1)}, u32[]{:S(2)}, u32[]{:S(2)}) async-start(bf16[64,3,128]{2,1,0:T(4,128)(2,1)} %broadcast_in_dim.49), calls=%async_computation.2 | async-start | bytes 131072 | tf_op jit(solution)/shard_map/all_to_all | solution.py:18
  61.1 8.9 %copy-start.2 = (bf16[64,8,448]{2,1,0:T(8,128)(2,1)S(1)}, bf16[64,8,448]{2,1,0:T(8,128)(2,1)}, u32[]{:S(2)}) copy-start(bf16[64,8,448]{2,1,0:T(8,128)(2,1)} %param.18) | copy-start | bytes 1376260
  70.6 48.2 %copy-start.7 = (f32[64,512]{1,0:T(8,128)S(1)}, f32[64,512]{1,0:T(8,128)}, u32[]{:S(2)}) copy-start(f32[64,512]{1,0:T(8,128)} %get-tuple-element.38) | copy-start | bytes 393220
  70.6 48.2 %copy-start.12 = (bf16[448,64,8]{0,2,1:T(8,128)(2,1)S(1)}, bf16[448,64,8]{0,2,1:T(8,128)(2,1)}, u32[]{:S(2)}) copy-start(bf16[448,64,8]{0,2,1:T(8,128)(2,1)} %param.20) | copy-start | bytes 1376260
  99.6 19.6 %copy-start.3 = (bf16[192,512]{1,0:T(8,128)(2,1)S(1)}, bf16[192,512]{1,0:T(8,128)(2,1)}, u32[]{:S(2)}) copy-start(bf16[192,512]{1,0:T(8,128)(2,1)} %fusion.19) | copy-start | bytes 589828
  120.1 15.0 %all-to-all-start.5 = ((bf16[64,3,128]{2,1,0:T(4,128)(2,1)}), bf16[64,3,128]{2,1,0:T(4,128)(2,1)}, u32[]{:S(2)}, u32[]{:S(2)}) async-start(bf16[64,3,128]{2,1,0:T(4,128)(2,1)} %reshape.519), calls=%async_computation.5 | async-start | bytes 131072 | tf_op jit(solution)/shard_map/all_to_all | solution.py:148
  126.9 21.1 %copy-start.1 = (f32[512,1024]{1,0:T(8,128)}, f32[512,1024]{1,0:T(8,128)S(1)}, u32[]{:S(2)}) copy-start(f32[512,1024]{1,0:T(8,128)S(1)} %fusion.118) | copy-start | bytes 6291460
  136.7 11.0 %all-to-all-start.6 = ((bf16[8,3,128]{2,1,0:T(4,128)(2,1)}), bf16[8,3,128]{2,1,0:T(4,128)(2,1)S(1)}, u32[]{:S(2)}, u32[]{:S(2)}) async-start(bf16[8,3,128]{2,1,0:T(4,128)(2,1)} %broadcast_in_dim.57), calls=%async_computation.6 | async-start | bytes 16384 | tf_op jit(solution)/shard_map/all_to_all | solution.py:18
  142.4 7.4 %collective-permute-start.2 = (bf16[256,1024]{1,0:T(8,128)(2,1)S(1)}, bf16[256,1024]{1,0:T(8,128)(2,1)}, u32[]{:S(2)}, u32[]{:S(2)}) collective-permute-start(bf16[256,1024]{1,0:T(8,128)(2,1)S(1)} %slice.66), channel_id=1, source_target_pairs={{0,8},{8,0},{1,9},{9,1},{2,10},{10,2},{3,11},{11,3},{4,12},{12,4},... | collective-permute-start | bytes 1572872 | tf_op jit(solution)/shard_map/ppermute | solution.py:156
  147.7 1.8 %copy-start.4 = (bf16[1,64,1024]{2,1,0:T(8,128)(2,1)S(1)}, bf16[1,64,1024]{2,1,0:T(8,128)(2,1)}, u32[]{:S(2)}) copy-start(bf16[1,64,1024]{2,1,0:T(8,128)(2,1)} %param.21) | copy-start | bytes 393220
  147.7 1.8 %copy-start.10 = (bf16[256]{0:T(256)(128)(2,1)S(1)}, bf16[256]{0:T(256)(128)(2,1)}, u32[]{:S(2)}) copy-start(bf16[256]{0:T(256)(128)(2,1)} %reduce.4) | copy-start | bytes 1540
  147.7 2.2 %copy-start.6 = (bf16[64,1024]{1,0:T(8,128)(2,1)S(1)}, bf16[64,1024]{1,0:T(8,128)(2,1)}, u32[]{:S(2)}) copy-start(bf16[64,1024]{1,0:T(8,128)(2,1)} %copy-done.5) | copy-start | bytes 393220
  147.7 2.2 %copy-start.11 = (bf16[256]{0:T(256)(128)(2,1)S(1)}, bf16[256]{0:T(256)(128)(2,1)}, u32[]{:S(2)}) copy-start(bf16[256]{0:T(256)(128)(2,1)} %reduce.5) | copy-start | bytes 1540
  148.0 1.8 %slice-start = ((f32[512,1024]{1,0:T(8,128)}), f32[256,1024]{1,0:T(8,128)S(1)}, s32[]{:S(2)}) async-start(f32[512,1024]{1,0:T(8,128)} %copy-done.1), calls=%async_computation.8 | async-start | bytes 2097152 | tf_op jit(solution)/shard_map/slice | solution.py:152

commit v6 on v5

--- a/solution.py
+++ b/solution.py
@@ -34,11 +34,14 @@
     slots = owner_map.shape[0]
 
     swap = [(0, 1), (1, 0)]
-    half = spread(inputs, CHIPS, chips)
-    down_other = lax.ppermute(b_down[0], "c", swap)
-    half, down_other = lax.optimization_barrier((half, down_other))
+    half = jnp.broadcast_to(inputs[None], (chips,) + inputs.shape)
+    half, a_gate, a_up, b_down = lax.optimization_barrier((half, a_gate, a_up, b_down))
+    half = lax.all_to_all(half, CHIPS, 0, 0, tiled=True)
+    factors = jnp.concatenate([a_gate[0].T, a_up[0].T, b_down[0]], axis=0)
+    other = lax.ppermute(factors, "c", swap)
+    shrink_pair = (factors[: 2 * rank], other[: 2 * rank])
+    down_pair = jnp.concatenate([factors[2 * rank :], other[2 * rank :]], axis=0)
     half = half.reshape(chips * own_rows, width)
-    piece = jnp.concatenate([half, lax.ppermute(half, "c", swap)], axis=0)
 
     adapter = adapter_ids[:, 0]
     table = jnp.arange(slots, dtype=jnp.int32)
@@ -52,23 +55,26 @@
         return jnp.where(lax.axis_index("c") == 0, by_core, by_core[::-1]).reshape(rows)
 
     row_slot, position = ordered(row_slot), ordered(position)
-    up_per = LANES // (2 * rank_part)
-    up_lines = OCAP // up_per
-    place_of = jnp.arange(OCAP, dtype=jnp.int32)
-    mine = ((row_slot == here_owner)[:, None] & (position[:, None] == place_of[None, :])).astype(BF16)
-    up_line = row_slot * up_lines + position // up_per
-    up_lines_all = jnp.arange(slots * up_lines, dtype=jnp.int32)
-    up_pick = (up_line[:, None] == up_lines_all[None, :]).astype(BF16)
-    lane = jnp.arange(LANES, dtype=jnp.int32)
-    up_lane = lane[:, None] // (2 * rank_part) == (position % up_per)[None, :]
     half_rows = chips * own_rows
     here_core = lax.axis_index("c")
     row_core = jnp.where(jnp.arange(rows) < half_rows, here_core, 1 - here_core)
+    worker = row_slot - row_slot % cores + row_core
     apart = (row_slot % cores) ^ row_core
+    seat = apart * OCAP + position
+    seats = cores * OCAP
+    seat_of = jnp.arange(seats, dtype=jnp.int32)
+    lane = jnp.arange(LANES, dtype=jnp.int32)
+    up_per = LANES // (2 * rank_part)
+    up_lines = seats // up_per
+    mine = (worker == here_owner)[:half_rows, None] & (seat[:half_rows, None] == seat_of[None, :])
+    mine = mine.astype(BF16)
+    up_line = worker * up_lines + seat // up_per
+    up_lines_all = jnp.arange(owners * up_lines, dtype=jnp.int32)
+    up_pick = (up_line[:, None] == up_lines_all[None, :]).astype(BF16)
+    up_lane = lane[:, None] // (2 * rank_part) == (seat % up_per)[None, :]
     down_per = LANES // rank_part
-    down_lines = cores * OCAP // down_per
-    seat = apart * OCAP + position
-    down_line = (row_slot - row_slot % cores + row_core) * down_lines + seat // down_per
+    down_lines = seats // down_per
+    down_line = worker * down_lines + seat // down_per
     down_lines_all = jnp.arange(owners * down_lines, dtype=jnp.int32)
     down_pick = (down_lines_all[:, None] == down_line[None, :]).astype(BF16)
     down_seat = jnp.arange(down_per, dtype=jnp.int32)[:, None] == (seat % down_per)[None, :]
@@ -76,39 +82,59 @@
     our_line = down_line[:half_rows, None] - here_owner * down_lines
     ours = (our_line == jnp.arange(down_lines, dtype=jnp.int32)[None, :]).astype(BF16)
     our_seat = (seat % down_per)[:half_rows, None] == (lane // rank_part)[None, :]
-    our_slot = [(apart[:half_rows, None] == u).astype(BF16) for u in range(cores)]
+    our_slot = jnp.arange(cores * rank, dtype=jnp.int32)[None, :] // rank == apart[:half_rows, None]
     slot_rows = (table[:, None] == row_slot[None, :]).astype(BF16)
 
-    selected = lax.dot_general(mine, piece, TN, preferred_element_type=F32).astype(BF16)
+    column = jnp.arange(parts * LANES, dtype=jnp.int32)
+    gathered = column // LANES * rank_part + column % rank_part
+    fold = gathered[:, None] == jnp.arange(cores * rank, dtype=jnp.int32)[None, :] % rank
+    masks = (
+        slot_rows,
+        slot_rows.astype(F32),
+        down_pick,
+        down_seat,
+        ours,
+        our_seat,
+        our_slot,
+        up_pick,
+        fold.astype(BF16),
+        shrink_pair,
+    )
+    half, masks = lax.optimization_barrier((half, masks))
+    slot_rows, slot_mask, down_pick, down_seat, ours, our_seat, our_slot, up_pick = masks[:8]
+    fold, shrink_pair = masks[8:]
+    selected = lax.dot_general(mine, half, TN, preferred_element_type=F32).astype(BF16)
     shrunk = jnp.concatenate(
         [
-            jnp.dot(selected, a_gate[0], preferred_element_type=F32),
-            jnp.dot(selected, a_up[0], preferred_element_type=F32),
+            lax.dot_general(
+                selected[u * OCAP : (u + 1) * OCAP],
+                shrink_pair[u],
+                NT,
+                preferred_element_type=F32,
+            )
+            for u in range(cores)
         ],
-        axis=1,
+        axis=0,
     ).astype(BF16)
-    column = jnp.arange(parts * LANES, dtype=jnp.int32)
     part, seat_up = column // LANES, column % LANES // (2 * rank_part)
     low = column % (2 * rank_part)
     source = part * rank_part + low % rank_part + low // rank_part * rank
     move = (jnp.arange(2 * rank, dtype=jnp.int32)[:, None] == source[None, :]).astype(BF16)
     shrunk = jnp.dot(shrunk, move, preferred_element_type=F32)
-    shrunk = jnp.where(place_of[:, None] % up_per == seat_up[None, :], shrunk, 0).astype(BF16)
-    line_of = jnp.arange(up_lines, dtype=jnp.int32)[:, None] == place_of[None, :] // up_per
+    shrunk = jnp.where(seat_of[:, None] % up_per == seat_up[None, :], shrunk, 0).astype(BF16)
+    line_of = jnp.arange(up_lines, dtype=jnp.int32)[:, None] == seat_of[None, :] // up_per
     shrunk = jnp.dot(line_of.astype(BF16), shrunk, preferred_element_type=F32).astype(BF16)
     shrunk = shrunk.reshape(up_lines, parts, LANES).transpose(1, 0, 2)
     shrunk = lax.all_to_all(shrunk, "z", 0, 0, tiled=True)
+    half, shrunk = lax.optimization_barrier((half, shrunk))
+    piece = jnp.concatenate([half, lax.ppermute(half, "c", swap)], axis=0)
     shrunk = jnp.sum(shrunk.astype(F32), axis=0).astype(BF16)
     low_all = spread(shrunk, OWN, owners)
     gate_base = lax.dot_general(w_gate, piece, NT, preferred_element_type=F32)
     up_base = lax.dot_general(w_up, piece, NT, preferred_element_type=F32)
-    masks = (down_pick, down_seat, ours, our_seat, *our_slot)
-    low_all, gate_base, up_base, masks = lax.optimization_barrier(
-        (low_all, gate_base, up_base, masks)
-    )
-    down_pick, down_seat, ours, our_seat, *our_slot = masks
+    low_all, gate_base, up_base = lax.optimization_barrier((low_all, gate_base, up_base))
     low_rows = lax.dot_general(
-        low_all.reshape(slots * up_lines, LANES),
+        low_all.reshape(owners * up_lines, LANES),
         up_pick,
         (((0,), (1,)), ((), ())),
         preferred_element_type=F32,
@@ -141,7 +167,7 @@
         a_down.reshape(units, slots * rank_part), hidden_all, TN, preferred_element_type=F32
     )
     rank_rows = jnp.sum(
-        rank_full.reshape(slots, rank_part, rows) * slot_rows.astype(F32)[:, None, :], axis=0
+        rank_full.reshape(slots, rank_part, rows) * slot_mask[:, None, :], axis=0
     ).astype(BF16)
     rank_wide = (down_seat * rank_rows[None, :, :]).reshape(LANES, rows)
     rank_sent = lax.dot_general(down_pick, rank_wide, NT, preferred_element_type=F32).astype(BF16)
@@ -158,13 +184,13 @@
         ours, rank_all, (((1,), (1,)), ((), ())), preferred_element_type=F32
     )
     rank_ours = jnp.where(our_seat[:, None, :], rank_ours, 0).astype(BF16)
-    gathered = column // LANES * rank_part + column % rank_part
-    fold = (gathered[:, None] == jnp.arange(rank, dtype=jnp.int32)[None, :]).astype(BF16)
     rank_ours = jnp.dot(
-        rank_ours.reshape(half_rows, parts * LANES), fold, preferred_element_type=F32
-    ).astype(BF16)
-    for in_slot, factor in zip(our_slot, (b_down[0], down_other)):
-        out = out + jnp.dot(rank_ours * in_slot, factor, preferred_element_type=F32)
+        rank_ours.reshape(half_rows, parts * LANES),
+        fold,
+        preferred_element_type=F32,
+    )
+    rank_ours = jnp.where(our_slot, rank_ours, 0).astype(BF16)
+    out = out + jnp.dot(rank_ours, down_pair, preferred_element_type=F32)
     out = out.astype(BF16)
     out = lax.all_to_all(out.reshape(chips, own_rows, width), CHIPS, 0, 0, tiled=True)
     return jnp.sum(out.astype(F32), axis=0).astype(BF16)

time: 174 us -> 172 us (0.989)
  blocking collectives: 69 us -> 86.8 us
  starting transfers between devices: 41.1 us -> 30.2 us
  waiting for transfers between devices: 35.2 us -> 27.1 us
  matrix products: 11.9 us -> 8.12 us
  local copies, waits for them, and re-layouts: 5.71 us -> 8.29 us
    all_to_all x0 -> x1, blocking collectives: none -> 17.9 us  [per_device(): shrunk = lax.all_to_all(shrunk, 'z', 0, 0, tiled=True)]
    all_to_all x3 -> x2, starting transfers between devices: 18.9 us -> 8.7 us  [spread(): return lax.all_to_all(copies, axes, 0, 0, tiled=True)]
    all_to_all x3 -> x2, waiting for transfers between devices: 20.7 us -> 11.7 us  [spread(): return lax.all_to_all(copies, axes, 0, 0, tiled=True)]
    unnamed x30 -> x34, local copies, waits for them, and re-layouts: 0.06 us -> 2.53 us
    optimization_barrier x2 -> x0, other arithmetic: 2.41 us -> none  [per_device(): lax.optimization_barrier((low_all, gate_base, up_base, masks))]
    all_to_all x1, waiting for transfers between devices: 5.85 us -> 8.14 us  [per_device(): half = lax.all_to_all(half, CHIPS, 0, 0, tiled=True)]
  transfers between devices with their start and end apart: 8 -> 7, of which waited for: 6 -> 4; matrix products, arithmetic and copies ran while one was open for 9% -> 8% of each run, Pallas kernels for 0% -> 0%
where the time goes in v6:
time: 172 us; the launch traced here: 171 us
  blocking collectives  86.8 us (50%)
  starting transfers between devices  30.2 us (18%)
  waiting for transfers between devices  27.1 us (16%)
  other arithmetic  9.73 us (6%)
  local copies, waits for them, and re-layouts  8.29 us (5%)
  matrix products  8.12 us (5%)
    all_to_all x1, blocking collectives, per_device(): both = lax.all_to_all(both, 'z', 0, 0, tiled=True)  29 us
    all_to_all x1, blocking collectives, per_device(): lax.all_to_all(out.reshape(chips, own_rows, width), CHIPS, 0, 0, tiled=True)  21 us
    all_to_all x1, blocking collectives, spread(): return lax.all_to_all(copies, axes, 0, 0, tiled=True)  18.9 us
    all_to_all x1, blocking collectives, per_device(): shrunk = lax.all_to_all(shrunk, 'z', 0, 0, tiled=True)  17.9 us
    all_to_all x2, waiting for transfers between devices, spread(): return lax.all_to_all(copies, axes, 0, 0, tiled=True)  11.7 us
    all_to_all x1, starting transfers between devices, per_device(): half = lax.all_to_all(half, CHIPS, 0, 0, tiled=True)  10.2 us
    all_to_all x2, starting transfers between devices, spread(): return lax.all_to_all(copies, axes, 0, 0, tiled=True)  8.7 us
    all_to_all x1, waiting for transfers between devices, per_device(): half = lax.all_to_all(half, CHIPS, 0, 0, tiled=True)  8.14 us
  transfers between devices with their start and end apart: 7, of which 4 were waited for; matrix products, arithmetic and copies ran while one was open for 8% of the time, Pallas kernels for 0%

profile of v6, /device:TPU:8, one launch (start us, length us, event | category | flops | bytes accessed | tf_op | source)
XLA Modules:
  0.0 170.9 jit_solution(12715647040410006079)
XLA Ops:
  0.0 1.7 broadcast_in_dim.48
  1.7 10.2 %all-to-all-start = ((bf16[32,8,1024]{2,1,0:T(8,128)(2,1)}), bf16[32,8,1024]{2,1,0:T(8,128)(2,1)S(1)}, u32[]{:S(2)}, u32[]{:S(2)}) async-start(bf16[32,8,1024]{2,1,0:T(8,128)(2,1)} %broadcast_in_dim.48), calls=%async_computation | async-start | bytes 1048576 | tf_op jit(solution)/shard_map/all_to_all | solution.py:39
  11.9 1.1 pad_maximum_fusion.1
  12.9 1.9 %collective-permute-start = (bf16[192,1024]{1,0:T(8,128)(2,1)S(1)}, bf16[192,1024]{1,0:T(8,128)(2,1)S(1)}, u32[]{:S(2)}, u32[]{:S(2)}) collective-permute-start(bf16[192,1024]{1,0:T(8,128)(2,1)S(1)} %pad_maximum_fusion.1), channel_id=1, source_target_pairs={{0,8},{8,0},{1,9},{9,1},{2,10},{10,2},{3,11},{11,3},{4,12},{12,4},... | collective-permute-start | bytes 1179656 | tf_op jit(solution)/shard_map/ppermute | solution.py:41
  15.4 1.2 reduce-window.6
  16.6 0.2 slice_reduce_fusion
  17.4 0.7 fusion.14
  18.2 0.7 broadcast_compare_fusion.1
  18.8 0.7 broadcast_compare_fusion
  19.5 0.7 fusion.54
  20.2 0.9 compare_convert_fusion
  21.3 8.1 %all-to-all-done = bf16[32,8,1024]{2,1,0:T(8,128)(2,1)S(1)} async-done(((bf16[32,8,1024]{2,1,0:T(8,128)(2,1)}), bf16[32,8,1024]{2,1,0:T(8,128)(2,1)S(1)}, u32[]{:S(2)}, u32[]{:S(2)}) %all-to-all-start) | async-done | bytes 524320 | tf_op jit(solution)/shard_map/all_to_all | solution.py:39
  29.5 0.3 convolution_convert_fusion
  30.2 0.3 fusion.6
  30.5 17.9 %all_to_all.40 = bf16[8,6,128]{2,1,0:T(8,128)(2,1)S(1)} all-to-all(bf16[8,6,128]{2,1,0:T(8,128)(2,1)S(1)} %fusion.6), channel_id=1, replica_groups=mesh['x'=4,'y'=8,'c'=2,'z'=8] {'z'}, dimensions={0} | all-to-all | bytes 24576 | tf_op jit(solution)/shard_map/all_to_all | solution.py:128
  48.4 1.9 %collective-permute-start.1 = (bf16[256,1024]{1,0:T(8,128)(2,1)S(1)}, bf16[256,1024]{1,0:T(8,128)(2,1)S(1)}, u32[]{:S(2)}, u32[]{:S(2)}) collective-permute-start(bf16[256,1024]{1,0:T(8,128)(2,1)S(1)} %bitcast.102), channel_id=1, source_target_pairs={{0,8},{8,0},{1,9},{9,1},{2,10},{10,2},{3,11},{11,3},{4,12},{12,4},... | collective-permute-start | bytes 1572872 | tf_op jit(solution)/shard_map/ppermute | solution.py:130
  50.4 0.7 broadcast_in_dim.55
  51.0 5.4 %all-to-all-start.2 = ((bf16[64,6,128]{2,1,0:T(8,128)(2,1)}), bf16[64,6,128]{2,1,0:T(8,128)(2,1)S(1)}, u32[]{:S(2)}, u32[]{:S(2)}) async-start(bf16[64,6,128]{2,1,0:T(8,128)(2,1)} %broadcast_in_dim.55), calls=%async_computation.2 | async-start | bytes 262144 | tf_op jit(solution)/shard_map/all_to_all | solution.py:18
  56.5 1.0 copy-done.11
  57.6 0.7 convolution_bitcast_fusion.3
  58.3 0.7 convolution_bitcast_fusion.4
  59.0 7.5 %all-to-all-done.2 = bf16[64,6,128]{2,1,0:T(8,128)(2,1)S(1)} async-done(((bf16[64,6,128]{2,1,0:T(8,128)(2,1)}), bf16[64,6,128]{2,1,0:T(8,128)(2,1)S(1)}, u32[]{:S(2)}, u32[]{:S(2)}) %all-to-all-start.2) | async-done | bytes 98336 | tf_op jit(solution)/shard_map/all_to_all | solution.py:18
  66.5 0.4 fusion.5
  66.9 1.6 convolution_bitcast_fusion.2
  68.4 0.2 add_convert_fusion.2
  68.7 0.5 convolution_bitcast_fusion.1
  69.2 0.2 add_convert_fusion.1
  69.5 29.0 %all_to_all.41 = bf16[8,2,56,512]{3,2,1,0:T(8,128)(2,1)S(1)} all-to-all(bf16[8,2,56,512]{3,2,1,0:T(8,128)(2,1)S(1)} %pad_maximum_fusion), channel_id=1, replica_groups=mesh['x'=4,'y'=8,'c'=2,'z'=8] {'z'}, dimensions={0} | all-to-all | bytes 1835008 | tf_op jit(solution)/shard_map/all_to_all | solution.py:161
  98.7 18.9 %all_to_all.42 = bf16[8,56,512]{2,1,0:T(8,128)(2,1)S(1)} all-to-all(bf16[8,56,512]{2,1,0:T(8,128)(2,1)S(1)} %broadcast_in_dim.58), channel_id=1, replica_groups=mesh['x'=4,'y'=8,'c'=2,'z'=8] {'z'}, dimensions={0} | all-to-all | bytes 917504 | tf_op jit(solution)/shard_map/all_to_all | solution.py:18
  117.7 0.4 multiply_reduce_fusion
  118.1 0.2 convolution_convert_fusion.1
  118.3 0.7 reshape.547
  119.0 5.5 %all-to-all-start.5 = ((bf16[64,3,128]{2,1,0:T(4,128)(2,1)}), bf16[64,3,128]{2,1,0:T(4,128)(2,1)}, u32[]{:S(2)}, u32[]{:S(2)}) async-start(bf16[64,3,128]{2,1,0:T(4,128)(2,1)} %reshape.547), calls=%async_computation.5 | async-start | bytes 131072 | tf_op jit(solution)/shard_map/all_to_all | solution.py:174
  124.5 0.7 fusion.111
  125.2 1.0 slice.97
  126.2 7.2 %all-to-all-done.5 = bf16[64,3,128]{2,1,0:T(4,128)(2,1)} async-done(((bf16[64,3,128]{2,1,0:T(4,128)(2,1)}), bf16[64,3,128]{2,1,0:T(4,128)(2,1)}, u32[]{:S(2)}, u32[]{:S(2)}) %all-to-all-start.5) | async-done | bytes 49184 | tf_op jit(solution)/shard_map/all_to_all | solution.py:174
  133.4 0.9 reduce_sum.77
  134.4 0.6 broadcast_in_dim.60
  135.0 3.3 %all-to-all-start.6 = ((bf16[8,3,128]{2,1,0:T(4,128)(2,1)}), bf16[8,3,128]{2,1,0:T(4,128)(2,1)S(1)}, u32[]{:S(2)}, u32[]{:S(2)}) async-start(bf16[8,3,128]{2,1,0:T(4,128)(2,1)} %broadcast_in_dim.60), calls=%async_computation.6 | async-start | bytes 16384 | tf_op jit(solution)/shard_map/all_to_all | solution.py:18
  138.3 2.0 %collective-permute-start.2 = (bf16[256,1024]{1,0:T(8,128)(2,1)}, bf16[256,1024]{1,0:T(8,128)(2,1)}, u32[]{:S(2)}, u32[]{:S(2)}) collective-permute-start(bf16[256,1024]{1,0:T(8,128)(2,1)} %slice.97), channel_id=1, source_target_pairs={{0,8},{8,0},{1,9},{9,1},{2,10},{10,2},{3,11},{11,3},{4,12},{12,4},... | collective-permute-start | bytes 1572872 | tf_op jit(solution)/shard_map/ppermute | solution.py:182
  140.3 1.4 copy.39
  141.7 4.3 %all-to-all-done.6 = bf16[8,3,128]{2,1,0:T(4,128)(2,1)S(1)} async-done(((bf16[8,3,128]{2,1,0:T(4,128)(2,1)}), bf16[8,3,128]{2,1,0:T(4,128)(2,1)S(1)}, u32[]{:S(2)}, u32[]{:S(2)}) %all-to-all-start.6) | async-done | bytes 6176 | tf_op jit(solution)/shard_map/all_to_all | solution.py:18
  146.0 0.3 fusion.69
  146.4 0.9 select_convert_fusion
  147.3 0.2 slice-done
  147.6 1.6 fusion.8
  149.2 21.0 %all_to_all.43 = bf16[32,8,1024]{2,1,0:T(8,128)(2,1)S(1)} all-to-all(bf16[32,8,1024]{2,1,0:T(8,128)(2,1)S(1)} %fusion.8), channel_id=1, replica_groups=mesh['x'=4,'y'=8,'c'=2,'z'=8] {'x','y'}, dimensions={0} | all-to-all | bytes 1048576 | tf_op jit(solution)/shard_map/all_to_all | solution.py:195
  170.2 0.7 reduce_sum.78
  (81 shorter events, 2.0 us)
Async XLA Ops:
  0.0 124.5 %copy-start = (bf16[448,1024]{1,0:T(8,128)(2,1)S(1)}, bf16[448,1024]{1,0:T(8,128)(2,1)}, u32[]{:S(2)}) copy-start(bf16[448,1024]{1,0:T(8,128)(2,1)} %param.15) | copy-start | bytes 2752516
  0.0 21.1 %copy-start.5 = (bf16[1,1024,64]{1,2,0:T(8,128)(2,1)S(1)}, bf16[1,1024,64]{1,2,0:T(8,128)(2,1)}, u32[]{:S(2)}) copy-start(bf16[1,1024,64]{1,2,0:T(8,128)(2,1)} %param.17) | copy-start | bytes 393220
  0.0 21.1 %copy-start.6 = (bf16[1,1024,64]{1,2,0:T(8,128)(2,1)S(1)}, bf16[1,1024,64]{1,2,0:T(8,128)(2,1)}, u32[]{:S(2)}) copy-start(bf16[1,1024,64]{1,2,0:T(8,128)(2,1)} %param.16) | copy-start | bytes 393220
  0.0 14.9 %copy-start.10 = (s32[64]{0:T(128)S(1)}, s32[64]{0:T(128)}, u32[]{:S(2)}) copy-start(s32[64]{0:T(128)} %param.23) | copy-start | bytes 772
  0.0 14.9 %copy-start.9 = (s32[512,1]{0,1:T(1,128)S(1)}, s32[512,1]{0,1:T(1,128)}, u32[]{:S(2)}) copy-start(s32[512,1]{0,1:T(1,128)} %param.22) | copy-start | bytes 6148
  1.7 27.8 %all-to-all-start = ((bf16[32,8,1024]{2,1,0:T(8,128)(2,1)}), bf16[32,8,1024]{2,1,0:T(8,128)(2,1)S(1)}, u32[]{:S(2)}, u32[]{:S(2)}) async-start(bf16[32,8,1024]{2,1,0:T(8,128)(2,1)} %broadcast_in_dim.48), calls=%async_computation | async-start | bytes 1048576 | tf_op jit(solution)/shard_map/all_to_all | solution.py:39
  12.9 8.4 %collective-permute-start = (bf16[192,1024]{1,0:T(8,128)(2,1)S(1)}, bf16[192,1024]{1,0:T(8,128)(2,1)S(1)}, u32[]{:S(2)}, u32[]{:S(2)}) collective-permute-start(bf16[192,1024]{1,0:T(8,128)(2,1)S(1)} %pad_maximum_fusion.1), channel_id=1, source_target_pairs={{0,8},{8,0},{1,9},{9,1},{2,10},{10,2},{3,11},{11,3},{4,12},{12,4},... | collective-permute-start | bytes 1179656 | tf_op jit(solution)/shard_map/ppermute | solution.py:41
  21.3 35.2 %copy-start.3 = (bf16[192,1024]{1,0:T(8,128)(2,1)}, bf16[192,1024]{1,0:T(8,128)(2,1)S(1)}, u32[]{:S(2)}) copy-start(bf16[192,1024]{1,0:T(8,128)(2,1)S(1)} %collective-permute-done) | copy-start | bytes 1179652
  48.4 8.1 %collective-permute-start.1 = (bf16[256,1024]{1,0:T(8,128)(2,1)S(1)}, bf16[256,1024]{1,0:T(8,128)(2,1)S(1)}, u32[]{:S(2)}, u32[]{:S(2)}) collective-permute-start(bf16[256,1024]{1,0:T(8,128)(2,1)S(1)} %bitcast.102), channel_id=1, source_target_pairs={{0,8},{8,0},{1,9},{9,1},{2,10},{10,2},{3,11},{11,3},{4,12},{12,4},... | collective-permute-start | bytes 1572872 | tf_op jit(solution)/shard_map/ppermute | solution.py:130
  51.0 15.4 %all-to-all-start.2 = ((bf16[64,6,128]{2,1,0:T(8,128)(2,1)}), bf16[64,6,128]{2,1,0:T(8,128)(2,1)S(1)}, u32[]{:S(2)}, u32[]{:S(2)}) async-start(bf16[64,6,128]{2,1,0:T(8,128)(2,1)} %broadcast_in_dim.55), calls=%async_computation.2 | async-start | bytes 262144 | tf_op jit(solution)/shard_map/all_to_all | solution.py:18
  56.4 1.2 copy-start.11
  56.5 1.8 %copy-start.12 = (bf16[448,1024]{1,0:T(8,128)(2,1)S(1)}, bf16[448,1024]{1,0:T(8,128)(2,1)}, u32[]{:S(2)}) copy-start(bf16[448,1024]{1,0:T(8,128)(2,1)} %param.13) | copy-start | bytes 2752516
  66.9 1.8 %copy-start.13 = (bf16[64,8,448]{2,1,0:T(8,128)(2,1)S(1)}, bf16[64,8,448]{2,1,0:T(8,128)(2,1)}, u32[]{:S(2)}) copy-start(bf16[64,8,448]{2,1,0:T(8,128)(2,1)} %param.19) | copy-start | bytes 1376260
  69.5 48.2 %copy-start.8 = (f32[64,512]{1,0:T(8,128)S(1)}, f32[64,512]{1,0:T(8,128)}, u32[]{:S(2)}) copy-start(f32[64,512]{1,0:T(8,128)} %get-tuple-element.45) | copy-start | bytes 393220
  69.5 48.2 %copy-start.14 = (bf16[448,64,8]{0,2,1:T(8,128)(2,1)S(1)}, bf16[448,64,8]{0,2,1:T(8,128)(2,1)}, u32[]{:S(2)}) copy-start(bf16[448,64,8]{0,2,1:T(8,128)(2,1)} %param.20) | copy-start | bytes 1376260
  98.5 19.6 %copy-start.7 = (bf16[192,512]{1,0:T(8,128)(2,1)S(1)}, bf16[192,512]{1,0:T(8,128)(2,1)}, u32[]{:S(2)}) copy-start(bf16[192,512]{1,0:T(8,128)(2,1)} %fusion.14) | copy-start | bytes 589828
  119.0 14.5 %all-to-all-start.5 = ((bf16[64,3,128]{2,1,0:T(4,128)(2,1)}), bf16[64,3,128]{2,1,0:T(4,128)(2,1)}, u32[]{:S(2)}, u32[]{:S(2)}) async-start(bf16[64,3,128]{2,1,0:T(4,128)(2,1)} %reshape.547), calls=%async_computation.5 | async-start | bytes 131072 | tf_op jit(solution)/shard_map/all_to_all | solution.py:174
  125.2 21.1 %copy-start.1 = (f32[512,1024]{1,0:T(8,128)}, f32[512,1024]{1,0:T(8,128)S(1)}, u32[]{:S(2)}) copy-start(f32[512,1024]{1,0:T(8,128)S(1)} %fusion.111) | copy-start | bytes 6291460
  126.2 21.1 %copy-start.2 = (bf16[1024,128]{1,0:T(8,128)(2,1)S(1)}, bf16[1024,128]{1,0:T(8,128)(2,1)}, u32[]{:S(2)}) copy-start(bf16[1024,128]{1,0:T(8,128)(2,1)} %compare_convert_fusion) | copy-start | bytes 786436
  126.2 21.1 %slice-start.1 = ((bf16[192,1024]{1,0:T(8,128)(2,1)}), bf16[64,1024]{1,0:T(8,128)(2,1)S(1)}, s32[]{:S(2)}) async-start(bf16[192,1024]{1,0:T(8,128)(2,1)} %copy-done.3), calls=%async_computation.9 | async-start | bytes 262144 | tf_op jit(solution)/shard_map/slice | solution.py:43
  126.2 21.1 %copy-start.4 = (bf16[1,64,1024]{2,1,0:T(8,128)(2,1)S(1)}, bf16[1,64,1024]{2,1,0:T(8,128)(2,1)}, u32[]{:S(2)}) copy-start(bf16[1,64,1024]{2,1,0:T(8,128)(2,1)} %param.21) | copy-start | bytes 393220
  135.0 11.0 %all-to-all-start.6 = ((bf16[8,3,128]{2,1,0:T(4,128)(2,1)}), bf16[8,3,128]{2,1,0:T(4,128)(2,1)S(1)}, u32[]{:S(2)}, u32[]{:S(2)}) async-start(bf16[8,3,128]{2,1,0:T(4,128)(2,1)} %broadcast_in_dim.60), calls=%async_computation.6 | async-start | bytes 16384 | tf_op jit(solution)/shard_map/all_to_all | solution.py:18
  138.3 9.0 %collective-permute-start.2 = (bf16[256,1024]{1,0:T(8,128)(2,1)}, bf16[256,1024]{1,0:T(8,128)(2,1)}, u32[]{:S(2)}, u32[]{:S(2)}) collective-permute-start(bf16[256,1024]{1,0:T(8,128)(2,1)} %slice.97), channel_id=1, source_target_pairs={{0,8},{8,0},{1,9},{9,1},{2,10},{10,2},{3,11},{11,3},{4,12},{12,4},... | collective-permute-start | bytes 1572872 | tf_op jit(solution)/shard_map/ppermute | solution.py:182
  146.3 1.2 slice-start

commit v7 on v6

--- a/solution.py
+++ b/solution.py
@@ -88,21 +88,24 @@
     column = jnp.arange(parts * LANES, dtype=jnp.int32)
     gathered = column // LANES * rank_part + column % rank_part
     fold = gathered[:, None] == jnp.arange(cores * rank, dtype=jnp.int32)[None, :] % rank
+    gather_up = jnp.arange(2 * rank_part, dtype=jnp.int32)[:, None] == lane[None, :] % (2 * rank_part)
     masks = (
-        slot_rows,
+        (slot_rows[:, :half_rows], slot_rows[:, half_rows:]),
         slot_rows.astype(F32),
         down_pick,
         down_seat,
         ours,
         our_seat,
         our_slot,
-        up_pick,
+        (up_pick, up_lane, gather_up.astype(BF16)),
         fold.astype(BF16),
         shrink_pair,
+        jnp.stack([b_gate.reshape(slots * rank_part, units), b_up.reshape(slots * rank_part, units)]),
     )
     half, masks = lax.optimization_barrier((half, masks))
-    slot_rows, slot_mask, down_pick, down_seat, ours, our_seat, our_slot, up_pick = masks[:8]
-    fold, shrink_pair = masks[8:]
+    slot_halves, slot_mask, down_pick, down_seat, ours, our_seat, our_slot, ups = masks[:8]
+    up_pick, up_lane, gather_up = ups
+    fold, shrink_pair, expand_pair = masks[8:]
     selected = lax.dot_general(mine, half, TN, preferred_element_type=F32).astype(BF16)
     shrunk = jnp.concatenate(
         [
@@ -126,13 +129,14 @@
     shrunk = jnp.dot(line_of.astype(BF16), shrunk, preferred_element_type=F32).astype(BF16)
     shrunk = shrunk.reshape(up_lines, parts, LANES).transpose(1, 0, 2)
     shrunk = lax.all_to_all(shrunk, "z", 0, 0, tiled=True)
+    shrunk = jnp.sum(shrunk.astype(F32), axis=0).astype(BF16)
+    shrunk = jnp.broadcast_to(shrunk[None], (owners,) + shrunk.shape)
     half, shrunk = lax.optimization_barrier((half, shrunk))
-    piece = jnp.concatenate([half, lax.ppermute(half, "c", swap)], axis=0)
-    shrunk = jnp.sum(shrunk.astype(F32), axis=0).astype(BF16)
-    low_all = spread(shrunk, OWN, owners)
-    gate_base = lax.dot_general(w_gate, piece, NT, preferred_element_type=F32)
-    up_base = lax.dot_general(w_up, piece, NT, preferred_element_type=F32)
-    low_all, gate_base, up_base = lax.optimization_barrier((low_all, gate_base, up_base))
+    low_all = lax.all_to_all(shrunk, OWN, 0, 0, tiled=True)
+    far = lax.ppermute(half, "c", swap)
+    base = [lax.dot_general(w, half, NT, preferred_element_type=F32) for w in (w_gate, w_up)]
+    low_all, base = lax.optimization_barrier((low_all, base))
+    far_base = [lax.dot_general(w, far, NT, preferred_element_type=F32) for w in (w_gate, w_up)]
     low_rows = lax.dot_general(
         low_all.reshape(owners * up_lines, LANES),
         up_pick,
@@ -140,23 +144,23 @@
         preferred_element_type=F32,
     )
     low_rows = jnp.where(up_lane, low_rows, 0).astype(BF16)
-    gather_up = jnp.arange(2 * rank_part, dtype=jnp.int32)[:, None] == lane[None, :] % (2 * rank_part)
-    low_rows = jnp.dot(gather_up.astype(BF16), low_rows, preferred_element_type=F32).astype(BF16)
-
-    def expand(low, weights):
-        wide = (slot_rows[:, None, :] * low[None, :, :]).reshape(slots * rank_part, rows)
-        return lax.dot_general(
-            weights.reshape(slots * rank_part, units), wide, TN, preferred_element_type=F32
-        )
-
-    gate_part = gate_base + expand(low_rows[:rank_part], b_gate)
-    up_part = up_base + expand(low_rows[rank_part:], b_up)
-    both = jnp.stack(
-        [
-            gate_part.astype(BF16).reshape(parts, units // parts, rows),
-            up_part.astype(BF16).reshape(parts, units // parts, rows),
-        ],
-        axis=1,
+    low_rows = jnp.dot(gather_up, low_rows, preferred_element_type=F32).astype(BF16)
+
+    def expand(low, weights, hot):
+        wide = (hot[:, None, :] * low[None, :, :]).reshape(slots * rank_part, half_rows)
+        return lax.dot_general(weights, wide, TN, preferred_element_type=F32)
+
+    def by_part(terms, cols):
+        low = low_rows[:, cols * half_rows : (cols + 1) * half_rows]
+        low = (low[:rank_part], low[rank_part:])
+        hot = slot_halves[cols]
+        sums = [terms[i] + expand(low[i], expand_pair[i], hot) for i in range(2)]
+        sums = [v.astype(BF16).reshape(parts, units // parts, half_rows) for v in sums]
+        return jnp.stack(sums, axis=1)
+
+    both = jnp.concatenate(
+        [by_part(base, 0), by_part(far_base, 1)],
+        axis=3,
     )
     both = lax.all_to_all(both, "z", 0, 0, tiled=True)
     both = jnp.sum(both.astype(F32), axis=0)

time: 172 us -> 187 us (1.087)
  matrix products: 8.12 us -> 18.3 us
  waiting for transfers between devices: 27.1 us -> 17 us
  other arithmetic: 9.73 us -> 19.6 us
  starting transfers between devices: 30.2 us -> 35.2 us
    all_to_all x0 -> x1, starting transfers between devices: none -> 10.2 us  [per_device(): low_all = lax.all_to_all(shrunk, OWN, 0, 0, tiled=True)]
    all_to_all x1, waiting for transfers between devices: 8.14 us -> 0.01 us  [per_device(): half = lax.all_to_all(half, CHIPS, 0, 0, tiled=True)]
    all_to_all x2 -> x1, waiting for transfers between devices: 11.7 us -> 4.27 us  [spread(): return lax.all_to_all(copies, axes, 0, 0, tiled=True)]
    dot_general x5 -> x9, matrix products: 3.74 us -> 10.3 us  [the longest x4 3.54 us: expand(): return lax.dot_general(weights, wide, TN, preferred_element_type=F32)]
    all_to_all x0 -> x1, waiting for transfers between devices: none -> 5.51 us  [per_device(): low_all = lax.all_to_all(shrunk, OWN, 0, 0, tiled=True)]
    all_to_all x2 -> x1, starting transfers between devices: 8.7 us -> 3.33 us  [spread(): return lax.all_to_all(copies, axes, 0, 0, tiled=True)]
    dot_general x2, matrix products: 0.36 us -> 2.51 us  [per_device(): lax.dot_general(selected[u * OCAP:(u + 1) * OCAP], shrink_pair[u], NT, pr...]
  transfers between devices with their start and end apart: 7 -> 7, of which waited for: 4 -> 3; matrix products, arithmetic and copies ran while one was open for 8% -> 17% of each run, Pallas kernels for 0% -> 0%
where the time goes in v7:
time: 187 us; the launch traced here: 186 us
  blocking collectives  86.9 us (46%)
  starting transfers between devices  35.2 us (19%)
  other arithmetic  19.6 us (10%)
  matrix products  18.3 us (10%)
  waiting for transfers between devices  17 us (9%)
  local copies, waits for them, and re-layouts  8.6 us (5%)
    all_to_all x1, blocking collectives, per_device(): both = lax.all_to_all(both, 'z', 0, 0, tiled=True)  28.9 us
    all_to_all x1, blocking collectives, per_device(): lax.all_to_all(out.reshape(chips, own_rows, width), CHIPS, 0, 0, tiled=True)  21 us
    all_to_all x1, blocking collectives, spread(): return lax.all_to_all(copies, axes, 0, 0, tiled=True)  19.1 us
    all_to_all x1, blocking collectives, per_device(): shrunk = lax.all_to_all(shrunk, 'z', 0, 0, tiled=True)  17.9 us
    all_to_all x1, starting transfers between devices, per_device(): low_all = lax.all_to_all(shrunk, OWN, 0, 0, tiled=True)  10.2 us
    all_to_all x1, starting transfers between devices, per_device(): half = lax.all_to_all(half, CHIPS, 0, 0, tiled=True)  10.2 us
    all_to_all x1, waiting for transfers between devices, per_device(): lax.all_to_all(rank_sent.reshape(owners, down_lines, LANES), OWN, 0, 0, t...  7.23 us
    all_to_all x1, waiting for transfers between devices, per_device(): low_all = lax.all_to_all(shrunk, OWN, 0, 0, tiled=True)  5.51 us
  transfers between devices with their start and end apart: 7, of which 3 were waited for; matrix products, arithmetic and copies ran while one was open for 17% of the time, Pallas kernels for 0%

profile of v7, /device:TPU:8, one launch (start us, length us, event | category | flops | bytes accessed | tf_op | source)
XLA Modules:
  0.0 186.0 jit_solution(5531885867962479783)
XLA Ops:
  0.0 1.7 broadcast_in_dim.47
  1.7 10.2 %all-to-all-start = ((bf16[32,8,1024]{2,1,0:T(8,128)(2,1)}), bf16[32,8,1024]{2,1,0:T(8,128)(2,1)S(1)}, u32[]{:S(2)}, u32[]{:S(2)}) async-start(bf16[32,8,1024]{2,1,0:T(8,128)(2,1)} %broadcast_in_dim.47), calls=%async_computation | async-start | bytes 1048576 | tf_op jit(solution)/shard_map/all_to_all | solution.py:39
  11.9 1.9 %pad_maximum_fusion.1 = bf16[192,1024]{1,0:T(8,128)(2,1)} fusion(bf16[64,1024]{1,0:T(8,128)(2,1)} %bitcast.150, bf16[64,1024]{1,0:T(8,128)(2,1)} %bitcast.154, bf16[64,1024]{1,0:T(8,128)(2,1)} %bitcast.156), kind=kLoop, calls=%fused_computation.46 | loop fusion | flops 1179648 | bytes 786432 | tf_op jit(solution)/shard_map/concatenate | solution.py:40
  13.8 1.9 %collective-permute-start = (bf16[192,1024]{1,0:T(8,128)(2,1)}, bf16[192,1024]{1,0:T(8,128)(2,1)S(1)}, u32[]{:S(2)}, u32[]{:S(2)}) collective-permute-start(bf16[192,1024]{1,0:T(8,128)(2,1)} %pad_maximum_fusion.1), channel_id=1, source_target_pairs={{0,8},{8,0},{1,9},{9,1},{2,10},{10,2},{3,11},{11,3},{4,12},{12,4},... | collective-permute-start | bytes 1179656 | tf_op jit(solution)/shard_map/ppermute | solution.py:41
  18.4 1.2 reduce-window.6
  21.6 0.7 fusion.72
  22.3 0.9 pad_maximum_fusion.2
  23.3 0.6 fusion.126
  23.9 1.4 broadcast_compare_fusion.2
  25.2 1.3 broadcast_compare_fusion.1
  26.6 1.4 broadcast_compare_fusion
  27.9 0.7 fusion.23
  28.7 0.9 compare_convert_fusion
  30.1 1.1 pad_maximum_fusion
  31.2 0.9 fusion.10
  32.1 0.8 slice.106
  33.0 1.1 convolution_convert_fusion
  34.1 1.7 convolution_convert_fusion.3
  35.8 0.8 convolution_convert_fusion.4
  36.6 1.0 fusion.9
  37.7 17.9 %all_to_all.40 = bf16[8,6,128]{2,1,0:T(8,128)(2,1)S(1)} all-to-all(bf16[8,6,128]{2,1,0:T(8,128)(2,1)S(1)} %fusion.9), channel_id=1, replica_groups=mesh['x'=4,'y'=8,'c'=2,'z'=8] {'z'}, dimensions={0} | all-to-all | bytes 24576 | tf_op jit(solution)/shard_map/all_to_all | solution.py:131
  55.6 0.7 broadcast_in_dim.54
  56.2 10.2 %all-to-all-start.2 = ((bf16[64,6,128]{2,1,0:T(8,128)(2,1)}), bf16[64,6,128]{2,1,0:T(8,128)(2,1)S(1)}, u32[]{:S(2)}, u32[]{:S(2)}) async-start(bf16[64,6,128]{2,1,0:T(8,128)(2,1)} %broadcast_in_dim.54), calls=%async_computation.2 | async-start | bytes 262144 | tf_op jit(solution)/shard_map/all_to_all | solution.py:135
  66.4 2.1 %collective-permute-start.1 = (bf16[256,1024]{1,0:T(8,128)(2,1)S(1)}, bf16[256,1024]{1,0:T(8,128)(2,1)}, u32[]{:S(2)}, u32[]{:S(2)}) collective-permute-start(bf16[256,1024]{1,0:T(8,128)(2,1)S(1)} %bitcast.141), channel_id=1, source_target_pairs={{0,8},{8,0},{1,9},{9,1},{2,10},{10,2},{3,11},{11,3},{4,12},{12,4},... | collective-permute-start | bytes 1572872 | tf_op jit(solution)/shard_map/ppermute | solution.py:136
  68.5 1.2 convolution_bitcast_fusion.3
  69.7 1.2 convolution_bitcast_fusion.4
  70.9 5.5 %all-to-all-done.2 = bf16[64,6,128]{2,1,0:T(8,128)(2,1)S(1)} async-done(((bf16[64,6,128]{2,1,0:T(8,128)(2,1)}), bf16[64,6,128]{2,1,0:T(8,128)(2,1)S(1)}, u32[]{:S(2)}, u32[]{:S(2)}) %all-to-all-start.2) | async-done | bytes 98336 | tf_op jit(solution)/shard_map/all_to_all | solution.py:135
  76.5 1.4 convolution_convert_fusion.2
  77.9 1.5 fusion.13
  79.4 1.4 fusion.16
  81.5 1.5 fusion.3
  83.0 1.5 fusion.2
  84.6 28.9 %all_to_all.41 = bf16[8,2,56,512]{3,2,1,0:T(8,128)(2,1)S(1)} all-to-all(bf16[8,2,56,512]{3,2,1,0:T(8,128)(2,1)S(1)} %maximum_maximum_fusion), channel_id=1, replica_groups=mesh['x'=4,'y'=8,'c'=2,'z'=8] {'z'}, dimensions={0} | all-to-all | bytes 1835008 | tf_op jit(solution)/shard_map/all_to_all | solution.py:165
  113.7 19.1 %all_to_all.42 = bf16[8,56,512]{2,1,0:T(8,128)(2,1)S(1)} all-to-all(bf16[8,56,512]{2,1,0:T(8,128)(2,1)S(1)} %broadcast_in_dim.58), channel_id=1, replica_groups=mesh['x'=4,'y'=8,'c'=2,'z'=8] {'z'}, dimensions={0} | all-to-all | bytes 917504 | tf_op jit(solution)/shard_map/all_to_all | solution.py:18
  133.5 0.7 reshape.598
  134.1 5.5 %all-to-all-start.5 = ((bf16[64,3,128]{2,1,0:T(4,128)(2,1)}), bf16[64,3,128]{2,1,0:T(4,128)(2,1)}, u32[]{:S(2)}, u32[]{:S(2)}) async-start(bf16[64,3,128]{2,1,0:T(4,128)(2,1)} %reshape.598), calls=%async_computation.5 | async-start | bytes 131072 | tf_op jit(solution)/shard_map/all_to_all | solution.py:178
  139.6 0.7 fusion.132
  140.4 1.0 slice.149
  141.3 7.2 %all-to-all-done.5 = bf16[64,3,128]{2,1,0:T(4,128)(2,1)} async-done(((bf16[64,3,128]{2,1,0:T(4,128)(2,1)}), bf16[64,3,128]{2,1,0:T(4,128)(2,1)}, u32[]{:S(2)}, u32[]{:S(2)}) %all-to-all-start.5) | async-done | bytes 49184 | tf_op jit(solution)/shard_map/all_to_all | solution.py:178
  148.6 0.9 reduce_sum.77
  150.1 3.3 %all-to-all-start.6 = ((bf16[8,3,128]{2,1,0:T(4,128)(2,1)}), bf16[8,3,128]{2,1,0:T(4,128)(2,1)S(1)}, u32[]{:S(2)}, u32[]{:S(2)}) async-start(bf16[8,3,128]{2,1,0:T(4,128)(2,1)} %broadcast_in_dim.60), calls=%async_computation.6 | async-start | bytes 16384 | tf_op jit(solution)/shard_map/all_to_all | solution.py:18
  153.4 2.0 %collective-permute-start.2 = (bf16[256,1024]{1,0:T(8,128)(2,1)}, bf16[256,1024]{1,0:T(8,128)(2,1)}, u32[]{:S(2)}, u32[]{:S(2)}) collective-permute-start(bf16[256,1024]{1,0:T(8,128)(2,1)} %slice.149), channel_id=1, source_target_pairs={{0,8},{8,0},{1,9},{9,1},{2,10},{10,2},{3,11},{11,3},{4,12},{12,4},... | collective-permute-start | bytes 1572872 | tf_op jit(solution)/shard_map/ppermute | solution.py:186
  155.5 1.4 copy.32
  156.8 4.3 %all-to-all-done.6 = bf16[8,3,128]{2,1,0:T(4,128)(2,1)S(1)} async-done(((bf16[8,3,128]{2,1,0:T(4,128)(2,1)}), bf16[8,3,128]{2,1,0:T(4,128)(2,1)S(1)}, u32[]{:S(2)}, u32[]{:S(2)}) %all-to-all-start.6) | async-done | bytes 6176 | tf_op jit(solution)/shard_map/all_to_all | solution.py:18
  161.5 0.9 select_convert_fusion
  162.7 1.6 fusion.11
  164.3 21.0 %all_to_all.43 = bf16[32,8,1024]{2,1,0:T(8,128)(2,1)S(1)} all-to-all(bf16[32,8,1024]{2,1,0:T(8,128)(2,1)S(1)} %fusion.11), channel_id=1, replica_groups=mesh['x'=4,'y'=8,'c'=2,'z'=8] {'x','y'}, dimensions={0} | all-to-all | bytes 1048576 | tf_op jit(solution)/shard_map/all_to_all | solution.py:199
  185.4 0.7 reduce_sum.78
  (98 shorter events, 8.3 us)
Async XLA Ops:
  0.0 139.6 %copy-start = (bf16[448,1024]{1,0:T(8,128)(2,1)S(1)}, bf16[448,1024]{1,0:T(8,128)(2,1)}, u32[]{:S(2)}) copy-start(bf16[448,1024]{1,0:T(8,128)(2,1)} %param.15) | copy-start | bytes 2752516
  0.0 22.3 %copy-start.10 = (bf16[1,1024,64]{1,2,0:T(8,128)(2,1)S(1)}, bf16[1,1024,64]{1,2,0:T(8,128)(2,1)}, u32[]{:S(2)}) copy-start(bf16[1,1024,64]{1,2,0:T(8,128)(2,1)} %param.17) | copy-start | bytes 393220
  0.0 18.0 %copy-start.19 = (s32[64]{0:T(128)S(1)}, s32[64]{0:T(128)}, u32[]{:S(2)}) copy-start(s32[64]{0:T(128)} %param.23) | copy-start | bytes 772
  0.0 18.0 %copy-start.18 = (s32[512,1]{0,1:T(1,128)S(1)}, s32[512,1]{0,1:T(1,128)}, u32[]{:S(2)}) copy-start(s32[512,1]{0,1:T(1,128)} %param.22) | copy-start | bytes 6148
  1.7 31.2 %all-to-all-start = ((bf16[32,8,1024]{2,1,0:T(8,128)(2,1)}), bf16[32,8,1024]{2,1,0:T(8,128)(2,1)S(1)}, u32[]{:S(2)}, u32[]{:S(2)}) async-start(bf16[32,8,1024]{2,1,0:T(8,128)(2,1)} %broadcast_in_dim.47), calls=%async_computation | async-start | bytes 1048576 | tf_op jit(solution)/shard_map/all_to_all | solution.py:39
  11.9 18.3 %copy-start.8 = (bf16[64,8,448]{2,1,0:T(8,128)(2,1)S(1)}, bf16[64,8,448]{2,1,0:T(8,128)(2,1)}, u32[]{:S(2)}) copy-start(bf16[64,8,448]{2,1,0:T(8,128)(2,1)} %param.19) | copy-start | bytes 1376260
  11.9 18.3 %copy-start.9 = (bf16[64,8,448]{2,1,0:T(8,128)(2,1)S(1)}, bf16[64,8,448]{2,1,0:T(8,128)(2,1)}, u32[]{:S(2)}) copy-start(bf16[64,8,448]{2,1,0:T(8,128)(2,1)} %param.18) | copy-start | bytes 1376260
  13.8 18.4 %collective-permute-start = (bf16[192,1024]{1,0:T(8,128)(2,1)}, bf16[192,1024]{1,0:T(8,128)(2,1)S(1)}, u32[]{:S(2)}, u32[]{:S(2)}) collective-permute-start(bf16[192,1024]{1,0:T(8,128)(2,1)} %pad_maximum_fusion.1), channel_id=1, source_target_pairs={{0,8},{8,0},{1,9},{9,1},{2,10},{10,2},{3,11},{11,3},{4,12},{12,4},... | collective-permute-start | bytes 1179656 | tf_op jit(solution)/shard_map/ppermute | solution.py:41
  31.2 37.2 %copy-start.2 = (bf16[448,1024]{1,0:T(8,128)(2,1)S(1)}, bf16[448,1024]{1,0:T(8,128)(2,1)}, u32[]{:S(2)}) copy-start(bf16[448,1024]{1,0:T(8,128)(2,1)} %param.14) | copy-start | bytes 2752516
  32.1 0.8 copy-start.6
  33.0 36.7 %copy-start.3 = (bf16[448,1024]{1,0:T(8,128)(2,1)S(1)}, bf16[448,1024]{1,0:T(8,128)(2,1)}, u32[]{:S(2)}) copy-start(bf16[448,1024]{1,0:T(8,128)(2,1)} %param.13) | copy-start | bytes 2752516
  56.2 20.2 %all-to-all-start.2 = ((bf16[64,6,128]{2,1,0:T(8,128)(2,1)}), bf16[64,6,128]{2,1,0:T(8,128)(2,1)S(1)}, u32[]{:S(2)}, u32[]{:S(2)}) async-start(bf16[64,6,128]{2,1,0:T(8,128)(2,1)} %broadcast_in_dim.54), calls=%async_computation.2 | async-start | bytes 262144 | tf_op jit(solution)/shard_map/all_to_all | solution.py:135
  66.4 15.1 %collective-permute-start.1 = (bf16[256,1024]{1,0:T(8,128)(2,1)S(1)}, bf16[256,1024]{1,0:T(8,128)(2,1)}, u32[]{:S(2)}, u32[]{:S(2)}) collective-permute-start(bf16[256,1024]{1,0:T(8,128)(2,1)S(1)} %bitcast.141), channel_id=1, source_target_pairs={{0,8},{8,0},{1,9},{9,1},{2,10},{10,2},{3,11},{11,3},{4,12},{12,4},... | collective-permute-start | bytes 1572872 | tf_op jit(solution)/shard_map/ppermute | solution.py:136
  70.9 9.9 %copy-start.15 = (bf16[64,256]{1,0:T(8,128)(2,1)S(1)}, bf16[64,256]{1,0:T(8,128)(2,1)}, u32[]{:S(2)}) copy-start(bf16[64,256]{1,0:T(8,128)(2,1)} %get-tuple-element.46) | copy-start | bytes 98308
  76.5 2.9 %copy-start.16 = (bf16[64,256]{1,0:T(8,128)(2,1)S(1)}, bf16[64,256]{1,0:T(8,128)(2,1)}, u32[]{:S(2)}) copy-start(bf16[64,256]{1,0:T(8,128)(2,1)} %get-tuple-element.52) | copy-start | bytes 98308
  77.9 2.9 %copy-start.5 = (bf16[2,512,448]{2,1,0:T(8,128)(2,1)S(1)}, bf16[2,512,448]{2,1,0:T(8,128)(2,1)}, u32[]{:S(2)}) copy-start(bf16[2,512,448]{2,1,0:T(8,128)(2,1)} %pad_maximum_fusion) | copy-start | bytes 2752516
  77.9 2.9 %copy-start.12 = (f32[448,256]{1,0:T(8,128)S(1)}, f32[448,256]{1,0:T(8,128)}, u32[]{:S(2)}) copy-start(f32[448,256]{1,0:T(8,128)} %convolution_bitcast_fusion.3) | copy-start | bytes 1376260
  77.9 3.3 %copy-start.11 = (f32[448,256]{1,0:T(8,128)S(1)}, f32[448,256]{1,0:T(8,128)}, u32[]{:S(2)}) copy-start(f32[448,256]{1,0:T(8,128)} %convolution_bitcast_fusion.4) | copy-start | bytes 1376260
  113.5 19.3 %copy-start.14 = (f32[64,512]{1,0:T(8,128)S(1)}, f32[64,512]{1,0:T(8,128)}, u32[]{:S(2)}) copy-start(f32[64,512]{1,0:T(8,128)} %get-tuple-element.53) | copy-start | bytes 393220
  113.5 19.3 %copy-start.20 = (bf16[448,64,8]{0,2,1:T(8,128)(2,1)S(1)}, bf16[448,64,8]{0,2,1:T(8,128)(2,1)}, u32[]{:S(2)}) copy-start(bf16[448,64,8]{0,2,1:T(8,128)(2,1)} %param.20) | copy-start | bytes 1376260
  113.6 19.6 %copy-start.13 = (bf16[192,512]{1,0:T(8,128)(2,1)S(1)}, bf16[192,512]{1,0:T(8,128)(2,1)}, u32[]{:S(2)}) copy-start(bf16[192,512]{1,0:T(8,128)(2,1)} %fusion.23) | copy-start | bytes 589828
  113.6 19.6 %copy-start.17 = (bf16[16,1,512]{2,0,1:T(8,128)(2,1)S(1)}, bf16[16,1,512]{2,0,1:T(8,128)(2,1)}, u32[]{:S(2)}) copy-start(bf16[16,1,512]{2,0,1:T(8,128)(2,1)} %fusion.71) | copy-start | bytes 49156
  134.1 14.4 %all-to-all-start.5 = ((bf16[64,3,128]{2,1,0:T(4,128)(2,1)}), bf16[64,3,128]{2,1,0:T(4,128)(2,1)}, u32[]{:S(2)}, u32[]{:S(2)}) async-start(bf16[64,3,128]{2,1,0:T(4,128)(2,1)} %reshape.598), calls=%async_computation.5 | async-start | bytes 131072 | tf_op jit(solution)/shard_map/all_to_all | solution.py:178
  140.4 21.1 %copy-start.1 = (f32[512,1024]{1,0:T(8,128)}, f32[512,1024]{1,0:T(8,128)S(1)}, u32[]{:S(2)}) copy-start(f32[512,1024]{1,0:T(8,128)S(1)} %fusion.132) | copy-start | bytes 6291460
  141.3 21.1 %copy-start.4 = (bf16[1024,128]{1,0:T(8,128)(2,1)S(1)}, bf16[1024,128]{1,0:T(8,128)(2,1)}, u32[]{:S(2)}) copy-start(bf16[1024,128]{1,0:T(8,128)(2,1)} %compare_convert_fusion) | copy-start | bytes 786436
  141.3 21.1 %slice-start.1 = ((bf16[192,1024]{1,0:T(8,128)(2,1)}), bf16[64,1024]{1,0:T(8,128)(2,1)S(1)}, s32[]{:S(2)}) async-start(bf16[192,1024]{1,0:T(8,128)(2,1)} %copy-done.6), calls=%async_computation.9 | async-start | bytes 262144 | tf_op jit(solution)/shard_map/slice | solution.py:43
  141.3 21.1 %copy-start.7 = (bf16[1,64,1024]{2,1,0:T(8,128)(2,1)S(1)}, bf16[1,64,1024]{2,1,0:T(8,128)(2,1)}, u32[]{:S(2)}) copy-start(bf16[1,64,1024]{2,1,0:T(8,128)(2,1)} %param.21) | copy-start | bytes 393220
  150.1 11.0 %all-to-all-start.6 = ((bf16[8,3,128]{2,1,0:T(4,128)(2,1)}), bf16[8,3,128]{2,1,0:T(4,128)(2,1)S(1)}, u32[]{:S(2)}, u32[]{:S(2)}) async-start(bf16[8,3,128]{2,1,0:T(4,128)(2,1)} %broadcast_in_dim.60), calls=%async_computation.6 | async-start | bytes 16384 | tf_op jit(solution)/shard_map/all_to_all | solution.py:18
  153.4 9.0 %collective-permute-start.2 = (bf16[256,1024]{1,0:T(8,128)(2,1)}, bf16[256,1024]{1,0:T(8,128)(2,1)}, u32[]{:S(2)}, u32[]{:S(2)}) collective-permute-start(bf16[256,1024]{1,0:T(8,128)(2,1)} %slice.149), channel_id=1, source_target_pairs={{0,8},{8,0},{1,9},{9,1},{2,10},{10,2},{3,11},{11,3},{4,12},{12,4},... | collective-permute-start | bytes 1572872 | tf_op jit(solution)/shard_map/ppermute | solution.py:186
  161.5 1.2 slice-start

commit v8 on v6

--- a/solution.py
+++ b/solution.py
@@ -88,21 +88,23 @@
     column = jnp.arange(parts * LANES, dtype=jnp.int32)
     gathered = column // LANES * rank_part + column % rank_part
     fold = gathered[:, None] == jnp.arange(cores * rank, dtype=jnp.int32)[None, :] % rank
+    one = lax.optimization_barrier(jnp.ones((), BF16))
     masks = (
         slot_rows,
         slot_rows.astype(F32),
         down_pick,
         down_seat,
         ours,
-        our_seat,
-        our_slot,
+        our_seat.astype(BF16),
+        our_slot.astype(BF16),
         up_pick,
         fold.astype(BF16),
         shrink_pair,
+        b_gate * one,
     )
     half, masks = lax.optimization_barrier((half, masks))
     slot_rows, slot_mask, down_pick, down_seat, ours, our_seat, our_slot, up_pick = masks[:8]
-    fold, shrink_pair = masks[8:]
+    fold, shrink_pair, b_gate = masks[8:]
     selected = lax.dot_general(mine, half, TN, preferred_element_type=F32).astype(BF16)
     shrunk = jnp.concatenate(
         [
@@ -183,13 +185,13 @@
     rank_ours = lax.dot_general(
         ours, rank_all, (((1,), (1,)), ((), ())), preferred_element_type=F32
     )
-    rank_ours = jnp.where(our_seat[:, None, :], rank_ours, 0).astype(BF16)
+    rank_ours = rank_ours.astype(BF16) * our_seat[:, None, :]
     rank_ours = jnp.dot(
         rank_ours.reshape(half_rows, parts * LANES),
         fold,
         preferred_element_type=F32,
     )
-    rank_ours = jnp.where(our_slot, rank_ours, 0).astype(BF16)
+    rank_ours = rank_ours.astype(BF16) * our_slot
     out = out + jnp.dot(rank_ours, down_pair, preferred_element_type=F32)
     out = out.astype(BF16)
     out = lax.all_to_all(out.reshape(chips, own_rows, width), CHIPS, 0, 0, tiled=True)

time: 172 us -> 173 us (level)
  no operation moved by 1% of the time
where the time goes in v8:
time: 173 us; the launch traced here: 172 us
  blocking collectives  86.9 us (50%)
  starting transfers between devices  30.3 us (18%)
  waiting for transfers between devices  26.9 us (16%)
  other arithmetic  11.4 us (7%)
  matrix products  8.94 us (5%)
  local copies, waits for them, and re-layouts  6.88 us (4%)
    all_to_all x1, blocking collectives, per_device(): both = lax.all_to_all(both, 'z', 0, 0, tiled=True)  29 us
    all_to_all x1, blocking collectives, per_device(): lax.all_to_all(out.reshape(chips, own_rows, width), CHIPS, 0, 0, tiled=True)  21 us
    all_to_all x1, blocking collectives, spread(): return lax.all_to_all(copies, axes, 0, 0, tiled=True)  18.9 us
    all_to_all x1, blocking collectives, per_device(): shrunk = lax.all_to_all(shrunk, 'z', 0, 0, tiled=True)  17.9 us
    all_to_all x2, waiting for transfers between devices, spread(): return lax.all_to_all(copies, axes, 0, 0, tiled=True)  13.1 us
    all_to_all x1, starting transfers between devices, per_device(): half = lax.all_to_all(half, CHIPS, 0, 0, tiled=True)  10.3 us
    all_to_all x2, starting transfers between devices, spread(): return lax.all_to_all(copies, axes, 0, 0, tiled=True)  8.7 us
    all_to_all x1, waiting for transfers between devices, per_device(): lax.all_to_all(rank_sent.reshape(owners, down_lines, LANES), OWN, 0, 0, t...  7.2 us
  transfers between devices with their start and end apart: 7, of which 4 were waited for; matrix products, arithmetic and copies ran while one was open for 8% of the time, Pallas kernels for 0%

profile of v8, /device:TPU:8, one launch (start us, length us, event | category | flops | bytes accessed | tf_op | source)
XLA Modules:
  0.0 171.8 jit_solution(7377653052282771910)
XLA Ops:
  0.0 1.6 broadcast_in_dim.36
  1.7 10.3 %all-to-all-start = ((bf16[32,8,1024]{2,1,0:T(8,128)(2,1)}), bf16[32,8,1024]{2,1,0:T(8,128)(2,1)S(1)}, u32[]{:S(2)}, u32[]{:S(2)}) async-start(bf16[32,8,1024]{2,1,0:T(8,128)(2,1)} %broadcast_in_dim.36), calls=%async_computation | async-start | bytes 1048576 | tf_op jit(solution)/shard_map/all_to_all | solution.py:39
  12.0 1.8 %pad_maximum_fusion.1 = bf16[192,1024]{1,0:T(8,128)(2,1)} fusion(bf16[64,1024]{1,0:T(8,128)(2,1)} %bitcast.108, bf16[64,1024]{1,0:T(8,128)(2,1)} %bitcast.110, bf16[64,1024]{1,0:T(8,128)(2,1)} %bitcast.112), kind=kLoop, calls=%fused_computation.39 | loop fusion | flops 1179648 | bytes 786432 | tf_op jit(solution)/shard_map/concatenate | solution.py:40
  13.8 1.9 %collective-permute-start = (bf16[192,1024]{1,0:T(8,128)(2,1)}, bf16[192,1024]{1,0:T(8,128)(2,1)S(1)}, u32[]{:S(2)}, u32[]{:S(2)}) collective-permute-start(bf16[192,1024]{1,0:T(8,128)(2,1)} %pad_maximum_fusion.1), channel_id=1, source_target_pairs={{0,8},{8,0},{1,9},{9,1},{2,10},{10,2},{3,11},{11,3},{4,12},{12,4},... | collective-permute-start | bytes 1179656 | tf_op jit(solution)/shard_map/ppermute | solution.py:41
  16.2 1.2 reduce-window.6
  17.4 0.2 slice_reduce_fusion
  18.2 0.7 fusion.54
  19.0 0.7 fusion.16
  19.7 0.7 compare_convert_fusion.2
  20.4 0.7 compare_convert_fusion.1
  21.1 0.9 compare_convert_fusion
  22.0 0.9 fusion.9
  23.0 6.6 %all-to-all-done = bf16[32,8,1024]{2,1,0:T(8,128)(2,1)S(1)} async-done(((bf16[32,8,1024]{2,1,0:T(8,128)(2,1)}), bf16[32,8,1024]{2,1,0:T(8,128)(2,1)S(1)}, u32[]{:S(2)}, u32[]{:S(2)}) %all-to-all-start) | async-done | bytes 524320 | tf_op jit(solution)/shard_map/all_to_all | solution.py:39
  29.6 0.3 convolution_convert_fusion
  30.3 0.3 fusion.8
  30.6 17.9 %all_to_all.40 = bf16[8,6,128]{2,1,0:T(8,128)(2,1)S(1)} all-to-all(bf16[8,6,128]{2,1,0:T(8,128)(2,1)S(1)} %fusion.8), channel_id=1, replica_groups=mesh['x'=4,'y'=8,'c'=2,'z'=8] {'z'}, dimensions={0} | all-to-all | bytes 24576 | tf_op jit(solution)/shard_map/all_to_all | solution.py:130
  48.5 1.9 %collective-permute-start.1 = (bf16[256,1024]{1,0:T(8,128)(2,1)S(1)}, bf16[256,1024]{1,0:T(8,128)(2,1)S(1)}, u32[]{:S(2)}, u32[]{:S(2)}) collective-permute-start(bf16[256,1024]{1,0:T(8,128)(2,1)S(1)} %bitcast.100), channel_id=1, source_target_pairs={{0,8},{8,0},{1,9},{9,1},{2,10},{10,2},{3,11},{11,3},{4,12},{12,4},... | collective-permute-start | bytes 1572872 | tf_op jit(solution)/shard_map/ppermute | solution.py:132
  50.5 0.7 broadcast_in_dim.42
  51.1 5.4 %all-to-all-start.2 = ((bf16[64,6,128]{2,1,0:T(8,128)(2,1)}), bf16[64,6,128]{2,1,0:T(8,128)(2,1)S(1)}, u32[]{:S(2)}, u32[]{:S(2)}) async-start(bf16[64,6,128]{2,1,0:T(8,128)(2,1)} %broadcast_in_dim.42), calls=%async_computation.2 | async-start | bytes 262144 | tf_op jit(solution)/shard_map/all_to_all | solution.py:18
  56.6 1.0 copy-done.13
  57.7 0.7 convolution_bitcast_fusion.3
  58.4 0.7 convolution_bitcast_fusion.4
  59.0 7.5 %all-to-all-done.2 = bf16[64,6,128]{2,1,0:T(8,128)(2,1)S(1)} async-done(((bf16[64,6,128]{2,1,0:T(8,128)(2,1)}), bf16[64,6,128]{2,1,0:T(8,128)(2,1)S(1)}, u32[]{:S(2)}, u32[]{:S(2)}) %all-to-all-start.2) | async-done | bytes 98336 | tf_op jit(solution)/shard_map/all_to_all | solution.py:18
  66.6 1.4 fusion.7
  68.0 1.4 convolution_bitcast_fusion.2
  69.3 0.2 add_convert_fusion.2
  69.6 0.5 convolution_bitcast_fusion.1
  70.0 0.2 add_convert_fusion.1
  70.4 29.0 %all_to_all.41 = bf16[8,2,56,512]{3,2,1,0:T(8,128)(2,1)S(1)} all-to-all(bf16[8,2,56,512]{3,2,1,0:T(8,128)(2,1)S(1)} %pad_maximum_fusion), channel_id=1, replica_groups=mesh['x'=4,'y'=8,'c'=2,'z'=8] {'z'}, dimensions={0} | all-to-all | bytes 1835008 | tf_op jit(solution)/shard_map/all_to_all | solution.py:163
  99.6 18.9 %all_to_all.42 = bf16[8,56,512]{2,1,0:T(8,128)(2,1)S(1)} all-to-all(bf16[8,56,512]{2,1,0:T(8,128)(2,1)S(1)} %broadcast_in_dim.45), channel_id=1, replica_groups=mesh['x'=4,'y'=8,'c'=2,'z'=8] {'z'}, dimensions={0} | all-to-all | bytes 917504 | tf_op jit(solution)/shard_map/all_to_all | solution.py:18
  118.6 0.4 multiply_reduce_fusion
  119.0 0.2 convolution_convert_fusion.2
  119.2 0.7 reshape.547
  119.9 5.5 %all-to-all-start.5 = ((bf16[64,3,128]{2,1,0:T(4,128)(2,1)}), bf16[64,3,128]{2,1,0:T(4,128)(2,1)}, u32[]{:S(2)}, u32[]{:S(2)}) async-start(bf16[64,3,128]{2,1,0:T(4,128)(2,1)} %reshape.547), calls=%async_computation.5 | async-start | bytes 131072 | tf_op jit(solution)/shard_map/all_to_all | solution.py:176
  125.4 0.7 fusion.108
  126.1 1.0 slice.97
  127.1 7.2 %all-to-all-done.5 = bf16[64,3,128]{2,1,0:T(4,128)(2,1)} async-done(((bf16[64,3,128]{2,1,0:T(4,128)(2,1)}), bf16[64,3,128]{2,1,0:T(4,128)(2,1)}, u32[]{:S(2)}, u32[]{:S(2)}) %all-to-all-start.5) | async-done | bytes 49184 | tf_op jit(solution)/shard_map/all_to_all | solution.py:176
  134.3 0.9 reduce_sum.77
  135.2 0.6 broadcast_in_dim.47
  135.8 3.3 %all-to-all-start.6 = ((bf16[8,3,128]{2,1,0:T(4,128)(2,1)}), bf16[8,3,128]{2,1,0:T(4,128)(2,1)S(1)}, u32[]{:S(2)}, u32[]{:S(2)}) async-start(bf16[8,3,128]{2,1,0:T(4,128)(2,1)} %broadcast_in_dim.47), calls=%async_computation.6 | async-start | bytes 16384 | tf_op jit(solution)/shard_map/all_to_all | solution.py:18
  139.2 2.0 %collective-permute-start.2 = (bf16[256,1024]{1,0:T(8,128)(2,1)}, bf16[256,1024]{1,0:T(8,128)(2,1)}, u32[]{:S(2)}, u32[]{:S(2)}) collective-permute-start(bf16[256,1024]{1,0:T(8,128)(2,1)} %slice.97), channel_id=1, source_target_pairs={{0,8},{8,0},{1,9},{9,1},{2,10},{10,2},{3,11},{11,3},{4,12},{12,4},... | collective-permute-start | bytes 1572872 | tf_op jit(solution)/shard_map/ppermute | solution.py:184
  141.2 5.6 %all-to-all-done.6 = bf16[8,3,128]{2,1,0:T(4,128)(2,1)S(1)} async-done(((bf16[8,3,128]{2,1,0:T(4,128)(2,1)}), bf16[8,3,128]{2,1,0:T(4,128)(2,1)S(1)}, u32[]{:S(2)}, u32[]{:S(2)}) %all-to-all-start.6) | async-done | bytes 6176 | tf_op jit(solution)/shard_map/all_to_all | solution.py:18
  146.8 0.3 fusion.69
  147.2 1.0 convert_multiply_fusion
  148.2 0.2 slice-done
  148.5 1.6 fusion.10
  150.1 21.0 %all_to_all.43 = bf16[32,8,1024]{2,1,0:T(8,128)(2,1)S(1)} all-to-all(bf16[32,8,1024]{2,1,0:T(8,128)(2,1)S(1)} %fusion.10), channel_id=1, replica_groups=mesh['x'=4,'y'=8,'c'=2,'z'=8] {'x','y'}, dimensions={0} | all-to-all | bytes 1048576 | tf_op jit(solution)/shard_map/all_to_all | solution.py:197
  171.1 0.7 reduce_sum.78
  (85 shorter events, 1.9 us)
Async XLA Ops:
  0.0 125.4 %copy-start = (bf16[448,1024]{1,0:T(8,128)(2,1)S(1)}, bf16[448,1024]{1,0:T(8,128)(2,1)}, u32[]{:S(2)}) copy-start(bf16[448,1024]{1,0:T(8,128)(2,1)} %param.15) | copy-start | bytes 2752516
  0.0 15.7 %copy-start.12 = (s32[64]{0:T(128)S(1)}, s32[64]{0:T(128)}, u32[]{:S(2)}) copy-start(s32[64]{0:T(128)} %param.23) | copy-start | bytes 772
  0.0 15.7 %copy-start.11 = (s32[512,1]{0,1:T(1,128)S(1)}, s32[512,1]{0,1:T(1,128)}, u32[]{:S(2)}) copy-start(s32[512,1]{0,1:T(1,128)} %param.22) | copy-start | bytes 6148
  1.7 21.2 %copy-start.6 = (bf16[1,1024,64]{1,2,0:T(8,128)(2,1)S(1)}, bf16[1,1024,64]{1,2,0:T(8,128)(2,1)}, u32[]{:S(2)}) copy-start(bf16[1,1024,64]{1,2,0:T(8,128)(2,1)} %param.17) | copy-start | bytes 393220
  1.7 21.2 %copy-start.7 = (bf16[1,1024,64]{1,2,0:T(8,128)(2,1)S(1)}, bf16[1,1024,64]{1,2,0:T(8,128)(2,1)}, u32[]{:S(2)}) copy-start(bf16[1,1024,64]{1,2,0:T(8,128)(2,1)} %param.16) | copy-start | bytes 393220
  1.7 21.3 %copy-start.5 = (bf16[64,8,448]{2,1,0:T(8,128)(2,1)S(1)}, bf16[64,8,448]{2,1,0:T(8,128)(2,1)}, u32[]{:S(2)}) copy-start(bf16[64,8,448]{2,1,0:T(8,128)(2,1)} %param.18) | copy-start | bytes 1376260
  1.7 27.9 %all-to-all-start = ((bf16[32,8,1024]{2,1,0:T(8,128)(2,1)}), bf16[32,8,1024]{2,1,0:T(8,128)(2,1)S(1)}, u32[]{:S(2)}, u32[]{:S(2)}) async-start(bf16[32,8,1024]{2,1,0:T(8,128)(2,1)} %broadcast_in_dim.36), calls=%async_computation | async-start | bytes 1048576 | tf_op jit(solution)/shard_map/all_to_all | solution.py:39
  13.8 9.2 %collective-permute-start = (bf16[192,1024]{1,0:T(8,128)(2,1)}, bf16[192,1024]{1,0:T(8,128)(2,1)S(1)}, u32[]{:S(2)}, u32[]{:S(2)}) collective-permute-start(bf16[192,1024]{1,0:T(8,128)(2,1)} %pad_maximum_fusion.1), channel_id=1, source_target_pairs={{0,8},{8,0},{1,9},{9,1},{2,10},{10,2},{3,11},{11,3},{4,12},{12,4},... | collective-permute-start | bytes 1179656 | tf_op jit(solution)/shard_map/ppermute | solution.py:41
  23.0 33.6 %copy-start.3 = (bf16[192,1024]{1,0:T(8,128)(2,1)}, bf16[192,1024]{1,0:T(8,128)(2,1)S(1)}, u32[]{:S(2)}) copy-start(bf16[192,1024]{1,0:T(8,128)(2,1)S(1)} %collective-permute-done) | copy-start | bytes 1179652
  48.5 8.0 %collective-permute-start.1 = (bf16[256,1024]{1,0:T(8,128)(2,1)S(1)}, bf16[256,1024]{1,0:T(8,128)(2,1)S(1)}, u32[]{:S(2)}, u32[]{:S(2)}) collective-permute-start(bf16[256,1024]{1,0:T(8,128)(2,1)S(1)} %bitcast.100), channel_id=1, source_target_pairs={{0,8},{8,0},{1,9},{9,1},{2,10},{10,2},{3,11},{11,3},{4,12},{12,4},... | collective-permute-start | bytes 1572872 | tf_op jit(solution)/shard_map/ppermute | solution.py:132
  51.1 15.4 %all-to-all-start.2 = ((bf16[64,6,128]{2,1,0:T(8,128)(2,1)}), bf16[64,6,128]{2,1,0:T(8,128)(2,1)S(1)}, u32[]{:S(2)}, u32[]{:S(2)}) async-start(bf16[64,6,128]{2,1,0:T(8,128)(2,1)} %broadcast_in_dim.42), calls=%async_computation.2 | async-start | bytes 262144 | tf_op jit(solution)/shard_map/all_to_all | solution.py:18
  56.5 1.2 copy-start.13
  56.5 1.8 %copy-start.14 = (bf16[448,1024]{1,0:T(8,128)(2,1)S(1)}, bf16[448,1024]{1,0:T(8,128)(2,1)}, u32[]{:S(2)}) copy-start(bf16[448,1024]{1,0:T(8,128)(2,1)} %param.13) | copy-start | bytes 2752516
  68.0 1.6 copy-start.10
  68.0 1.6 copy-start.15
  70.4 48.2 %copy-start.9 = (f32[64,512]{1,0:T(8,128)S(1)}, f32[64,512]{1,0:T(8,128)}, u32[]{:S(2)}) copy-start(f32[64,512]{1,0:T(8,128)} %get-tuple-element.47) | copy-start | bytes 393220
  70.4 48.2 %copy-start.16 = (bf16[448,64,8]{0,2,1:T(8,128)(2,1)S(1)}, bf16[448,64,8]{0,2,1:T(8,128)(2,1)}, u32[]{:S(2)}) copy-start(bf16[448,64,8]{0,2,1:T(8,128)(2,1)} %param.20) | copy-start | bytes 1376260
  99.4 19.6 %copy-start.8 = (bf16[192,512]{1,0:T(8,128)(2,1)S(1)}, bf16[192,512]{1,0:T(8,128)(2,1)}, u32[]{:S(2)}) copy-start(bf16[192,512]{1,0:T(8,128)(2,1)} %fusion.16) | copy-start | bytes 589828
  119.9 14.4 %all-to-all-start.5 = ((bf16[64,3,128]{2,1,0:T(4,128)(2,1)}), bf16[64,3,128]{2,1,0:T(4,128)(2,1)}, u32[]{:S(2)}, u32[]{:S(2)}) async-start(bf16[64,3,128]{2,1,0:T(4,128)(2,1)} %reshape.547), calls=%async_computation.5 | async-start | bytes 131072 | tf_op jit(solution)/shard_map/all_to_all | solution.py:176
  126.1 21.1 %copy-start.1 = (f32[512,1024]{1,0:T(8,128)}, f32[512,1024]{1,0:T(8,128)S(1)}, u32[]{:S(2)}) copy-start(f32[512,1024]{1,0:T(8,128)S(1)} %fusion.108) | copy-start | bytes 6291460
  127.1 21.1 %copy-start.2 = (bf16[1024,128]{1,0:T(8,128)(2,1)S(1)}, bf16[1024,128]{1,0:T(8,128)(2,1)}, u32[]{:S(2)}) copy-start(bf16[1024,128]{1,0:T(8,128)(2,1)} %compare_convert_fusion) | copy-start | bytes 786436
  127.1 21.1 %slice-start.1 = ((bf16[192,1024]{1,0:T(8,128)(2,1)}), bf16[64,1024]{1,0:T(8,128)(2,1)S(1)}, s32[]{:S(2)}) async-start(bf16[192,1024]{1,0:T(8,128)(2,1)} %copy-done.3), calls=%async_computation.9 | async-start | bytes 262144 | tf_op jit(solution)/shard_map/slice | solution.py:43
  127.1 21.1 %copy-start.4 = (bf16[1,64,1024]{2,1,0:T(8,128)(2,1)S(1)}, bf16[1,64,1024]{2,1,0:T(8,128)(2,1)}, u32[]{:S(2)}) copy-start(bf16[1,64,1024]{2,1,0:T(8,128)(2,1)} %param.21) | copy-start | bytes 393220
  135.8 11.0 %all-to-all-start.6 = ((bf16[8,3,128]{2,1,0:T(4,128)(2,1)}), bf16[8,3,128]{2,1,0:T(4,128)(2,1)S(1)}, u32[]{:S(2)}, u32[]{:S(2)}) async-start(bf16[8,3,128]{2,1,0:T(4,128)(2,1)} %broadcast_in_dim.47), calls=%async_computation.6 | async-start | bytes 16384 | tf_op jit(solution)/shard_map/all_to_all | solution.py:18
  139.2 9.0 %collective-permute-start.2 = (bf16[256,1024]{1,0:T(8,128)(2,1)}, bf16[256,1024]{1,0:T(8,128)(2,1)}, u32[]{:S(2)}, u32[]{:S(2)}) collective-permute-start(bf16[256,1024]{1,0:T(8,128)(2,1)} %slice.97), channel_id=1, source_target_pairs={{0,8},{8,0},{1,9},{9,1},{2,10},{10,2},{3,11},{11,3},{4,12},{12,4},... | collective-permute-start | bytes 1572872 | tf_op jit(solution)/shard_map/ppermute | solution.py:184
  147.2 1.3 slice-start

commit v9 on v6

--- a/solution.py
+++ b/solution.py
@@ -88,21 +88,21 @@
     column = jnp.arange(parts * LANES, dtype=jnp.int32)
     gathered = column // LANES * rank_part + column % rank_part
     fold = gathered[:, None] == jnp.arange(cores * rank, dtype=jnp.int32)[None, :] % rank
+    one = lax.optimization_barrier(jnp.ones((), BF16))
     masks = (
-        slot_rows,
         slot_rows.astype(F32),
         down_pick,
         down_seat,
         ours,
         our_seat,
         our_slot,
-        up_pick,
         fold.astype(BF16),
         shrink_pair,
+        b_gate * one,
     )
     half, masks = lax.optimization_barrier((half, masks))
-    slot_rows, slot_mask, down_pick, down_seat, ours, our_seat, our_slot, up_pick = masks[:8]
-    fold, shrink_pair = masks[8:]
+    slot_mask, down_pick, down_seat, ours, our_seat, our_slot = masks[:6]
+    fold, shrink_pair, b_gate = masks[6:]
     selected = lax.dot_general(mine, half, TN, preferred_element_type=F32).astype(BF16)
     shrunk = jnp.concatenate(
         [
@@ -144,7 +144,7 @@
     low_rows = jnp.dot(gather_up.astype(BF16), low_rows, preferred_element_type=F32).astype(BF16)
 
     def expand(low, weights):
-        wide = (slot_rows[:, None, :] * low[None, :, :]).reshape(slots * rank_part, rows)
+        wide = (slot_mask.astype(BF16)[:, None, :] * low[None, :, :]).reshape(slots * rank_part, rows)
         return lax.dot_general(
             weights.reshape(slots * rank_part, units), wide, TN, preferred_element_type=F32
         )

time: 172 us -> 177 us (1.029)
  other arithmetic: 9.73 us -> 14.4 us
  waiting for transfers between devices: 27.1 us -> 23.1 us
  matrix products: 8.12 us -> 10.3 us
    all_to_all x1, waiting for transfers between devices: 8.14 us -> 4.19 us  [per_device(): half = lax.all_to_all(half, CHIPS, 0, 0, tiled=True)]
  transfers between devices with their start and end apart: 7 -> 7, of which waited for: 4 -> 4; matrix products, arithmetic and copies ran while one was open for 8% -> 11% of each run, Pallas kernels for 0% -> 0%
where the time goes in v9:
time: 177 us; the launch traced here: 176 us
  blocking collectives  86.8 us (49%)
  starting transfers between devices  31.1 us (18%)
  waiting for transfers between devices  23.1 us (13%)
  other arithmetic  14.4 us (8%)
  matrix products  10.3 us (6%)
  local copies, waits for them, and re-layouts  9.5 us (5%)
    all_to_all x1, blocking collectives, per_device(): both = lax.all_to_all(both, 'z', 0, 0, tiled=True)  29 us
    all_to_all x1, blocking collectives, per_device(): lax.all_to_all(out.reshape(chips, own_rows, width), CHIPS, 0, 0, tiled=True)  21 us
    all_to_all x1, blocking collectives, spread(): return lax.all_to_all(copies, axes, 0, 0, tiled=True)  18.9 us
    all_to_all x1, blocking collectives, per_device(): shrunk = lax.all_to_all(shrunk, 'z', 0, 0, tiled=True)  17.9 us
    all_to_all x2, waiting for transfers between devices, spread(): return lax.all_to_all(copies, axes, 0, 0, tiled=True)  11.7 us
    all_to_all x1, starting transfers between devices, per_device(): half = lax.all_to_all(half, CHIPS, 0, 0, tiled=True)  10.3 us
    all_to_all x2, starting transfers between devices, spread(): return lax.all_to_all(copies, axes, 0, 0, tiled=True)  9.46 us
    all_to_all x1, waiting for transfers between devices, per_device(): lax.all_to_all(rank_sent.reshape(owners, down_lines, LANES), OWN, 0, 0, t...  7.19 us
  transfers between devices with their start and end apart: 7, of which 4 were waited for; matrix products, arithmetic and copies ran while one was open for 11% of the time, Pallas kernels for 0%

profile of v9, /device:TPU:8, one launch (start us, length us, event | category | flops | bytes accessed | tf_op | source)
XLA Modules:
  0.0 175.8 jit_solution(18338039712237794858)
XLA Ops:
  0.0 1.7 broadcast_in_dim.48
  1.7 10.3 %all-to-all-start = ((bf16[32,8,1024]{2,1,0:T(8,128)(2,1)}), bf16[32,8,1024]{2,1,0:T(8,128)(2,1)S(1)}, u32[]{:S(2)}, u32[]{:S(2)}) async-start(bf16[32,8,1024]{2,1,0:T(8,128)(2,1)} %broadcast_in_dim.48), calls=%async_computation | async-start | bytes 1048576 | tf_op jit(solution)/shard_map/all_to_all | solution.py:39
  12.0 1.8 %pad_maximum_fusion.1 = bf16[192,1024]{1,0:T(8,128)(2,1)} fusion(bf16[64,1024]{1,0:T(8,128)(2,1)} %bitcast.107, bf16[64,1024]{1,0:T(8,128)(2,1)} %bitcast.109, bf16[64,1024]{1,0:T(8,128)(2,1)} %bitcast.111), kind=kLoop, calls=%fused_computation.35 | loop fusion | flops 1179648 | bytes 786432 | tf_op jit(solution)/shard_map/concatenate | solution.py:40
  13.8 1.9 %collective-permute-start = (bf16[192,1024]{1,0:T(8,128)(2,1)}, bf16[192,1024]{1,0:T(8,128)(2,1)S(1)}, u32[]{:S(2)}, u32[]{:S(2)}) collective-permute-start(bf16[192,1024]{1,0:T(8,128)(2,1)} %pad_maximum_fusion.1), channel_id=1, source_target_pairs={{0,8},{8,0},{1,9},{9,1},{2,10},{10,2},{3,11},{11,3},{4,12},{12,4},... | collective-permute-start | bytes 1179656 | tf_op jit(solution)/shard_map/ppermute | solution.py:41
  15.8 0.6 add_select_fusion.3
  16.8 1.2 reduce-window.6
  18.7 0.6 add_select_fusion.6
  19.3 0.6 fusion.98
  20.5 0.6 fusion.92
  21.1 0.7 broadcast_compare_fusion.1
  21.8 0.7 broadcast_compare_fusion
  22.5 0.7 fusion.15
  23.3 0.9 compare_convert_fusion
  24.2 0.6 and_select_fusion.2
  24.7 0.5 slice.61
  25.4 4.2 %all-to-all-done = bf16[32,8,1024]{2,1,0:T(8,128)(2,1)S(1)} async-done(((bf16[32,8,1024]{2,1,0:T(8,128)(2,1)}), bf16[32,8,1024]{2,1,0:T(8,128)(2,1)S(1)}, u32[]{:S(2)}, u32[]{:S(2)}) %all-to-all-start) | async-done | bytes 524320 | tf_op jit(solution)/shard_map/all_to_all | solution.py:39
  29.6 1.0 convolution_convert_fusion
  31.0 1.0 fusion.6
  32.0 17.9 %all_to_all.40 = bf16[8,6,128]{2,1,0:T(8,128)(2,1)S(1)} all-to-all(bf16[8,6,128]{2,1,0:T(8,128)(2,1)S(1)} %fusion.6), channel_id=1, replica_groups=mesh['x'=4,'y'=8,'c'=2,'z'=8] {'z'}, dimensions={0} | all-to-all | bytes 24576 | tf_op jit(solution)/shard_map/all_to_all | solution.py:128
  49.9 1.9 %collective-permute-start.1 = (bf16[256,1024]{1,0:T(8,128)(2,1)S(1)}, bf16[256,1024]{1,0:T(8,128)(2,1)S(1)}, u32[]{:S(2)}, u32[]{:S(2)}) collective-permute-start(bf16[256,1024]{1,0:T(8,128)(2,1)S(1)} %bitcast.99), channel_id=1, source_target_pairs={{0,8},{8,0},{1,9},{9,1},{2,10},{10,2},{3,11},{11,3},{4,12},{12,4},... | collective-permute-start | bytes 1572872 | tf_op jit(solution)/shard_map/ppermute | solution.py:130
  51.8 0.6 and_select_fusion
  52.4 0.6 convert_element_type.118
  53.0 0.7 broadcast_in_dim.55
  53.7 6.1 %all-to-all-start.2 = ((bf16[64,6,128]{2,1,0:T(8,128)(2,1)}), bf16[64,6,128]{2,1,0:T(8,128)(2,1)S(1)}, u32[]{:S(2)}, u32[]{:S(2)}) async-start(bf16[64,6,128]{2,1,0:T(8,128)(2,1)} %broadcast_in_dim.55), calls=%async_computation.2 | async-start | bytes 262144 | tf_op jit(solution)/shard_map/all_to_all | solution.py:18
  59.9 1.0 copy-done.13
  61.0 0.7 convolution_bitcast_fusion.3
  61.7 0.7 convolution_bitcast_fusion.4
  62.4 7.5 %all-to-all-done.2 = bf16[64,6,128]{2,1,0:T(8,128)(2,1)S(1)} async-done(((bf16[64,6,128]{2,1,0:T(8,128)(2,1)}), bf16[64,6,128]{2,1,0:T(8,128)(2,1)S(1)}, u32[]{:S(2)}, u32[]{:S(2)}) %all-to-all-start.2) | async-done | bytes 98336 | tf_op jit(solution)/shard_map/all_to_all | solution.py:18
  69.8 0.7 reshape.543
  70.5 1.4 fusion.4
  72.0 1.4 convolution_bitcast_fusion.2
  74.4 29.0 %all_to_all.41 = bf16[8,2,56,512]{3,2,1,0:T(8,128)(2,1)S(1)} all-to-all(bf16[8,2,56,512]{3,2,1,0:T(8,128)(2,1)S(1)} %pad_maximum_fusion), channel_id=1, replica_groups=mesh['x'=4,'y'=8,'c'=2,'z'=8] {'z'}, dimensions={0} | all-to-all | bytes 1835008 | tf_op jit(solution)/shard_map/all_to_all | solution.py:161
  103.6 18.9 %all_to_all.42 = bf16[8,56,512]{2,1,0:T(8,128)(2,1)S(1)} all-to-all(bf16[8,56,512]{2,1,0:T(8,128)(2,1)S(1)} %broadcast_in_dim.58), channel_id=1, replica_groups=mesh['x'=4,'y'=8,'c'=2,'z'=8] {'z'}, dimensions={0} | all-to-all | bytes 917504 | tf_op jit(solution)/shard_map/all_to_all | solution.py:18
  123.2 0.7 reshape.547
  123.9 5.5 %all-to-all-start.5 = ((bf16[64,3,128]{2,1,0:T(4,128)(2,1)}), bf16[64,3,128]{2,1,0:T(4,128)(2,1)}, u32[]{:S(2)}, u32[]{:S(2)}) async-start(bf16[64,3,128]{2,1,0:T(4,128)(2,1)} %reshape.547), calls=%async_computation.5 | async-start | bytes 131072 | tf_op jit(solution)/shard_map/all_to_all | solution.py:174
  129.4 0.7 fusion.112
  130.1 1.0 slice.97
  131.1 7.2 %all-to-all-done.5 = bf16[64,3,128]{2,1,0:T(4,128)(2,1)} async-done(((bf16[64,3,128]{2,1,0:T(4,128)(2,1)}), bf16[64,3,128]{2,1,0:T(4,128)(2,1)}, u32[]{:S(2)}, u32[]{:S(2)}) %all-to-all-start.5) | async-done | bytes 49184 | tf_op jit(solution)/shard_map/all_to_all | solution.py:174
  138.3 0.9 reduce_sum.77
  139.3 0.6 broadcast_in_dim.60
  139.9 3.3 %all-to-all-start.6 = ((bf16[8,3,128]{2,1,0:T(4,128)(2,1)}), bf16[8,3,128]{2,1,0:T(4,128)(2,1)S(1)}, u32[]{:S(2)}, u32[]{:S(2)}) async-start(bf16[8,3,128]{2,1,0:T(4,128)(2,1)} %broadcast_in_dim.60), calls=%async_computation.6 | async-start | bytes 16384 | tf_op jit(solution)/shard_map/all_to_all | solution.py:18
  143.2 2.0 %collective-permute-start.2 = (bf16[256,1024]{1,0:T(8,128)(2,1)}, bf16[256,1024]{1,0:T(8,128)(2,1)}, u32[]{:S(2)}, u32[]{:S(2)}) collective-permute-start(bf16[256,1024]{1,0:T(8,128)(2,1)} %slice.97), channel_id=1, source_target_pairs={{0,8},{8,0},{1,9},{9,1},{2,10},{10,2},{3,11},{11,3},{4,12},{12,4},... | collective-permute-start | bytes 1572872 | tf_op jit(solution)/shard_map/ppermute | solution.py:182
  145.2 1.4 copy.39
  146.6 4.3 %all-to-all-done.6 = bf16[8,3,128]{2,1,0:T(4,128)(2,1)S(1)} async-done(((bf16[8,3,128]{2,1,0:T(4,128)(2,1)}), bf16[8,3,128]{2,1,0:T(4,128)(2,1)S(1)}, u32[]{:S(2)}, u32[]{:S(2)}) %all-to-all-start.6) | async-done | bytes 6176 | tf_op jit(solution)/shard_map/all_to_all | solution.py:18
  151.2 0.9 select_convert_fusion
  152.5 1.6 fusion.7
  154.1 21.0 %all_to_all.43 = bf16[32,8,1024]{2,1,0:T(8,128)(2,1)S(1)} all-to-all(bf16[32,8,1024]{2,1,0:T(8,128)(2,1)S(1)} %fusion.7), channel_id=1, replica_groups=mesh['x'=4,'y'=8,'c'=2,'z'=8] {'x','y'}, dimensions={0} | all-to-all | bytes 1048576 | tf_op jit(solution)/shard_map/all_to_all | solution.py:195
  175.1 0.7 reduce_sum.78
  (87 shorter events, 4.7 us)
Async XLA Ops:
  0.0 129.4 %copy-start = (bf16[448,1024]{1,0:T(8,128)(2,1)S(1)}, bf16[448,1024]{1,0:T(8,128)(2,1)}, u32[]{:S(2)}) copy-start(bf16[448,1024]{1,0:T(8,128)(2,1)} %param.15) | copy-start | bytes 2752516
  0.0 25.3 %copy-start.6 = (bf16[1,1024,64]{1,2,0:T(8,128)(2,1)S(1)}, bf16[1,1024,64]{1,2,0:T(8,128)(2,1)}, u32[]{:S(2)}) copy-start(bf16[1,1024,64]{1,2,0:T(8,128)(2,1)} %param.17) | copy-start | bytes 393220
  0.0 25.3 %copy-start.7 = (bf16[1,1024,64]{1,2,0:T(8,128)(2,1)S(1)}, bf16[1,1024,64]{1,2,0:T(8,128)(2,1)}, u32[]{:S(2)}) copy-start(bf16[1,1024,64]{1,2,0:T(8,128)(2,1)} %param.16) | copy-start | bytes 393220
  0.0 16.3 %copy-start.12 = (s32[64]{0:T(128)S(1)}, s32[64]{0:T(128)}, u32[]{:S(2)}) copy-start(s32[64]{0:T(128)} %param.23) | copy-start | bytes 772
  0.0 16.3 %copy-start.11 = (s32[512,1]{0,1:T(1,128)S(1)}, s32[512,1]{0,1:T(1,128)}, u32[]{:S(2)}) copy-start(s32[512,1]{0,1:T(1,128)} %param.22) | copy-start | bytes 6148
  1.7 23.6 %copy-start.5 = (bf16[64,8,448]{2,1,0:T(8,128)(2,1)S(1)}, bf16[64,8,448]{2,1,0:T(8,128)(2,1)}, u32[]{:S(2)}) copy-start(bf16[64,8,448]{2,1,0:T(8,128)(2,1)} %param.18) | copy-start | bytes 1376260
  1.7 27.9 %all-to-all-start = ((bf16[32,8,1024]{2,1,0:T(8,128)(2,1)}), bf16[32,8,1024]{2,1,0:T(8,128)(2,1)S(1)}, u32[]{:S(2)}, u32[]{:S(2)}) async-start(bf16[32,8,1024]{2,1,0:T(8,128)(2,1)} %broadcast_in_dim.48), calls=%async_computation | async-start | bytes 1048576 | tf_op jit(solution)/shard_map/all_to_all | solution.py:39
  13.8 11.6 %collective-permute-start = (bf16[192,1024]{1,0:T(8,128)(2,1)}, bf16[192,1024]{1,0:T(8,128)(2,1)S(1)}, u32[]{:S(2)}, u32[]{:S(2)}) collective-permute-start(bf16[192,1024]{1,0:T(8,128)(2,1)} %pad_maximum_fusion.1), channel_id=1, source_target_pairs={{0,8},{8,0},{1,9},{9,1},{2,10},{10,2},{3,11},{11,3},{4,12},{12,4},... | collective-permute-start | bytes 1179656 | tf_op jit(solution)/shard_map/ppermute | solution.py:41
  25.4 34.5 %copy-start.3 = (bf16[192,1024]{1,0:T(8,128)(2,1)}, bf16[192,1024]{1,0:T(8,128)(2,1)S(1)}, u32[]{:S(2)}) copy-start(bf16[192,1024]{1,0:T(8,128)(2,1)S(1)} %collective-permute-done) | copy-start | bytes 1179652
  49.9 10.0 %collective-permute-start.1 = (bf16[256,1024]{1,0:T(8,128)(2,1)S(1)}, bf16[256,1024]{1,0:T(8,128)(2,1)S(1)}, u32[]{:S(2)}, u32[]{:S(2)}) collective-permute-start(bf16[256,1024]{1,0:T(8,128)(2,1)S(1)} %bitcast.99), channel_id=1, source_target_pairs={{0,8},{8,0},{1,9},{9,1},{2,10},{10,2},{3,11},{11,3},{4,12},{12,4},... | collective-permute-start | bytes 1572872 | tf_op jit(solution)/shard_map/ppermute | solution.py:130
  53.7 16.2 %all-to-all-start.2 = ((bf16[64,6,128]{2,1,0:T(8,128)(2,1)}), bf16[64,6,128]{2,1,0:T(8,128)(2,1)S(1)}, u32[]{:S(2)}, u32[]{:S(2)}) async-start(bf16[64,6,128]{2,1,0:T(8,128)(2,1)} %broadcast_in_dim.55), calls=%async_computation.2 | async-start | bytes 262144 | tf_op jit(solution)/shard_map/all_to_all | solution.py:18
  59.8 1.2 copy-start.13
  59.9 1.8 %copy-start.14 = (bf16[448,1024]{1,0:T(8,128)(2,1)S(1)}, bf16[448,1024]{1,0:T(8,128)(2,1)}, u32[]{:S(2)}) copy-start(bf16[448,1024]{1,0:T(8,128)(2,1)} %param.13) | copy-start | bytes 2752516
  71.9 1.6 copy-start.9
  71.9 1.6 copy-start.15
  74.3 48.2 %copy-start.16 = (bf16[448,64,8]{0,2,1:T(8,128)(2,1)S(1)}, bf16[448,64,8]{0,2,1:T(8,128)(2,1)}, u32[]{:S(2)}) copy-start(bf16[448,64,8]{0,2,1:T(8,128)(2,1)} %param.20) | copy-start | bytes 1376260
  103.4 19.6 %copy-start.8 = (bf16[192,512]{1,0:T(8,128)(2,1)S(1)}, bf16[192,512]{1,0:T(8,128)(2,1)}, u32[]{:S(2)}) copy-start(bf16[192,512]{1,0:T(8,128)(2,1)} %fusion.15) | copy-start | bytes 589828
  123.9 14.5 %all-to-all-start.5 = ((bf16[64,3,128]{2,1,0:T(4,128)(2,1)}), bf16[64,3,128]{2,1,0:T(4,128)(2,1)}, u32[]{:S(2)}, u32[]{:S(2)}) async-start(bf16[64,3,128]{2,1,0:T(4,128)(2,1)} %reshape.547), calls=%async_computation.5 | async-start | bytes 131072 | tf_op jit(solution)/shard_map/all_to_all | solution.py:174
  130.1 21.1 %copy-start.1 = (f32[512,1024]{1,0:T(8,128)}, f32[512,1024]{1,0:T(8,128)S(1)}, u32[]{:S(2)}) copy-start(f32[512,1024]{1,0:T(8,128)S(1)} %fusion.112) | copy-start | bytes 6291460
  130.1 20.7 %copy-start.10 = (bf16[256,3]{0,1:T(4,128)(2,1)S(1)}, bf16[256,3]{0,1:T(4,128)(2,1)}, u32[]{:S(2)}) copy-start(bf16[256,3]{0,1:T(4,128)(2,1)} %fusion.92) | copy-start | bytes 4612
  131.1 21.1 %copy-start.2 = (bf16[1024,128]{1,0:T(8,128)(2,1)S(1)}, bf16[1024,128]{1,0:T(8,128)(2,1)}, u32[]{:S(2)}) copy-start(bf16[1024,128]{1,0:T(8,128)(2,1)} %compare_convert_fusion) | copy-start | bytes 786436
  131.1 21.1 %slice-start.1 = ((bf16[192,1024]{1,0:T(8,128)(2,1)}), bf16[64,1024]{1,0:T(8,128)(2,1)S(1)}, s32[]{:S(2)}) async-start(bf16[192,1024]{1,0:T(8,128)(2,1)} %copy-done.3), calls=%async_computation.9 | async-start | bytes 262144 | tf_op jit(solution)/shard_map/slice | solution.py:43
  131.1 21.1 %copy-start.4 = (bf16[1,64,1024]{2,1,0:T(8,128)(2,1)S(1)}, bf16[1,64,1024]{2,1,0:T(8,128)(2,1)}, u32[]{:S(2)}) copy-start(bf16[1,64,1024]{2,1,0:T(8,128)(2,1)} %param.21) | copy-start | bytes 393220
  139.9 11.0 %all-to-all-start.6 = ((bf16[8,3,128]{2,1,0:T(4,128)(2,1)}), bf16[8,3,128]{2,1,0:T(4,128)(2,1)S(1)}, u32[]{:S(2)}, u32[]{:S(2)}) async-start(bf16[8,3,128]{2,1,0:T(4,128)(2,1)} %broadcast_in_dim.60), calls=%async_computation.6 | async-start | bytes 16384 | tf_op jit(solution)/shard_map/all_to_all | solution.py:18
  143.2 9.0 %collective-permute-start.2 = (bf16[256,1024]{1,0:T(8,128)(2,1)}, bf16[256,1024]{1,0:T(8,128)(2,1)}, u32[]{:S(2)}, u32[]{:S(2)}) collective-permute-start(bf16[256,1024]{1,0:T(8,128)(2,1)} %slice.97), channel_id=1, source_target_pairs={{0,8},{8,0},{1,9},{9,1},{2,10},{10,2},{3,11},{11,3},{4,12},{12,4},... | collective-permute-start | bytes 1572872 | tf_op jit(solution)/shard_map/ppermute | solution.py:182
  151.2 1.2 slice-start

commit v10 on v8

--- a/solution.py
+++ b/solution.py
@@ -88,7 +88,6 @@
     column = jnp.arange(parts * LANES, dtype=jnp.int32)
     gathered = column // LANES * rank_part + column % rank_part
     fold = gathered[:, None] == jnp.arange(cores * rank, dtype=jnp.int32)[None, :] % rank
-    one = lax.optimization_barrier(jnp.ones((), BF16))
     masks = (
         slot_rows,
         slot_rows.astype(F32),
@@ -100,11 +99,10 @@
         up_pick,
         fold.astype(BF16),
         shrink_pair,
-        b_gate * one,
     )
     half, masks = lax.optimization_barrier((half, masks))
     slot_rows, slot_mask, down_pick, down_seat, ours, our_seat, our_slot, up_pick = masks[:8]
-    fold, shrink_pair, b_gate = masks[8:]
+    fold, shrink_pair = masks[8:]
     selected = lax.dot_general(mine, half, TN, preferred_element_type=F32).astype(BF16)
     shrunk = jnp.concatenate(
         [

time: 173 us -> 172 us (level)
  transfers between devices with their start and end apart: 7 -> 7, of which waited for: 4 -> 4; matrix products, arithmetic and copies ran while one was open for 8% -> 7% of each run, Pallas kernels for 0% -> 0%
where the time goes in v10:
time: 172 us; the launch traced here: 171 us
  blocking collectives  86.8 us (50%)
  starting transfers between devices  30.2 us (18%)
  waiting for transfers between devices  28.5 us (17%)
  other arithmetic  9.81 us (6%)
  matrix products  8.15 us (5%)
  local copies, waits for them, and re-layouts  6.89 us (4%)
    all_to_all x1, blocking collectives, per_device(): both = lax.all_to_all(both, 'z', 0, 0, tiled=True)  29 us
    all_to_all x1, blocking collectives, per_device(): lax.all_to_all(out.reshape(chips, own_rows, width), CHIPS, 0, 0, tiled=True)  21 us
    all_to_all x1, blocking collectives, spread(): return lax.all_to_all(copies, axes, 0, 0, tiled=True)  18.9 us
    all_to_all x1, blocking collectives, per_device(): shrunk = lax.all_to_all(shrunk, 'z', 0, 0, tiled=True)  17.9 us
    all_to_all x2, waiting for transfers between devices, spread(): return lax.all_to_all(copies, axes, 0, 0, tiled=True)  13.1 us
    all_to_all x1, starting transfers between devices, per_device(): half = lax.all_to_all(half, CHIPS, 0, 0, tiled=True)  10.2 us
    all_to_all x2, starting transfers between devices, spread(): return lax.all_to_all(copies, axes, 0, 0, tiled=True)  8.7 us
    all_to_all x1, waiting for transfers between devices, per_device(): half = lax.all_to_all(half, CHIPS, 0, 0, tiled=True)  8.11 us
  transfers between devices with their start and end apart: 7, of which 4 were waited for; matrix products, arithmetic and copies ran while one was open for 7% of the time, Pallas kernels for 0%

profile of v10, /device:TPU:8, one launch (start us, length us, event | category | flops | bytes accessed | tf_op | source)
XLA Modules:
  0.0 171.0 jit_solution(3722590450840586636)
XLA Ops:
  0.0 1.7 broadcast_in_dim.36
  1.7 10.2 %all-to-all-start = ((bf16[32,8,1024]{2,1,0:T(8,128)(2,1)}), bf16[32,8,1024]{2,1,0:T(8,128)(2,1)S(1)}, u32[]{:S(2)}, u32[]{:S(2)}) async-start(bf16[32,8,1024]{2,1,0:T(8,128)(2,1)} %broadcast_in_dim.36), calls=%async_computation | async-start | bytes 1048576 | tf_op jit(solution)/shard_map/all_to_all | solution.py:39
  11.9 1.1 pad_maximum_fusion.1
  12.9 1.9 %collective-permute-start = (bf16[192,1024]{1,0:T(8,128)(2,1)S(1)}, bf16[192,1024]{1,0:T(8,128)(2,1)S(1)}, u32[]{:S(2)}, u32[]{:S(2)}) collective-permute-start(bf16[192,1024]{1,0:T(8,128)(2,1)S(1)} %pad_maximum_fusion.1), channel_id=1, source_target_pairs={{0,8},{8,0},{1,9},{9,1},{2,10},{10,2},{3,11},{11,3},{4,12},{12,4},... | collective-permute-start | bytes 1179656 | tf_op jit(solution)/shard_map/ppermute | solution.py:41
  15.4 1.2 reduce-window.6
  16.6 0.2 slice_reduce_fusion
  17.4 0.7 fusion.16
  18.2 0.7 compare_convert_fusion.2
  18.9 0.7 compare_convert_fusion.1
  19.6 0.7 fusion.54
  20.3 0.9 compare_convert_fusion
  21.4 8.1 %all-to-all-done = bf16[32,8,1024]{2,1,0:T(8,128)(2,1)S(1)} async-done(((bf16[32,8,1024]{2,1,0:T(8,128)(2,1)}), bf16[32,8,1024]{2,1,0:T(8,128)(2,1)S(1)}, u32[]{:S(2)}, u32[]{:S(2)}) %all-to-all-start) | async-done | bytes 524320 | tf_op jit(solution)/shard_map/all_to_all | solution.py:39
  29.5 0.3 convolution_convert_fusion
  30.0 0.2 convolution_convert_fusion.4
  30.2 0.3 fusion.8
  30.5 17.9 %all_to_all.40 = bf16[8,6,128]{2,1,0:T(8,128)(2,1)S(1)} all-to-all(bf16[8,6,128]{2,1,0:T(8,128)(2,1)S(1)} %fusion.8), channel_id=1, replica_groups=mesh['x'=4,'y'=8,'c'=2,'z'=8] {'z'}, dimensions={0} | all-to-all | bytes 24576 | tf_op jit(solution)/shard_map/all_to_all | solution.py:128
  48.4 1.9 %collective-permute-start.1 = (bf16[256,1024]{1,0:T(8,128)(2,1)S(1)}, bf16[256,1024]{1,0:T(8,128)(2,1)S(1)}, u32[]{:S(2)}, u32[]{:S(2)}) collective-permute-start(bf16[256,1024]{1,0:T(8,128)(2,1)S(1)} %bitcast.102), channel_id=1, source_target_pairs={{0,8},{8,0},{1,9},{9,1},{2,10},{10,2},{3,11},{11,3},{4,12},{12,4},... | collective-permute-start | bytes 1572872 | tf_op jit(solution)/shard_map/ppermute | solution.py:130
  50.4 0.7 broadcast_in_dim.42
  51.0 5.4 %all-to-all-start.2 = ((bf16[64,6,128]{2,1,0:T(8,128)(2,1)}), bf16[64,6,128]{2,1,0:T(8,128)(2,1)S(1)}, u32[]{:S(2)}, u32[]{:S(2)}) async-start(bf16[64,6,128]{2,1,0:T(8,128)(2,1)} %broadcast_in_dim.42), calls=%async_computation.2 | async-start | bytes 262144 | tf_op jit(solution)/shard_map/all_to_all | solution.py:18
  56.5 1.0 copy-done.11
  57.6 0.7 convolution_bitcast_fusion.3
  58.3 0.7 convolution_bitcast_fusion.4
  59.0 7.5 %all-to-all-done.2 = bf16[64,6,128]{2,1,0:T(8,128)(2,1)S(1)} async-done(((bf16[64,6,128]{2,1,0:T(8,128)(2,1)}), bf16[64,6,128]{2,1,0:T(8,128)(2,1)S(1)}, u32[]{:S(2)}, u32[]{:S(2)}) %all-to-all-start.2) | async-done | bytes 98336 | tf_op jit(solution)/shard_map/all_to_all | solution.py:18
  66.5 0.4 fusion.7
  66.9 1.6 convolution_bitcast_fusion.2
  68.4 0.2 add_convert_fusion.2
  68.7 0.5 convolution_bitcast_fusion.1
  69.2 0.2 add_convert_fusion.1
  69.5 29.0 %all_to_all.41 = bf16[8,2,56,512]{3,2,1,0:T(8,128)(2,1)S(1)} all-to-all(bf16[8,2,56,512]{3,2,1,0:T(8,128)(2,1)S(1)} %pad_maximum_fusion), channel_id=1, replica_groups=mesh['x'=4,'y'=8,'c'=2,'z'=8] {'z'}, dimensions={0} | all-to-all | bytes 1835008 | tf_op jit(solution)/shard_map/all_to_all | solution.py:161
  98.7 18.9 %all_to_all.42 = bf16[8,56,512]{2,1,0:T(8,128)(2,1)S(1)} all-to-all(bf16[8,56,512]{2,1,0:T(8,128)(2,1)S(1)} %broadcast_in_dim.45), channel_id=1, replica_groups=mesh['x'=4,'y'=8,'c'=2,'z'=8] {'z'}, dimensions={0} | all-to-all | bytes 917504 | tf_op jit(solution)/shard_map/all_to_all | solution.py:18
  117.7 0.4 multiply_reduce_fusion
  118.1 0.2 convolution_convert_fusion.2
  118.3 0.7 reshape.547
  119.0 5.5 %all-to-all-start.5 = ((bf16[64,3,128]{2,1,0:T(4,128)(2,1)}), bf16[64,3,128]{2,1,0:T(4,128)(2,1)}, u32[]{:S(2)}, u32[]{:S(2)}) async-start(bf16[64,3,128]{2,1,0:T(4,128)(2,1)} %reshape.547), calls=%async_computation.5 | async-start | bytes 131072 | tf_op jit(solution)/shard_map/all_to_all | solution.py:174
  124.5 0.7 fusion.108
  125.2 1.0 slice.97
  126.2 7.2 %all-to-all-done.5 = bf16[64,3,128]{2,1,0:T(4,128)(2,1)} async-done(((bf16[64,3,128]{2,1,0:T(4,128)(2,1)}), bf16[64,3,128]{2,1,0:T(4,128)(2,1)}, u32[]{:S(2)}, u32[]{:S(2)}) %all-to-all-start.5) | async-done | bytes 49184 | tf_op jit(solution)/shard_map/all_to_all | solution.py:174
  133.4 0.9 reduce_sum.77
  134.4 0.6 broadcast_in_dim.47
  135.0 3.3 %all-to-all-start.6 = ((bf16[8,3,128]{2,1,0:T(4,128)(2,1)}), bf16[8,3,128]{2,1,0:T(4,128)(2,1)S(1)}, u32[]{:S(2)}, u32[]{:S(2)}) async-start(bf16[8,3,128]{2,1,0:T(4,128)(2,1)} %broadcast_in_dim.47), calls=%async_computation.6 | async-start | bytes 16384 | tf_op jit(solution)/shard_map/all_to_all | solution.py:18
  138.3 2.0 %collective-permute-start.2 = (bf16[256,1024]{1,0:T(8,128)(2,1)}, bf16[256,1024]{1,0:T(8,128)(2,1)}, u32[]{:S(2)}, u32[]{:S(2)}) collective-permute-start(bf16[256,1024]{1,0:T(8,128)(2,1)} %slice.97), channel_id=1, source_target_pairs={{0,8},{8,0},{1,9},{9,1},{2,10},{10,2},{3,11},{11,3},{4,12},{12,4},... | collective-permute-start | bytes 1572872 | tf_op jit(solution)/shard_map/ppermute | solution.py:182
  140.3 5.6 %all-to-all-done.6 = bf16[8,3,128]{2,1,0:T(4,128)(2,1)S(1)} async-done(((bf16[8,3,128]{2,1,0:T(4,128)(2,1)}), bf16[8,3,128]{2,1,0:T(4,128)(2,1)S(1)}, u32[]{:S(2)}, u32[]{:S(2)}) %all-to-all-start.6) | async-done | bytes 6176 | tf_op jit(solution)/shard_map/all_to_all | solution.py:18
  146.0 0.3 fusion.69
  146.4 1.0 convert_multiply_fusion
  147.4 0.2 slice-done
  147.6 1.6 fusion.10
  149.2 21.0 %all_to_all.43 = bf16[32,8,1024]{2,1,0:T(8,128)(2,1)S(1)} all-to-all(bf16[32,8,1024]{2,1,0:T(8,128)(2,1)S(1)} %fusion.10), channel_id=1, replica_groups=mesh['x'=4,'y'=8,'c'=2,'z'=8] {'x','y'}, dimensions={0} | all-to-all | bytes 1048576 | tf_op jit(solution)/shard_map/all_to_all | solution.py:195
  170.3 0.7 reduce_sum.78
  (80 shorter events, 1.8 us)
Async XLA Ops:
  0.0 124.5 %copy-start = (bf16[448,1024]{1,0:T(8,128)(2,1)S(1)}, bf16[448,1024]{1,0:T(8,128)(2,1)}, u32[]{:S(2)}) copy-start(bf16[448,1024]{1,0:T(8,128)(2,1)} %param.15) | copy-start | bytes 2752516
  0.0 21.1 %copy-start.5 = (bf16[1,1024,64]{1,2,0:T(8,128)(2,1)S(1)}, bf16[1,1024,64]{1,2,0:T(8,128)(2,1)}, u32[]{:S(2)}) copy-start(bf16[1,1024,64]{1,2,0:T(8,128)(2,1)} %param.17) | copy-start | bytes 393220
  0.0 21.1 %copy-start.6 = (bf16[1,1024,64]{1,2,0:T(8,128)(2,1)S(1)}, bf16[1,1024,64]{1,2,0:T(8,128)(2,1)}, u32[]{:S(2)}) copy-start(bf16[1,1024,64]{1,2,0:T(8,128)(2,1)} %param.16) | copy-start | bytes 393220
  0.0 14.9 %copy-start.10 = (s32[64]{0:T(128)S(1)}, s32[64]{0:T(128)}, u32[]{:S(2)}) copy-start(s32[64]{0:T(128)} %param.23) | copy-start | bytes 772
  0.0 14.9 %copy-start.9 = (s32[512,1]{0,1:T(1,128)S(1)}, s32[512,1]{0,1:T(1,128)}, u32[]{:S(2)}) copy-start(s32[512,1]{0,1:T(1,128)} %param.22) | copy-start | bytes 6148
  1.7 27.8 %all-to-all-start = ((bf16[32,8,1024]{2,1,0:T(8,128)(2,1)}), bf16[32,8,1024]{2,1,0:T(8,128)(2,1)S(1)}, u32[]{:S(2)}, u32[]{:S(2)}) async-start(bf16[32,8,1024]{2,1,0:T(8,128)(2,1)} %broadcast_in_dim.36), calls=%async_computation | async-start | bytes 1048576 | tf_op jit(solution)/shard_map/all_to_all | solution.py:39
  12.9 8.4 %collective-permute-start = (bf16[192,1024]{1,0:T(8,128)(2,1)S(1)}, bf16[192,1024]{1,0:T(8,128)(2,1)S(1)}, u32[]{:S(2)}, u32[]{:S(2)}) collective-permute-start(bf16[192,1024]{1,0:T(8,128)(2,1)S(1)} %pad_maximum_fusion.1), channel_id=1, source_target_pairs={{0,8},{8,0},{1,9},{9,1},{2,10},{10,2},{3,11},{11,3},{4,12},{12,4},... | collective-permute-start | bytes 1179656 | tf_op jit(solution)/shard_map/ppermute | solution.py:41
  21.3 35.2 %copy-start.3 = (bf16[192,1024]{1,0:T(8,128)(2,1)}, bf16[192,1024]{1,0:T(8,128)(2,1)S(1)}, u32[]{:S(2)}) copy-start(bf16[192,1024]{1,0:T(8,128)(2,1)S(1)} %collective-permute-done) | copy-start | bytes 1179652
  48.4 8.1 %collective-permute-start.1 = (bf16[256,1024]{1,0:T(8,128)(2,1)S(1)}, bf16[256,1024]{1,0:T(8,128)(2,1)S(1)}, u32[]{:S(2)}, u32[]{:S(2)}) collective-permute-start(bf16[256,1024]{1,0:T(8,128)(2,1)S(1)} %bitcast.102), channel_id=1, source_target_pairs={{0,8},{8,0},{1,9},{9,1},{2,10},{10,2},{3,11},{11,3},{4,12},{12,4},... | collective-permute-start | bytes 1572872 | tf_op jit(solution)/shard_map/ppermute | solution.py:130
  51.0 15.4 %all-to-all-start.2 = ((bf16[64,6,128]{2,1,0:T(8,128)(2,1)}), bf16[64,6,128]{2,1,0:T(8,128)(2,1)S(1)}, u32[]{:S(2)}, u32[]{:S(2)}) async-start(bf16[64,6,128]{2,1,0:T(8,128)(2,1)} %broadcast_in_dim.42), calls=%async_computation.2 | async-start | bytes 262144 | tf_op jit(solution)/shard_map/all_to_all | solution.py:18
  56.4 1.2 copy-start.11
  56.5 1.8 %copy-start.12 = (bf16[448,1024]{1,0:T(8,128)(2,1)S(1)}, bf16[448,1024]{1,0:T(8,128)(2,1)}, u32[]{:S(2)}) copy-start(bf16[448,1024]{1,0:T(8,128)(2,1)} %param.13) | copy-start | bytes 2752516
  66.9 1.8 %copy-start.13 = (bf16[64,8,448]{2,1,0:T(8,128)(2,1)S(1)}, bf16[64,8,448]{2,1,0:T(8,128)(2,1)}, u32[]{:S(2)}) copy-start(bf16[64,8,448]{2,1,0:T(8,128)(2,1)} %param.19) | copy-start | bytes 1376260
  69.5 48.2 %copy-start.8 = (f32[64,512]{1,0:T(8,128)S(1)}, f32[64,512]{1,0:T(8,128)}, u32[]{:S(2)}) copy-start(f32[64,512]{1,0:T(8,128)} %get-tuple-element.45) | copy-start | bytes 393220
  69.5 48.2 %copy-start.14 = (bf16[448,64,8]{0,2,1:T(8,128)(2,1)S(1)}, bf16[448,64,8]{0,2,1:T(8,128)(2,1)}, u32[]{:S(2)}) copy-start(bf16[448,64,8]{0,2,1:T(8,128)(2,1)} %param.20) | copy-start | bytes 1376260
  98.5 19.6 %copy-start.7 = (bf16[192,512]{1,0:T(8,128)(2,1)S(1)}, bf16[192,512]{1,0:T(8,128)(2,1)}, u32[]{:S(2)}) copy-start(bf16[192,512]{1,0:T(8,128)(2,1)} %fusion.16) | copy-start | bytes 589828
  119.0 14.5 %all-to-all-start.5 = ((bf16[64,3,128]{2,1,0:T(4,128)(2,1)}), bf16[64,3,128]{2,1,0:T(4,128)(2,1)}, u32[]{:S(2)}, u32[]{:S(2)}) async-start(bf16[64,3,128]{2,1,0:T(4,128)(2,1)} %reshape.547), calls=%async_computation.5 | async-start | bytes 131072 | tf_op jit(solution)/shard_map/all_to_all | solution.py:174
  125.2 21.1 %copy-start.1 = (f32[512,1024]{1,0:T(8,128)}, f32[512,1024]{1,0:T(8,128)S(1)}, u32[]{:S(2)}) copy-start(f32[512,1024]{1,0:T(8,128)S(1)} %fusion.108) | copy-start | bytes 6291460
  126.2 21.1 %copy-start.2 = (bf16[1024,128]{1,0:T(8,128)(2,1)S(1)}, bf16[1024,128]{1,0:T(8,128)(2,1)}, u32[]{:S(2)}) copy-start(bf16[1024,128]{1,0:T(8,128)(2,1)} %compare_convert_fusion) | copy-start | bytes 786436
  126.2 21.1 %slice-start.1 = ((bf16[192,1024]{1,0:T(8,128)(2,1)}), bf16[64,1024]{1,0:T(8,128)(2,1)S(1)}, s32[]{:S(2)}) async-start(bf16[192,1024]{1,0:T(8,128)(2,1)} %copy-done.3), calls=%async_computation.9 | async-start | bytes 262144 | tf_op jit(solution)/shard_map/slice | solution.py:43
  126.2 21.2 %copy-start.4 = (bf16[1,64,1024]{2,1,0:T(8,128)(2,1)S(1)}, bf16[1,64,1024]{2,1,0:T(8,128)(2,1)}, u32[]{:S(2)}) copy-start(bf16[1,64,1024]{2,1,0:T(8,128)(2,1)} %param.21) | copy-start | bytes 393220
  135.0 11.0 %all-to-all-start.6 = ((bf16[8,3,128]{2,1,0:T(4,128)(2,1)}), bf16[8,3,128]{2,1,0:T(4,128)(2,1)S(1)}, u32[]{:S(2)}, u32[]{:S(2)}) async-start(bf16[8,3,128]{2,1,0:T(4,128)(2,1)} %broadcast_in_dim.47), calls=%async_computation.6 | async-start | bytes 16384 | tf_op jit(solution)/shard_map/all_to_all | solution.py:18
  138.3 9.0 %collective-permute-start.2 = (bf16[256,1024]{1,0:T(8,128)(2,1)}, bf16[256,1024]{1,0:T(8,128)(2,1)}, u32[]{:S(2)}, u32[]{:S(2)}) collective-permute-start(bf16[256,1024]{1,0:T(8,128)(2,1)} %slice.97), channel_id=1, source_target_pairs={{0,8},{8,0},{1,9},{9,1},{2,10},{10,2},{3,11},{11,3},{4,12},{12,4},... | collective-permute-start | bytes 1572872 | tf_op jit(solution)/shard_map/ppermute | solution.py:182
  146.3 1.3 slice-start
